TPU v7x, 32 devices: a whole 2x2x4 slice. The times are simulated.
32 devices in a mesh: shard: 4 (over y, x), seq: 8 (over z, core).
Axes of the slice: x: 2, y: 2, z: 4, core: 2. Of those that a mesh axis runs over, the one named last changes fastest.
Arguments:
- layer_input: bfloat16 [4096, 2048], P(('shard', 'seq')), may hold values from -6 to 6
- doc_lengths: int32 [16], replicated, may hold values from 1 to 3640, as said below
- norm_gain: bfloat16 [2048], P(('shard', 'seq')), may hold values from 0.5 to 1.5
- query_weight: bfloat16 [2048, 2048], P(('shard', 'seq')), may hold values from -0.125 to 0.125
- key_weight: bfloat16 [2048, 2048], P(('shard', 'seq')), may hold values from -0.125 to 0.125
- value_weight: bfloat16 [2048, 2048], P(('shard', 'seq')), may hold values from -0.125 to 0.125
- output_weight: bfloat16 [2048, 2048], P(('shard', 'seq')), may hold values from -6 to 6
- feed_gain: bfloat16 [2048], P(('shard', 'seq')), may hold values from 0.5 to 1.5
- gate_weight: bfloat16 [8192, 2048], P(('shard', 'seq')), may hold values from -0.125 to 0.125
- up_weight: bfloat16 [8192, 2048], P(('shard', 'seq')), may hold values from -0.125 to 0.125
- down_weight: bfloat16 [8192, 2048], P(('shard', 'seq')), may hold values from -0.0625 to 0.0625
- output_grad: bfloat16 [4096, 2048], P(('shard', 'seq')), may hold values from -6 to 6
Outputs:
- layer_output: bfloat16 [4096, 2048], P(('shard', 'seq'))
- input_grad: bfloat16 [4096, 2048], P(('shard', 'seq'))
- norm_gain_grad: float32 [2048], P(('shard', 'seq'))
- query_weight_grad: float32 [2048, 2048], P(('shard', 'seq'))
- key_weight_grad: float32 [2048, 2048], P(('shard', 'seq'))
- value_weight_grad: float32 [2048, 2048], P(('shard', 'seq'))
- output_weight_grad: float32 [2048, 2048], P(('shard', 'seq'))
- feed_gain_grad: float32 [2048], P(('shard', 'seq'))
- gate_weight_grad: float32 [8192, 2048], P(('shard', 'seq'))
- up_weight_grad: float32 [8192, 2048], P(('shard', 'seq'))
- down_weight_grad: float32 [8192, 2048], P(('shard', 'seq'))
Inputs may be any that keep to these rules, and one draw needn't show every extreme that they name: `doc_lengths`: the lengths add up to 4096. One document, neither the first nor the last, has the largest length; it begins within the first 1024 positions of the stream and ends within the last 1024.
All inputs are finite; a program needn't handle non-finite values.
Results may differ from a plain program's by a relative error of at most 0.014.
Values may be sent and summed in bfloat16 or wider, within the bound.
No kernel may reach another device: no remote copies, remote signals or barrier semaphores. Data moves between devices by JAX's collectives and lax.ppermute only.
A program may use at most 704 MiB of HBM per device.

v0:
```python
import math

import jax
import jax.numpy as jnp
from jax import lax
from jax.sharding import PartitionSpec as P

HEAD_DIM = 64


NORM_EPS = 1e-05
ROPE_BASE = 130000.0


def rope_tables(positions, width):
    half_width = width // 2
    exponent = -2.0 * jnp.arange(half_width, dtype=jnp.float32) / width
    inverse = jnp.power(jnp.float32(ROPE_BASE), exponent)
    angles = positions.astype(jnp.float32)[:, None] * inverse[None, :]
    return (jnp.cos(angles), jnp.sin(angles))


def rotate(values, cos_table, sin_table):
    half_width = values.shape[-1] // 2
    front = values[..., :half_width]
    back_half = values[..., half_width:]
    cos_wide = cos_table[:, None, :]
    sin_wide = sin_table[:, None, :]
    return jnp.concatenate(
        [front * cos_wide - back_half * sin_wide, back_half * cos_wide + front * sin_wide], axis=-1
    )


def unrotate(values, cos_table, sin_table):
    half_width = values.shape[-1] // 2
    front = values[..., :half_width]
    back_half = values[..., half_width:]
    cos_wide = cos_table[:, None, :]
    sin_wide = sin_table[:, None, :]
    return jnp.concatenate(
        [front * cos_wide + back_half * sin_wide, back_half * cos_wide - front * sin_wide], axis=-1
    )


def doc_numbers(doc_lengths, positions):
    doc_ends = jnp.cumsum(doc_lengths)
    return jnp.sum((doc_ends[:, None] <= positions[None, :]).astype(jnp.int32), axis=0)


def normalize(values, gain_vec):
    scale_row = lax.rsqrt(jnp.mean(values * values, axis=-1, keepdims=True) + NORM_EPS)
    return (values * scale_row * gain_vec, scale_row)


def norm_back(grad_in, values, scale_row, gain_vec):
    unit_rows = values * scale_row
    gain_grad = jnp.sum(grad_in * unit_rows, axis=0)
    unit_grad = grad_in * gain_vec
    value_grad = scale_row * (
        unit_grad - unit_rows * jnp.mean(unit_grad * unit_rows, axis=-1, keepdims=True)
    )
    return (value_grad, gain_grad)


def times_trans(lhs_mat, rhs_mat):
    return lax.dot_general(
        lhs_mat, rhs_mat, (((1,), (1,)), ((), ())), preferred_element_type=jnp.float32
    )


def trans_times(lhs_mat, rhs_mat):
    return lax.dot_general(
        lhs_mat, rhs_mat, (((0,), (0,)), ((), ())), preferred_element_type=jnp.float32
    )


def per_device(
    layer_input,
    doc_lengths,
    norm_gain,
    query_weight,
    key_weight,
    value_weight,
    output_weight,
    feed_gain,
    gate_weight,
    up_weight,
    down_weight,
    output_grad,
):
    tok_rows = layer_input.shape[0]
    width = layer_input.shape[1]
    seq_count = lax.axis_size("seq")
    shard_count = lax.axis_size("shard")
    span_len = tok_rows * seq_count
    stream_len = span_len * shard_count
    span_start = lax.axis_index("shard") * span_len
    own_positions = (
        span_start + lax.axis_index("seq") * tok_rows + jnp.arange(tok_rows, dtype=jnp.int32)
    )
    span_positions = span_start + jnp.arange(span_len, dtype=jnp.int32)
    all_positions = jnp.arange(stream_len, dtype=jnp.int32)
    key_docs = doc_numbers(doc_lengths, all_positions)
    query_docs = lax.dynamic_slice_in_dim(key_docs, span_start, span_len)
    score_scale = HEAD_DIM ** (-0.5)
    gathered = (
        lax.all_gather(query_weight, ("shard", "seq"), axis=0, tiled=True),
        lax.all_gather(key_weight, ("shard", "seq"), axis=0, tiled=True),
        lax.all_gather(value_weight, ("shard", "seq"), axis=0, tiled=True),
        lax.all_gather(output_weight, ("shard", "seq"), axis=0, tiled=True),
        lax.all_gather(norm_gain, ("shard", "seq"), axis=0, tiled=True),
        lax.all_gather(feed_gain, ("shard", "seq"), axis=0, tiled=True),
    )
    query_full, key_full, value_full, output_full = (
        gathered[0],
        gathered[1],
        gathered[2],
        gathered[3],
    )
    gain_one = gathered[4].astype(jnp.float32)
    gain_two = gathered[5].astype(jnp.float32)
    inputs = layer_input.astype(jnp.float32)
    normed, scale_one = normalize(inputs, gain_one)
    normed_low = normed.astype(jnp.bfloat16)
    own_cos, own_sin = rope_tables(own_positions, HEAD_DIM)
    query_proj = jnp.dot(normed_low, query_full, preferred_element_type=jnp.float32)
    key_proj = jnp.dot(normed_low, key_full, preferred_element_type=jnp.float32)
    value_proj = jnp.dot(normed_low, value_full, preferred_element_type=jnp.float32)
    query_rot = rotate(query_proj.reshape(tok_rows, -1, HEAD_DIM), own_cos, own_sin).reshape(
        tok_rows, width
    )
    key_rot = rotate(key_proj.reshape(tok_rows, -1, HEAD_DIM), own_cos, own_sin).reshape(
        tok_rows, width
    )
    stacked = jnp.stack(
        [
            query_rot.astype(jnp.bfloat16),
            key_rot.astype(jnp.bfloat16),
            value_proj.astype(jnp.bfloat16),
        ]
    )
    head_triple = lax.all_to_all(stacked, "seq", split_axis=2, concat_axis=1, tiled=True)
    head_width = head_triple.shape[2]
    heads_dev = head_width // HEAD_DIM
    head_query = head_triple[0].reshape(span_len, heads_dev, HEAD_DIM)
    key_value = lax.all_gather(head_triple[1:], "shard", axis=1, tiled=True)
    key_block = math.gcd(stream_len, max(512, stream_len // 16))
    block_count = stream_len // key_block
    key_blocks = key_value[0].reshape(block_count, key_block, heads_dev, HEAD_DIM)
    value_blocks = key_value[1].reshape(block_count, key_block, heads_dev, HEAD_DIM)
    pos_blocks = all_positions.reshape(block_count, key_block)
    doc_blocks = key_docs.reshape(block_count, key_block)

    def block_scores(key_blk, key_pos, key_doc):
        scores = (
            jnp.einsum("qhd,khd->hqk", head_query, key_blk, preferred_element_type=jnp.float32)
            * score_scale
        )
        allowed = (key_pos[None, :] <= span_positions[:, None]) & (
            key_doc[None, :] == query_docs[:, None]
        )
        return jnp.where(allowed[None], scores, -jnp.inf)

    def total_step(state_pair, pieces):
        run_max, run_sum = state_pair
        scores = block_scores(pieces[0], pieces[1], pieces[2])
        new_max = jnp.maximum(run_max, jnp.max(scores, axis=-1))
        new_sum = run_sum * jnp.exp(run_max - new_max) + jnp.sum(
            jnp.exp(scores - new_max[..., None]), axis=-1
        )
        return ((new_max, new_sum), None)

    start_max = jnp.full((heads_dev, span_len), -1e30, jnp.float32)
    start_sum = jnp.zeros((heads_dev, span_len), jnp.float32)
    totals, unused = lax.scan(
        total_step, (start_max, start_sum), (key_blocks, pos_blocks, doc_blocks)
    )
    log_total = totals[0] + jnp.log(totals[1])

    def output_step(accum, pieces):
        scores = block_scores(pieces[0], pieces[2], pieces[3])
        probs = jnp.exp(scores - log_total[..., None]).astype(jnp.bfloat16)
        return (
            accum
            + jnp.einsum("hqk,khd->qhd", probs, pieces[1], preferred_element_type=jnp.float32),
            None,
        )

    start_acc = jnp.zeros((span_len, heads_dev, HEAD_DIM), jnp.float32)
    head_out32, unused = lax.scan(
        output_step, start_acc, (key_blocks, value_blocks, pos_blocks, doc_blocks)
    )
    head_out = head_out32.reshape(span_len, head_width).astype(jnp.bfloat16)
    token_out = lax.all_to_all(head_out, "seq", split_axis=0, concat_axis=1, tiled=True)
    middle = inputs + jnp.dot(token_out, output_full, preferred_element_type=jnp.float32)
    normed_two, scale_two = normalize(middle, gain_two)
    feed_low = normed_two.astype(jnp.bfloat16)
    feed_mats = (
        lax.all_gather(gate_weight, ("shard", "seq"), axis=0, tiled=True),
        lax.all_gather(up_weight, ("shard", "seq"), axis=0, tiled=True),
        lax.all_gather(down_weight, ("shard", "seq"), axis=0, tiled=True),
    )
    gate_full, up_full, down_full = (feed_mats[0], feed_mats[1], feed_mats[2])
    gate_val = times_trans(feed_low, gate_full)
    up_val = times_trans(feed_low, up_full)
    hidden = (jax.nn.silu(gate_val) * up_val).astype(jnp.bfloat16)
    down_val = jnp.dot(hidden, down_full, preferred_element_type=jnp.float32)
    layer_output = (middle + down_val).astype(jnp.bfloat16)
    hidden_grad = times_trans(output_grad, down_full)
    sigmoid_val = jax.nn.sigmoid(gate_val)
    gate_grad = (
        hidden_grad * up_val * (sigmoid_val * (1.0 + gate_val * (1.0 - sigmoid_val)))
    ).astype(jnp.bfloat16)
    up_grad = (hidden_grad * jax.nn.silu(gate_val)).astype(jnp.bfloat16)
    feed_grad = jnp.dot(gate_grad, gate_full, preferred_element_type=jnp.float32) + jnp.dot(
        up_grad, up_full, preferred_element_type=jnp.float32
    )
    feed_sums = lax.psum_scatter(
        jnp.stack(
            [
                trans_times(gate_grad, feed_low),
                trans_times(up_grad, feed_low),
                trans_times(hidden, output_grad),
            ],
            axis=1,
        ),
        ("shard", "seq"),
        scatter_dimension=0,
        tiled=True,
    )
    middle_norm_grad, gain_two_grad = norm_back(feed_grad, middle, scale_two, gain_two)
    middle_grad = output_grad.astype(jnp.float32) + middle_norm_grad
    attend_grad = middle_grad.astype(jnp.bfloat16)
    output_term = trans_times(token_out, attend_grad)
    token_out_grad = times_trans(attend_grad, output_full).astype(jnp.bfloat16)
    head_out_grad = lax.all_to_all(
        token_out_grad, "seq", split_axis=1, concat_axis=0, tiled=True
    ).reshape(span_len, heads_dev, HEAD_DIM)
    row_dots = jnp.transpose(jnp.sum(head_out_grad.astype(jnp.float32) * head_out32, axis=-1))

    def grad_step(query_acc, pieces):
        key_blk, value_blk, key_pos, key_doc = pieces
        scores = block_scores(key_blk, key_pos, key_doc)
        probs = jnp.exp(scores - log_total[..., None])
        prob_grad = jnp.einsum(
            "qhd,khd->hqk", head_out_grad, value_blk, preferred_element_type=jnp.float32
        )
        score_grad = (probs * (prob_grad - row_dots[..., None])).astype(jnp.bfloat16)
        query_next = query_acc + score_scale * jnp.einsum(
            "hqk,khd->qhd", score_grad, key_blk, preferred_element_type=jnp.float32
        )
        key_part = score_scale * jnp.einsum(
            "hqk,qhd->khd", score_grad, head_query, preferred_element_type=jnp.float32
        )
        value_part = jnp.einsum(
            "hqk,qhd->khd",
            probs.astype(jnp.bfloat16),
            head_out_grad,
            preferred_element_type=jnp.float32,
        )
        return (query_next, (key_part, value_part))

    query_grad, block_grads = lax.scan(
        grad_step, start_acc, (key_blocks, value_blocks, pos_blocks, doc_blocks)
    )
    pair_grads = jnp.stack(
        [
            block_grads[0].reshape(stream_len, head_width),
            block_grads[1].reshape(stream_len, head_width),
        ]
    )
    own_pair = lax.psum_scatter(
        pair_grads.astype(jnp.bfloat16), "shard", scatter_dimension=1, tiled=True
    ).astype(jnp.float32)
    span_cos, span_sin = rope_tables(span_positions, HEAD_DIM)
    query_back = unrotate(query_grad, span_cos, span_sin).reshape(span_len, head_width)
    key_back = unrotate(
        own_pair[0].reshape(span_len, heads_dev, HEAD_DIM), span_cos, span_sin
    ).reshape(span_len, head_width)
    back_stack = jnp.stack([query_back, key_back, own_pair[1]]).astype(jnp.bfloat16)
    token_grads = lax.all_to_all(back_stack, "seq", split_axis=1, concat_axis=2, tiled=True)
    norm_grad = (
        times_trans(token_grads[0], query_full)
        + times_trans(token_grads[1], key_full)
        + times_trans(token_grads[2], value_full)
    )
    input_norm_grad, gain_one_grad = norm_back(norm_grad, inputs, scale_one, gain_one)
    input_grad = (middle_grad + input_norm_grad).astype(jnp.bfloat16)
    query_term = trans_times(normed_low, token_grads[0])
    key_term = trans_times(normed_low, token_grads[1])
    value_term = trans_times(normed_low, token_grads[2])
    summed = (
        lax.psum_scatter(query_term, ("shard", "seq"), scatter_dimension=0, tiled=True),
        lax.psum_scatter(key_term, ("shard", "seq"), scatter_dimension=0, tiled=True),
        lax.psum_scatter(value_term, ("shard", "seq"), scatter_dimension=0, tiled=True),
        lax.psum_scatter(output_term, ("shard", "seq"), scatter_dimension=0, tiled=True),
        lax.psum_scatter(gain_one_grad, ("shard", "seq"), scatter_dimension=0, tiled=True),
        lax.psum_scatter(gain_two_grad, ("shard", "seq"), scatter_dimension=0, tiled=True),
    )
    query_wgrad, key_wgrad, value_wgrad = (summed[0], summed[1], summed[2])
    output_wgrad, gain_one_out, gain_two_out = (summed[3], summed[4], summed[5])
    return (
        layer_output,
        input_grad,
        gain_one_out,
        query_wgrad,
        key_wgrad,
        value_wgrad,
        output_wgrad,
        gain_two_out,
        feed_sums[:, 0],
        feed_sums[:, 1],
        feed_sums[:, 2],
    )


def solution(mesh):
    return jax.shard_map(
        per_device,
        mesh=mesh,
        in_specs=(
            P(("shard", "seq"), None),
            P(),
            P(("shard", "seq")),
            P(("shard", "seq"), None),
            P(("shard", "seq"), None),
            P(("shard", "seq"), None),
            P(("shard", "seq"), None),
            P(("shard", "seq")),
            P(("shard", "seq"), None),
            P(("shard", "seq"), None),
            P(("shard", "seq"), None),
            P(("shard", "seq"), None),
        ),
        out_specs=(
            P(("shard", "seq"), None),
            P(("shard", "seq"), None),
            P(("shard", "seq")),
            P(("shard", "seq"), None),
            P(("shard", "seq"), None),
            P(("shard", "seq"), None),
            P(("shard", "seq"), None),
            P(("shard", "seq")),
            P(("shard", "seq"), None),
            P(("shard", "seq"), None),
            P(("shard", "seq"), None),
        ),
        check_vma=False,
    )
```

profile of v0, /device:TPU:8, one launch (start us, length us, event | category | flops | bytes accessed | tf_op | source)
XLA Modules:
  0.0 4348.2 jit_solution(10012328975832775761)
XLA Ops:
  11.2 41.1 all-reduce.5
  53.7 36.2 all-gather.11.cloned.1.call-done
  96.9 72.0 %all-gather.9.cloned.1.call-done = bf16[2048,2048]{1,0:T(8,128)(2,1)} async-done(((bf16[64,2048]{1,0:T(8,128)(2,1)}), bf16[2048,2048]{1,0:T(8,128)(2,1)}) %all-gather.9.cloned.1.call-update) | async-done | bytes 8388624 | tf_op jit(solution)/shard_map/all_gather | solution.py:107
  176.6 71.3 %all-gather.13.cloned.1.call-done = bf16[2048,2048]{1,0:T(8,128)(2,1)} async-done(((bf16[64,2048]{1,0:T(8,128)(2,1)}), bf16[2048,2048]{1,0:T(8,128)(2,1)}) %all-gather.13.cloned.1.call-update) | async-done | bytes 8388624 | tf_op jit(solution)/shard_map/all_gather | solution.py:109
  256.9 50.4 %all_to_all.62 = bf16[3,128,2048]{1,0,2:T(4,128)(2,1)S(1)} all-to-all(bf16[3,128,2048]{1,0,2:T(4,128)(2,1)S(1)} %copy.139), channel_id=1, replica_groups=mesh['shard'=4,'seq'=8] {'seq'}, dimensions={2} | all-to-all | bytes 3145728 | tf_op jit(solution)/shard_map/all_to_all | solution.py:142
  312.8 48.9 %all-gather.15.cloned.1.call-done = bf16[2,4096,256]{2,1,0:T(8,128)(2,1)} async-done(((bf16[2,1024,256]{2,1,0:T(8,128)(2,1)}), bf16[2,4096,256]{2,1,0:T(8,128)(2,1)}) %all-gather.15.cloned.1.call-update) | async-done | bytes 4194320 | tf_op jit(solution)/shard_map/all_gather | solution.py:146
  388.4 32.5 while.39
  420.9 53.4 %while.40 = (s32[]{:T(128)}, f32[1024,4,64]{0,2,1:T(8,128)}, bf16[8,512,4,64]{1,3,2,0:T(8,128)(2,1)}, s32[8,512]{1,0:T(8,128)S(1)}, s32[8,512]{1,0:T(8,128)S(1)}...) while((s32[]{:T(128)}, f32[1024,4,64]{0,2,1:T(8,128)}, ...), condition=%wide.region_8.9_spmd.clone, body=%wide.region_7.8_spmd.clone.sunk | while | flops 547357696 | bytes 4236942 | solution.py:190
  493.6 25.2 all-to-all-done.1
  524.0 122.0 %all-gather.21.cloned.1.call-done = bf16[8192,2048]{1,0:T(8,128)(2,1)} async-done(((bf16[256,2048]{1,0:T(8,128)(2,1)}), bf16[8192,2048]{1,0:T(8,128)(2,1)}) %all-gather.21.cloned.1.call-update) | async-done | bytes 33554448 | tf_op jit(solution)/shard_map/all_gather | solution.py:200
  663.9 178.0 %all-gather.19.cloned.1.call-done = bf16[8192,2048]{1,0:T(8,128)(2,1)} async-done(((bf16[256,2048]{1,0:T(8,128)(2,1)}), bf16[8192,2048]{1,0:T(8,128)(2,1)}) %all-gather.19.cloned.1.call-update) | async-done | bytes 33554448 | tf_op jit(solution)/shard_map/all_gather | solution.py:199
  860.0 177.9 %all-gather.23.cloned.1.call-done = bf16[8192,2048]{1,0:T(8,128)(2,1)} async-done(((bf16[256,2048]{1,0:T(8,128)(2,1)}), bf16[8192,2048]{1,0:T(8,128)(2,1)}) %all-gather.23.cloned.1.call-update) | async-done | bytes 33554448 | tf_op jit(solution)/shard_map/all_gather | solution.py:201
  1118.2 110.2 %while.41 = (s32[]{:T(128)}, f32[1024,4,64]{0,2,1:T(8,128)S(1)}, bf16[8,512,4,64]{1,3,2,0:T(8,128)(2,1)}, bf16[8,512,4,64]{1,3,2,0:T(8,128)(2,1)}, bf16[8,512,4,...) while((s32[]{:T(128)}, f32[1024,4,64]{0,2,1:T(8,128)S(1)}, ...), condition=%wide.region_13.14_spmd.clone, body=%wide.region_12.13_spmd.clone.sunk | while | flops 1365640192 | bytes 47522012 | solution.py:263
  1248.4 25.1 convolution_bitcast_fusion.1
  1273.5 24.2 convolution_bitcast_fusion.2
  1297.7 23.1 convolution_bitcast_fusion
  1320.8 130.3 %pad_maximum_fusion = f32[8192,3,2048]{2,0,1:T(8,128)} fusion(f32[8192,1,2048]{2,0,1:T(8,128)} %convolution_bitcast_fusion, f32[8192,1,2048]{2,0,1:T(8,128)} %convolution_bitcast_fusion.1, f32[8192,1,2048]{2,0,1:T(8,128)} %convolution_bitcast_fusion.2), kind=kLoop, calls=%fused_computation.69 | loop fusion | flops 100663296 | bytes 402653184 | tf_op jit(solution)/shard_map/stack | solution.py:219
  1468.3 84.9 %all_to_all.63 = bf16[3,1024,256]{2,0,1:T(4,128)(2,1)S(1)} all-to-all(bf16[3,1024,256]{2,0,1:T(4,128)(2,1)} %copy.156), channel_id=1, replica_groups=mesh['shard'=4,'seq'=8] {'seq'}, dimensions={1} | all-to-all | bytes 3145728 | tf_op jit(solution)/shard_map/all_to_all | solution.py:281
  1615.8 43.9 %all-reduce.4 = (f32[2048]{0:T(1024)S(1)}, f32[2048]{0:T(1024)S(1)}) all-reduce(f32[2048]{0:T(1024)S(1)} %get-tuple-element.485, f32[2048]{0:T(1024)S(1)} %copy-done.26), channel_id=3, replica_groups=mesh['shard'=4,'seq'=8] {'shard','seq'}, use_global_device_ids=true, to_apply=%region_17.18.clone | all-reduce | flops 4096 | bytes 32768
  1662.1 1928.5 %reduce-scatter.17.cloned.1.call-done = f32[256,3,2048]{2,0,1:T(8,128)} async-done(((f32[8192,3,2048]{2,0,1:T(8,128)}), f32[256,3,2048]{2,0,1:T(8,128)}) %reduce-scatter.17.cloned.1.call-update) | async-done | bytes 6291472 | tf_op jit(solution)/shard_map/reduce_scatter | solution.py:218
  3596.3 183.4 %reduce-scatter.15.cloned.1.call-done = f32[64,2048]{1,0:T(8,128)} async-done(((f32[2048,2048]{1,0:T(8,128)}), f32[64,2048]{1,0:T(8,128)}) %reduce-scatter.15.cloned.1.call-update) | async-done | bytes 524304 | tf_op jit(solution)/shard_map/reduce_scatter | solution.py:296
  3779.7 187.1 %reduce-scatter.13.cloned.1.call-done = f32[64,2048]{1,0:T(8,128)} async-done(((f32[2048,2048]{1,0:T(8,128)}), f32[64,2048]{1,0:T(8,128)}) %reduce-scatter.13.cloned.1.call-update) | async-done | bytes 524304 | tf_op jit(solution)/shard_map/reduce_scatter | solution.py:295
  3966.8 187.3 %reduce-scatter.11.cloned.1.call-done = f32[64,2048]{1,0:T(8,128)} async-done(((f32[2048,2048]{1,0:T(8,128)}), f32[64,2048]{1,0:T(8,128)}) %reduce-scatter.11.cloned.1.call-update) | async-done | bytes 524304 | tf_op jit(solution)/shard_map/reduce_scatter | solution.py:294
  4154.1 187.1 %reduce-scatter.9.cloned.1.call-done = f32[64,2048]{1,0:T(8,128)} async-done(((f32[2048,2048]{1,0:T(8,128)}), f32[64,2048]{1,0:T(8,128)}) %reduce-scatter.9.cloned.1.call-update) | async-done | bytes 524304 | tf_op jit(solution)/shard_map/reduce_scatter | solution.py:293
  (368 shorter events, 503.9 us)
Async XLA Ops:
  7.2 82.7 %all-gather.11.cloned.1.call-start = ((), (), s32[]{:S(2)}) async-start(), calls=%async_computation.11 | async-start | bytes 8650752 | tf_op jit(solution)/shard_map/all_gather | solution.py:108
  7.9 161.0 %all-gather.9.cloned.1.call-start = ((), (), s32[]{:S(2)}) async-start(), calls=%async_computation.10 | async-start | bytes 8650752 | tf_op jit(solution)/shard_map/all_gather | solution.py:107
  8.7 239.2 %all-gather.13.cloned.1.call-start = ((), (), s32[]{:S(2)}) async-start(), calls=%async_computation.12 | async-start | bytes 8650752 | tf_op jit(solution)/shard_map/all_gather | solution.py:109
  9.4 352.3 %all-gather.15.cloned.1.call-start = ((), (), s32[]{:S(2)}) async-start(), calls=%async_computation.13 | async-start | bytes 5242880 | tf_op jit(solution)/shard_map/all_gather | solution.py:146
  52.2 195.7 %copy-start.21 = (f32[2048]{0:T(1024)}, f32[2048]{0:T(1024)S(1)}, u32[]{:S(2)}) copy-start(f32[2048]{0:T(1024)S(1)} %convert_element_type.104) | copy-start | bytes 24580
  52.2 44.6 %copy-start.27 = (f32[32]{0:T(128)}, f32[32]{0:T(128)S(1)}, u32[]{:S(2)}) copy-start(f32[32]{0:T(128)S(1)} %multiply_power_fusion) | copy-start | bytes 388
  53.5 194.4 %copy-start.24 = (f32[128]{0:T(128)}, f32[128]{0:T(128)S(1)}, u32[]{:S(2)}) copy-start(f32[128]{0:T(128)S(1)} %add_rsqrt_fusion.1) | copy-start | bytes 1540
  53.7 115.2 %copy-start.2 = (bf16[128,2048]{1,0:T(8,128)(2,1)S(1)}, bf16[128,2048]{1,0:T(8,128)(2,1)}, u32[]{:S(2)}) copy-start(bf16[128,2048]{1,0:T(8,128)(2,1)} %param.18) | copy-start | bytes 1572868
  309.0 184.6 %all-gather.17.cloned.1.call-start = ((), (), s32[]{:S(2)}) async-start(), calls=%async_computation.14 | async-start | bytes 8650752 | tf_op jit(solution)/shard_map/all_gather | solution.py:110
  309.6 336.3 %all-gather.21.cloned.1.call-start = ((), (), s32[]{:S(2)}) async-start(), calls=%async_computation.16 | async-start | bytes 34603008 | tf_op jit(solution)/shard_map/all_gather | solution.py:200
  310.2 531.7 %all-gather.19.cloned.1.call-start = ((), (), s32[]{:S(2)}) async-start(), calls=%async_computation.15 | async-start | bytes 34603008 | tf_op jit(solution)/shard_map/all_gather | solution.py:199
  310.9 727.0 %all-gather.23.cloned.1.call-start = ((), (), s32[]{:S(2)}) async-start(), calls=%async_computation.17 | async-start | bytes 34603008 | tf_op jit(solution)/shard_map/all_gather | solution.py:201
  312.1 53.4 %copy-start.23 = (s32[4096]{0:T(1024)}, s32[4096]{0:T(1024)S(1)}, u32[]{:S(2)}) copy-start(s32[4096]{0:T(1024)S(1)} %convert_reduce_fusion) | copy-start | bytes 49156
  474.3 44.5 %copy-start.6 = (bf16[8,512,4,64]{1,3,2,0:T(8,128)(2,1)}, bf16[8,512,4,64]{1,3,2,0:T(8,128)(2,1)S(1)}, u32[]{:S(2)}) copy-start(bf16[8,512,4,64]{1,3,2,0:T(8,128)(2,1)S(1)} %get-tuple-element.966) | copy-start | bytes 6291460
  477.3 41.5 all-to-all-start.1
  523.8 562.4 %copy-start.4 = (f32[128,2048]{1,0:T(8,128)}, f32[128,2048]{1,0:T(8,128)S(1)}, u32[]{:S(2)}) copy-start(f32[128,2048]{1,0:T(8,128)S(1)} %get-tuple-element.595) | copy-start | bytes 3145732
  663.9 374.0 %copy-start.18 = (bf16[128,2048]{1,0:T(8,128)(2,1)S(1)}, bf16[128,2048]{1,0:T(8,128)(2,1)}, u32[]{:S(2)}) copy-start(bf16[128,2048]{1,0:T(8,128)(2,1)} %param.29) | copy-start | bytes 1572868
  1094.1 18.7 all-to-all-start.2
  1100.5 363.2 %reduce-scatter.7.cloned.1.call-start = ((), (), s32[]{:S(2)}) async-start(), calls=%async_computation.18 | async-start | bytes 5242880 | tf_op jit(solution)/shard_map/reduce_scatter | solution.py:272
  1246.8 2343.8 %reduce-scatter.17.cloned.1.call-start = ((), (), s32[]{:S(2)}) async-start(), calls=%async_computation.23 | async-start | bytes 207618048 | tf_op jit(solution)/shard_map/reduce_scatter | solution.py:218
  1451.2 2328.5 %reduce-scatter.15.cloned.1.call-start = ((), (), s32[]{:S(2)}) async-start(), calls=%async_computation.22 | async-start | bytes 17301504 | tf_op jit(solution)/shard_map/reduce_scatter | solution.py:296
  1462.5 2504.3 %reduce-scatter.13.cloned.1.call-start = ((), (), s32[]{:S(2)}) async-start(), calls=%async_computation.21 | async-start | bytes 17301504 | tf_op jit(solution)/shard_map/reduce_scatter | solution.py:295
  1562.8 2591.3 %reduce-scatter.11.cloned.1.call-start = ((), (), s32[]{:S(2)}) async-start(), calls=%async_computation.20 | async-start | bytes 17301504 | tf_op jit(solution)/shard_map/reduce_scatter | solution.py:294
  1572.4 2768.8 %reduce-scatter.9.cloned.1.call-start = ((), (), s32[]{:S(2)}) async-start(), calls=%async_computation.19 | async-start | bytes 17301504 | tf_op jit(solution)/shard_map/reduce_scatter | solution.py:293
  (32 other events, 230.5 us)
Sparse Core Ops, SparseCore 0:
  11.0 78.8 all-gather.10
  92.9 75.9 all-gather.8
  171.9 75.9 all-gather.12
  309.1 52.4 all-gather.14
  364.5 77.2 all-gather.16
  444.7 201.1 all-gather.20
  648.9 192.9 all-gather.18
  844.9 192.9 all-gather.22
  1246.9 53.2 reduce-scatter.6
  1451.3 2139.2 reduce-scatter.16
  3593.4 186.2 reduce-scatter.14
  3782.4 184.3 reduce-scatter.12
  3969.7 184.3 reduce-scatter.10
  4156.8 184.3 reduce-scatter.8
where the time goes:
time: 4370 us; the launch traced here: 4350 us
  waiting for transfers between devices  3420 us (78%)
  matrix products  416 us (10%)
  blocking collectives  220 us (5%)
  other arithmetic  178 us (4%)
  local copies, waits for them, and re-layouts  72.6 us (2%)
    reduce_scatter x1, waiting for transfers between devices, per_device(): lax.psum_scatter(jnp.stack([trans_times(gate_grad, feed_low), trans_times...  1930 us
    reduce_scatter x1, waiting for transfers between devices, per_device(): lax.psum_scatter(key_term, ('shard', 'seq'), scatter_dimension=0, tiled=T...  187 us
    reduce_scatter x1, waiting for transfers between devices, per_device(): lax.psum_scatter(query_term, ('shard', 'seq'), scatter_dimension=0, tiled...  187 us
    reduce_scatter x1, waiting for transfers between devices, per_device(): lax.psum_scatter(value_term, ('shard', 'seq'), scatter_dimension=0, tiled...  187 us
    reduce_scatter x1, waiting for transfers between devices, per_device(): lax.psum_scatter(output_term, ('shard', 'seq'), scatter_dimension=0, tile...  183 us
    all_gather x1, waiting for transfers between devices, per_device(): lax.all_gather(gate_weight, ('shard', 'seq'), axis=0, tiled=True)  178 us
    all_gather x1, waiting for transfers between devices, per_device(): lax.all_gather(down_weight, ('shard', 'seq'), axis=0, tiled=True)  178 us
    another operation x1, other arithmetic, per_device(): jnp.stack([trans_times(gate_grad, feed_low), trans_times(up_grad, feed_lo...  130 us
  transfers between devices with their start and end apart: 16, of which 14 were waited for; matrix products, arithmetic and copies ran while one was open for 11% of the time, Pallas kernels for 0%

commit v1 on v0

--- a/solution.py
+++ b/solution.py
@@ -1,8 +1,11 @@
+import functools
 import math
 
 import jax
 import jax.numpy as jnp
 from jax import lax
+from jax.experimental import pallas as pl
+from jax.experimental.pallas import tpu as pltpu
 from jax.sharding import PartitionSpec as P
 
 HEAD_DIM = 64
@@ -74,7 +77,7 @@
     )
 
 
-def per_device(
+def per_device_any(
     layer_input,
     doc_lengths,
     norm_gain,
@@ -314,9 +317,515 @@
     )
 
 
+HEADS = 32
+BF16 = jnp.bfloat16
+F32 = jnp.float32
+
+
+def dot_nn(lhs_mat, rhs_mat):
+    return lax.dot_general(
+        lhs_mat, rhs_mat, (((1,), (0,)), ((), ())), preferred_element_type=jnp.float32
+    )
+
+
+def slot_block(slot, place, half):
+    z, core = place // 2, place % 2
+    return ((z + slot // 2) % half) * 2 + (core + slot) % 2
+
+
+def fwd_kernel(tok, place_ref, lo_ref, full_ref, start_ref, qkv_ref, out_ref, blocks_ref, lse_ref,
+               k_nat, m_s, l_s, acc_s):
+    i = pl.program_id(0)
+    spans, rows, span = qkv_ref.shape
+    slots = span // tok
+    place = place_ref[0]
+    scale2 = HEAD_DIM ** -0.5 * math.log2(math.e)
+
+    @pl.when(i == 0)
+    def _():
+        for s in range(spans):
+            k_nat[pl.ds(s * span, span), :] = qkv_ref[s, HEAD_DIM : 2 * HEAD_DIM, :].T
+
+    q_t = qkv_ref[i, :HEAD_DIM, :]
+    m_s[...] = jnp.full_like(m_s, -1e30)
+    l_s[...] = jnp.zeros_like(l_s)
+    acc_s[...] = jnp.zeros_like(acc_s)
+
+    def step(j, masked):
+        s_t = dot_nn(k_nat[pl.ds(pl.multiple_of(j * span, span), span), :], q_t) * scale2
+        if masked:
+            s_t = jnp.where(allowed_pairs(i, j, place, tok, span, start_ref), s_t, -jnp.inf)
+        m_old = m_s[...]
+        m_new = jnp.maximum(m_old, jnp.max(s_t, axis=0, keepdims=True))
+        alpha = jnp.exp2(m_old - m_new)
+        p_t = jnp.exp2(s_t - m_new)
+        l_s[...] = l_s[...] * alpha + jnp.sum(p_t, axis=0, keepdims=True)
+        m_s[...] = m_new
+        acc_s[...] = acc_s[...] * alpha + dot_nn(
+            qkv_ref[j, 2 * HEAD_DIM :, :], p_t.astype(jnp.bfloat16)
+        )
+
+    def loop_body(masked):
+        def body(j, carry):
+            step(j, masked)
+            return carry
+
+        return body
+
+    lax.fori_loop(lo_ref[i], full_ref[i], loop_body(True), 0)
+    lax.fori_loop(full_ref[i], i, loop_body(False), 0)
+    step(i, True)
+    out = acc_s[...] / l_s[...]
+    out_ref[...] = out
+    lse_ref[...] = m_s[...] + jnp.log2(l_s[...])
+    for slot in range(slots):
+        blocks_ref[slot_block(slot, place, slots // 2)] = out[
+            :, slot * tok : (slot + 1) * tok
+        ].astype(jnp.bfloat16)
+
+
+def span_positions_of(lane, place, tok, span):
+    half = span // tok // 2
+    return slot_block(lane // tok, place, half) * tok + lane % tok
+
+
+def allowed_pairs(i, j, place, tok, span, start_ref):
+    k_lane = lax.broadcasted_iota(jnp.int32, (span, 128), 0)
+    k_pos = (j * span + span_positions_of(k_lane, place, tok, span))[:, :1]
+    q_lane = lax.broadcasted_iota(jnp.int32, (8, span), 1)
+    q_pos = (i * span + span_positions_of(q_lane, place, tok, span))[:1]
+    start = start_ref[i]
+    return (k_pos <= q_pos) & (k_pos >= start)
+
+
+def bwd_kernel(tok, place_ref, hi_ref, full_ref, start_ref, qkv_ref, lse_ref, out_ref, dob_ref,
+               dq_ref, dk_ref, dv_ref, dk_s, dv_s, do_s, di_s):
+    j = pl.program_id(0)
+    spans, rows, span = qkv_ref.shape
+    slots = span // tok
+    place = place_ref[0]
+    scale = HEAD_DIM ** -0.5
+    scale2 = scale * math.log2(math.e)
+
+    @pl.when(j == 0)
+    def _():
+        dq_ref[...] = jnp.zeros_like(dq_ref)
+        for s in range(spans):
+            for slot in range(slots):
+                do_s[s, :, slot * tok : (slot + 1) * tok] = dob_ref[
+                    s * slots + slot_block(slot, place, slots // 2)
+                ]
+            cols = slice(s * span, (s + 1) * span)
+            di_s[s] = jnp.sum(do_s[s].astype(jnp.float32) * out_ref[:, cols], axis=0, keepdims=True)
+
+    k_t = qkv_ref[j, HEAD_DIM : 2 * HEAD_DIM, :]
+    k_nat = k_t.T
+    v_nat = qkv_ref[j, 2 * HEAD_DIM :, :].T
+    dk_s[...] = jnp.zeros_like(dk_s)
+    dv_s[...] = jnp.zeros_like(dv_s)
+
+    def step(i, masked):
+        cols = pl.ds(pl.multiple_of(i * span, span), span)
+        q_t = qkv_ref[i, :HEAD_DIM, :]
+        p_t = jnp.exp2(dot_nn(k_nat, q_t) * scale2 - lse_ref[:, cols])
+        if masked:
+            p_t = jnp.where(allowed_pairs(i, j, place, tok, span, start_ref), p_t, 0.0)
+        do_t = do_s[i]
+        dv_s[...] += times_trans(do_t, p_t.astype(jnp.bfloat16))
+        ds_t = (p_t * (dot_nn(v_nat, do_t) - di_s[i])).astype(jnp.bfloat16)
+        dk_s[...] += times_trans(q_t, ds_t)
+        dq_ref[:, cols] += dot_nn(k_t, ds_t)
+
+    step(j, True)
+
+    def body(i, carry):
+        whole = full_ref[i] <= j
+
+        @pl.when(whole)
+        def _():
+            step(i, False)
+
+        @pl.when(jnp.logical_not(whole))
+        def _():
+            step(i, True)
+
+        return carry
+
+    lax.fori_loop(j + 1, hi_ref[j], body, 0)
+    dk_ref[...] = dk_s[...] * scale
+    dv_ref[...] = dv_s[...]
+
+    @pl.when(j == pl.num_programs(0) - 1)
+    def _():
+        dq_ref[...] = dq_ref[...] * scale
+
+
+def doc_bounds(doc_lengths, positions):
+    spans, span = positions.shape
+    ends = jnp.cumsum(doc_lengths)
+    over = ends[:, None, None] <= positions[None]
+    start = jnp.max(jnp.where(over, ends[:, None, None], 0), axis=0).astype(jnp.int32)
+    stop = jnp.min(jnp.where(over, spans * span, ends[:, None, None]), axis=0).astype(jnp.int32)
+    first = jnp.min(start, axis=1) // span
+    whole = jnp.minimum(
+        (jnp.max(start, axis=1) + span - 1) // span, jnp.arange(spans, dtype=jnp.int32)
+    )
+    last = (jnp.max(stop, axis=1) + span - 1) // span
+    return start[:, None, :], first, whole, last
+
+
+def attend(qkv, tok, place, bounds):
+    spans, rows, span = qkv.shape
+    stream = spans * span
+    slots = span // tok
+    start, first, whole, last = bounds
+    smem = pl.BlockSpec(memory_space=pltpu.SMEM)
+    vmem = pl.BlockSpec(memory_space=pltpu.VMEM)
+    return pl.pallas_call(
+        functools.partial(fwd_kernel, tok),
+        grid=(spans,),
+        in_specs=[smem, smem, smem, vmem, vmem],
+        out_specs=[
+            pl.BlockSpec((HEAD_DIM, span), lambda i: (0, i)),
+            pl.BlockSpec((slots, HEAD_DIM, tok), lambda i: (i, 0, 0)),
+            pl.BlockSpec((1, span), lambda i: (0, i)),
+        ],
+        out_shape=[
+            jax.ShapeDtypeStruct((HEAD_DIM, stream), jnp.float32),
+            jax.ShapeDtypeStruct((stream // tok, HEAD_DIM, tok), jnp.bfloat16),
+            jax.ShapeDtypeStruct((1, stream), jnp.float32),
+        ],
+        scratch_shapes=[
+            pltpu.VMEM((stream, HEAD_DIM), jnp.bfloat16),
+            pltpu.VMEM((1, span), jnp.float32),
+            pltpu.VMEM((1, span), jnp.float32),
+            pltpu.VMEM((HEAD_DIM, span), jnp.float32),
+        ],
+        compiler_params=pltpu.CompilerParams(vmem_limit_bytes=40 * 2**20),
+        cost_estimate=pl.CostEstimate(
+            flops=stream * stream * 256 * 2, bytes_accessed=stream * 1024, transcendentals=stream * stream // 2
+        ),
+        name="attend",
+    )(place, first, whole, start, qkv)
+
+
+def attend_back(qkv, lse, out, out_grad, tok, place, bounds):
+    spans, rows, span = qkv.shape
+    stream = spans * span
+    start, first, whole, last = bounds
+    smem = pl.BlockSpec(memory_space=pltpu.SMEM)
+    vmem = pl.BlockSpec(memory_space=pltpu.VMEM)
+    return pl.pallas_call(
+        functools.partial(bwd_kernel, tok),
+        grid=(spans,),
+        in_specs=[smem, smem, smem, vmem, vmem, vmem, vmem, vmem],
+        out_specs=[
+            pl.BlockSpec((HEAD_DIM, stream), lambda j: (0, 0)),
+            pl.BlockSpec((HEAD_DIM, span), lambda j: (0, j)),
+            pl.BlockSpec((HEAD_DIM, span), lambda j: (0, j)),
+        ],
+        out_shape=[jax.ShapeDtypeStruct((HEAD_DIM, stream), jnp.float32)] * 3,
+        scratch_shapes=[
+            pltpu.VMEM((HEAD_DIM, span), jnp.float32),
+            pltpu.VMEM((HEAD_DIM, span), jnp.float32),
+            pltpu.VMEM((spans, HEAD_DIM, span), jnp.bfloat16),
+            pltpu.VMEM((spans, 1, span), jnp.float32),
+        ],
+        compiler_params=pltpu.CompilerParams(vmem_limit_bytes=40 * 2**20),
+        cost_estimate=pl.CostEstimate(
+            flops=5 * stream * stream * 256, bytes_accessed=stream * 2048, transcendentals=stream * stream // 2
+        ),
+        name="attend_back",
+    )(place, whole_last(last), whole, start, qkv, lse, out, out_grad)
+
+
+def whole_last(last):
+    return last
+
+
+def swap_cores(values):
+    count = lax.axis_size("seq")
+    return lax.ppermute(values, "seq", [(i, i ^ 1) for i in range(count)])
+
+
+def from_chip(values, step):
+    count = lax.axis_size("seq")
+    return lax.ppermute(values, "seq", [((i + 2 * step) % count, i) for i in range(count)])
+
+
+def from_shard(values, flip):
+    return lax.ppermute(values, "shard", [(i, i ^ flip) for i in range(4)])
+
+
+def gather_seq(values):
+    half = lax.axis_size("seq") // 2
+    same = [values] + [from_chip(values, step) for step in range(1, half)]
+    return [block for one in same for block in (one, swap_cores(one))]
+
+
+def scatter_seq(parts):
+    half = lax.axis_size("seq") // 2
+    total = None
+    for step in range(half):
+        pair = parts[2 * step].astype(F32) + swap_cores(parts[2 * step + 1].astype(BF16)).astype(F32)
+        if step:
+            pair = from_chip(pair.astype(BF16), -step).astype(F32)
+        total = pair if total is None else total + pair
+    return total
+
+
+def gather_shard(block):
+    rows = block.shape[0] // 2
+    one, two = from_shard(block, 1), from_shard(block, 2)
+    far = [from_shard(one[:rows], 2), from_shard(two[rows:], 1)]
+    return [block, one, two, jnp.concatenate(far)]
+
+
+def scatter_shard(parts):
+    rows = parts[3].shape[0] // 2
+    low = parts[3].astype(BF16)
+    top, bottom = from_shard(low[:rows], 1), from_shard(low[rows:], 2)
+    one = jnp.concatenate([parts[1][:rows], parts[1][rows:] + bottom.astype(F32)])
+    two = jnp.concatenate([parts[2][:rows] + top.astype(F32), parts[2][rows:]])
+    return (
+        parts[0]
+        + from_shard(one.astype(BF16), 1).astype(F32)
+        + from_shard(two.astype(BF16), 2).astype(F32)
+    )
+
+
+def to_natural_shards(slots):
+    own = lax.axis_index("shard")
+    stacked = jnp.stack(slots)
+    return jnp.concatenate(
+        [lax.dynamic_index_in_dim(stacked, own ^ k, 0, keepdims=False) for k in range(4)]
+    )
+
+
+def bits_of(flat):
+    seq_bits = [("seq", 1 << b) for b in range(lax.axis_size("seq").bit_length() - 1)]
+    return seq_bits + [("shard", 1), ("shard", 2)]
+
+
+def gather_small(row):
+    rows = row
+    for axis, flip in bits_of(row):
+        count = lax.axis_size(axis)
+        other = lax.ppermute(rows, axis, [(i, i ^ flip) for i in range(count)])
+        upper = (lax.axis_index(axis) & flip) != 0
+        rows = jnp.concatenate(
+            [jnp.where(upper, other, rows), jnp.where(upper, rows, other)], axis=0
+        )
+    return rows
+
+
+def scatter_small(rows):
+    for axis, flip in reversed(bits_of(rows)):
+        count = lax.axis_size(axis)
+        upper = (lax.axis_index(axis) & flip) != 0
+        half = rows.shape[0] // 2
+        keep = jnp.where(upper, rows[half:], rows[:half])
+        give = jnp.where(upper, rows[:half], rows[half:])
+        rows = keep + lax.ppermute(give, axis, [(i, i ^ flip) for i in range(count)])
+    return rows
+
+
+def rotate_rows(front, back, cos_t, sin_t):
+    return jnp.concatenate([front * cos_t - back * sin_t, back * cos_t + front * sin_t], axis=-2)
+
+
+def per_device(
+    layer_input,
+    doc_lengths,
+    norm_gain,
+    query_weight,
+    key_weight,
+    value_weight,
+    output_weight,
+    feed_gain,
+    gate_weight,
+    up_weight,
+    down_weight,
+    output_grad,
+):
+    tok, width = layer_input.shape
+    seqs, shards = lax.axis_size("seq"), lax.axis_size("shard")
+    shard, seq = lax.axis_index("shard"), lax.axis_index("seq")
+    span = tok * seqs
+    half_head = HEAD_DIM // 2
+    place = jnp.reshape(seq, (1,)).astype(jnp.int32)
+
+    lanes = jnp.arange(span, dtype=jnp.int32)
+    in_span = slot_block(lanes // tok, seq.astype(jnp.int32), seqs // 2) * tok + lanes % tok
+    positions = jnp.arange(shards, dtype=jnp.int32)[:, None] * span + in_span[None]
+    bounds = doc_bounds(doc_lengths, positions)
+    exponent = -2.0 * jnp.arange(half_head, dtype=jnp.float32) / HEAD_DIM
+    inverse = jnp.power(jnp.float32(ROPE_BASE), exponent)
+    angles = positions.astype(F32)[:, None, :] * inverse[None, :, None]
+    cos_all, sin_all = jnp.cos(angles), jnp.sin(angles)
+    cos_own = lax.dynamic_index_in_dim(cos_all, shard, 0, keepdims=False)
+    sin_own = lax.dynamic_index_in_dim(sin_all, shard, 0, keepdims=False)
+
+    inputs_slots = gather_seq(layer_input)
+    gain_col = norm_gain.astype(F32)[:, None]
+    heads_here = HEADS // seqs
+    own_rows = query_weight.shape[0]
+    packed = jnp.stack(
+        [
+            (weight.astype(F32) * gain_col).astype(BF16).reshape(own_rows, shards, seqs, HEAD_DIM)
+            for weight in (query_weight, key_weight, value_weight)
+        ],
+        axis=2,
+    )
+    packed = jnp.transpose(packed, (3, 0, 1, 2, 4)).reshape(seqs, own_rows, heads_here * 3 * HEAD_DIM)
+    columns = lax.all_to_all(packed, "seq", split_axis=0, concat_axis=0, tiled=True)
+    columns = to_natural_shards(
+        gather_shard(columns.reshape(seqs * own_rows, heads_here * 3 * HEAD_DIM))
+    )
+
+    span_inputs = jnp.concatenate(inputs_slots).astype(F32)
+    scale_span = lax.rsqrt(jnp.mean(span_inputs * span_inputs, axis=-1, keepdims=True) + NORM_EPS)
+    unit_low = (span_inputs * scale_span).astype(BF16)
+    qkv = lax.dot_general(
+        columns, unit_low, (((0,), (1,)), ((), ())), preferred_element_type=F32
+    ).reshape(shards, 3, HEAD_DIM, span)
+    turned = rotate_rows(
+        qkv[:, :2, :half_head], qkv[:, :2, half_head:], cos_own[None, None], sin_own[None, None]
+    )
+    qkv_low = jnp.concatenate([turned, qkv[:, 2:]], axis=1).astype(BF16)
+    head_qkv = lax.all_to_all(
+        qkv_low.reshape(shards, 3 * HEAD_DIM, span), "shard", split_axis=0, concat_axis=0, tiled=True
+    )
+
+    head_out, out_blocks, lse = attend(head_qkv, tok, place, bounds)
+    token_out = lax.all_to_all(
+        out_blocks, ("shard", "seq"), split_axis=0, concat_axis=0, tiled=True
+    ).reshape(width, tok)
+
+    output_full = lax.all_gather(output_weight, ("shard", "seq"), axis=0, tiled=True)
+    gain_two = gather_small(feed_gain.astype(F32)[None, :]).reshape(1, width)
+    grad_slots = gather_seq(output_grad)
+    span_grad = jnp.concatenate(grad_slots)
+    gate_here = jnp.concatenate(gather_shard(gate_weight))
+    up_here = jnp.concatenate(gather_shard(up_weight))
+    down_here = jnp.concatenate(gather_shard(down_weight))
+
+    inputs = layer_input.astype(F32)
+    middle = inputs + trans_times(token_out, output_full)
+    normed_two, scale_two = normalize(middle, gain_two)
+    feed_low = jnp.concatenate(gather_seq(normed_two.astype(BF16)))
+
+    gate_val = times_trans(feed_low, gate_here)
+    up_val = times_trans(feed_low, up_here)
+    hidden_grad = times_trans(span_grad, down_here)
+    sigmoid_val = jax.nn.sigmoid(gate_val)
+    hidden = (gate_val * sigmoid_val * up_val).astype(BF16)
+    gate_grad = (
+        hidden_grad * up_val * (sigmoid_val * (1.0 + gate_val * (1.0 - sigmoid_val)))
+    ).astype(BF16)
+    up_grad = (hidden_grad * (gate_val * sigmoid_val)).astype(BF16)
+    feed_part = dot_nn(gate_grad, gate_here) + dot_nn(up_grad, up_here)
+    feed_grad = scatter_seq(feed_part.reshape(seqs, tok, width))
+
+    middle_norm_grad, gain_two_part = norm_back(feed_grad, middle, scale_two, gain_two)
+    middle_grad = output_grad.astype(F32) + middle_norm_grad
+    attend_grad = middle_grad.astype(BF16)
+    token_out_grad = times_trans(output_full, attend_grad).astype(BF16)
+    out_grad_blocks = lax.all_to_all(
+        token_out_grad.reshape(HEADS, HEAD_DIM, tok),
+        ("shard", "seq"),
+        split_axis=0,
+        concat_axis=0,
+        tiled=True,
+    )
+    query_grad, key_grad, value_grad = attend_back(
+        head_qkv, lse, head_out, out_grad_blocks, tok, place, bounds
+    )
+
+    def by_span(grad):
+        return jnp.transpose(grad.reshape(HEAD_DIM, shards, span), (1, 0, 2))
+
+    def turn_back(grad):
+        rows = by_span(grad)
+        return rotate_rows(rows[:, :half_head], rows[:, half_head:], cos_all, -sin_all)
+
+    back = jnp.concatenate(
+        [turn_back(query_grad), turn_back(key_grad), by_span(value_grad)], axis=1
+    ).astype(BF16)
+    span_back = lax.all_to_all(back, "shard", split_axis=0, concat_axis=0, tiled=True).reshape(
+        heads_here * 3 * HEAD_DIM, span
+    )
+    unit_part = lax.dot_general(
+        span_back, columns, (((0,), (1,)), ((), ())), preferred_element_type=F32
+    )
+    unit_grad = scatter_seq(unit_part.reshape(seqs, tok, width))
+    scale_one = lax.rsqrt(jnp.mean(inputs * inputs, axis=-1, keepdims=True) + NORM_EPS)
+    unit_rows = inputs * scale_one
+    input_grad = (
+        middle_grad
+        + scale_one * (unit_grad - unit_rows * jnp.mean(unit_grad * unit_rows, axis=-1, keepdims=True))
+    ).astype(BF16)
+
+    cols_part = lax.dot_general(
+        unit_low, span_back, (((0,), (1,)), ((), ())), preferred_element_type=F32
+    ).reshape(shards, seqs * own_rows, heads_here * 3 * HEAD_DIM)
+    cols_sum = scatter_shard(
+        [lax.dynamic_index_in_dim(cols_part, shard ^ k, 0, keepdims=False) for k in range(4)]
+    )
+    cols_all = lax.all_to_all(
+        cols_sum.astype(BF16).reshape(seqs, own_rows, -1), "seq", split_axis=0, concat_axis=0, tiled=True
+    ).reshape(seqs, own_rows, shards, 3, HEAD_DIM)
+    unit_wgrads = jnp.transpose(cols_all, (3, 1, 2, 0, 4)).reshape(3, own_rows, width).astype(F32)
+    query_wgrad, key_wgrad, value_wgrad = [unit_wgrads[i] * gain_col for i in range(3)]
+    gain_one_out = sum(
+        jnp.sum(unit_wgrads[i] * weight.astype(F32), axis=1)
+        for i, weight in enumerate((query_weight, key_weight, value_weight))
+    )
+
+    out_low = by_span(head_out).astype(BF16)
+    out_slots = jnp.concatenate(
+        [
+            from_shard(lax.dynamic_index_in_dim(out_low, shard ^ k, 0, keepdims=False), k)
+            if k
+            else lax.dynamic_index_in_dim(out_low, shard, 0, keepdims=False)
+            for k in range(4)
+        ]
+    )
+    span_attend_grad = jnp.concatenate(gather_seq(attend_grad))
+    out_part = dot_nn(out_slots, span_attend_grad).reshape(shards, HEAD_DIM, width)
+    output_wgrad = scatter_shard([out_part[k] for k in range(4)])
+    gain_two_out = scatter_small(gain_two_part.reshape(shards * seqs, -1)).reshape(-1)
+
+    down_part = dot_nn(hidden, down_here)
+    layer_output = (middle + scatter_seq(down_part.reshape(seqs, tok, width))).astype(BF16)
+
+    def feed_wgrad(lhs_mat, rhs_mat):
+        part = trans_times(lhs_mat, rhs_mat).reshape(shards, -1, width)
+        return scatter_shard([part[k] for k in range(4)])
+
+    down_wgrad = feed_wgrad(hidden, span_grad)
+    gate_wgrad = feed_wgrad(gate_grad, feed_low)
+    up_wgrad = feed_wgrad(up_grad, feed_low)
+    return (
+        layer_output,
+        input_grad,
+        gain_one_out,
+        query_wgrad,
+        key_wgrad,
+        value_wgrad,
+        output_wgrad,
+        gain_two_out,
+        gate_wgrad,
+        up_wgrad,
+        down_wgrad,
+    )
+
+
 def solution(mesh):
+    shards, seqs = mesh.shape["shard"], mesh.shape["seq"]
+    body = per_device if shards == 4 and shards * seqs == HEADS else per_device_any
     return jax.shard_map(
-        per_device,
+        body,
         mesh=mesh,
         in_specs=(
             P(("shard", "seq"), None),

time: 4370 us -> 912 us (0.21)
  waiting for transfers between devices: 3420 us -> 375 us
  matrix products: 416 us -> 104 us
  blocking collectives: 220 us -> 0 us
  starting transfers between devices: 23.4 us -> 141 us
  other arithmetic: 178 us -> 83.4 us
  Pallas kernels: 0 us -> 59.5 us
  local copies, waits for them, and re-layouts: 72.6 us -> 122 us
    reduce_scatter x6 -> x0, waiting for transfers between devices: 2670 us -> none  [the longest x1 1930 us: per_device(): lax.psum_scatter(jnp.stack([trans_times(gate_grad, feed_low), trans_times...]
    all_gather x7 -> x0, waiting for transfers between devices: 706 us -> none  [the longest x1 178 us: per_device(): lax.all_gather(gate_weight, ('shard', 'seq'), axis=0, tiled=True)]
    ppermute x0 -> x98, waiting for transfers between devices: none -> 371 us  [the longest x21 175 us: from_chip(): lax.ppermute(values, 'seq', [((i + 2 * step) % count, i) for i in range(c...]
    dot_general x63 -> x7, matrix products: 229 us -> 41.5 us  [the longest x4 28.4 us: dot_nn(): lax.dot_general(lhs_mat, rhs_mat, (((1,), (0,)), ((), ())), preferred_ele...]
    all_to_all x2 -> x0, blocking collectives: 135 us -> none  [the longest x1 84.9 us: per_device(): lax.all_to_all(back_stack, 'seq', split_axis=1, concat_axis=2, tiled=True)]
    another operation x11, other arithmetic: 137 us -> 7.2 us  [the longest x1 130 us: per_device(): jnp.stack([trans_times(gate_grad, feed_low), trans_times(up_grad, feed_lo...]
    ppermute x0 -> x98, starting transfers between devices: none -> 113 us  [the longest x21 57.7 us: from_chip(): lax.ppermute(values, 'seq', [((i + 2 * step) % count, i) for i in range(c...]
    unnamed x2 -> x0, blocking collectives: 85 us -> none
  transfers between devices with their start and end apart: 16 -> 105, of which waited for: 14 -> 39; matrix products, arithmetic and copies ran while one was open for 11% -> 24% of each run, Pallas kernels for 0% -> 7%
where the time goes in v1:
time: 912 us; the launch traced here: 900 us
  waiting for transfers between devices  375 us (41%)
  starting transfers between devices  141 us (15%)
  local copies, waits for them, and re-layouts  122 us (13%)
  matrix products  104 us (11%)
  other arithmetic  83.4 us (9%)
  Pallas kernels  59.5 us (7%)
  between operations  15.6 us (2%)
    ppermute x21, waiting for transfers between devices, from_chip(): lax.ppermute(values, 'seq', [((i + 2 * step) % count, i) for i in range(c...  175 us
    ppermute x39, waiting for transfers between devices, from_shard(): return lax.ppermute(values, 'shard', [(i, i ^ flip) for i in range(4)])  134 us
    unnamed x148, local copies, waits for them, and re-layouts  63.7 us
    ppermute x21, starting transfers between devices, from_chip(): lax.ppermute(values, 'seq', [((i + 2 * step) % count, i) for i in range(c...  57.7 us
    ppermute x5, waiting for transfers between devices, gather_small(): other = lax.ppermute(rows, axis, [(i, i ^ flip) for i in range(count)])  55.5 us
    ppermute x39, starting transfers between devices, from_shard(): return lax.ppermute(values, 'shard', [(i, i ^ flip) for i in range(4)])  44.7 us
    dot_general x4, matrix products, times_trans(): lax.dot_general(lhs_mat, rhs_mat, (((1,), (1,)), ((), ())), preferred_ele...  35.1 us
    pallas_call x1, Pallas kernels, attend_back(): pl.pallas_call(functools.partial(bwd_kernel, tok), grid=(spans,), in_spec...  33 us
  transfers between devices with their start and end apart: 105, of which 39 were waited for; matrix products, arithmetic and copies ran while one was open for 24% of the time, Pallas kernels for 7%

profile of v1, /device:TPU:8, one launch (start us, length us, event | category | flops | bytes accessed | tf_op | source)
XLA Modules:
  0.0 900.0 jit_solution(4278009446961004880)
XLA Ops:
  42.5 23.6 %collective-permute-done.12 = f32[2,64]{1,0:T(2,128)S(1)} collective-permute-done((f32[2,64]{1,0:T(2,128)S(1)}, f32[2,64]{1,0:T(2,128)S(1)}, u32[]{:S(2)}, u32[]{:S(2)}) %collective-permute-start.12) | collective-permute-done | bytes 544 | tf_op jit(solution)/shard_map/ppermute | solution.py:614
  66.9 27.1 %collective-permute-done.13 = f32[4,64]{1,0:T(4,128)S(1)} collective-permute-done((f32[4,64]{1,0:T(4,128)S(1)}, f32[4,64]{1,0:T(4,128)S(1)}, u32[]{:S(2)}, u32[]{:S(2)}) %collective-permute-start.13) | collective-permute-done | bytes 1056 | tf_op jit(solution)/shard_map/ppermute | solution.py:614
  113.3 12.3 %collective-permute-done.43 = bf16[128,2048]{1,0:T(8,128)(2,1)S(1)} collective-permute-done((bf16[128,2048]{1,0:T(8,128)(2,1)S(1)}, bf16[128,2048]{1,0:T(8,128)(2,1)S(1)}, u32[]{:S(2)}, u32[]{:S(2)}) %collective-permute-start.43) | collective-permute-done | bytes 524320 | tf_op jit(solution)/shard_map/ppermute | solution.py:553
  132.4 15.3 %collective-permute-done.45 = bf16[128,2048]{1,0:T(8,128)(2,1)} collective-permute-done((bf16[128,2048]{1,0:T(8,128)(2,1)S(1)}, bf16[128,2048]{1,0:T(8,128)(2,1)}, u32[]{:S(2)}, u32[]{:S(2)}) %collective-permute-start.45) | collective-permute-done | bytes 524320 | tf_op jit(solution)/shard_map/ppermute | solution.py:553
  189.5 24.5 %collective-permute-done.1 = bf16[512,768]{1,0:T(8,128)(2,1)S(1)} collective-permute-done((bf16[512,768]{1,0:T(8,128)(2,1)S(1)}, bf16[512,768]{1,0:T(8,128)(2,1)S(1)}, u32[]{:S(2)}, u32[]{:S(2)}) %collective-permute-start.1) | collective-permute-done | bytes 786464 | tf_op jit(solution)/shard_map/ppermute | solution.py:557
  228.2 9.3 %collective-permute-done.2 = bf16[256,768]{1,0:T(8,128)(2,1)S(1)} collective-permute-done((bf16[256,768]{1,0:T(8,128)(2,1)S(1)}, bf16[256,768]{1,0:T(8,128)(2,1)S(1)}, u32[]{:S(2)}, u32[]{:S(2)}) %collective-permute-start.2) | collective-permute-done | bytes 393248 | tf_op jit(solution)/shard_map/ppermute | solution.py:557
  273.1 26.6 %attend.1 = (f32[64,4096]{1,0:T(8,128)S(1)}, bf16[32,64,128]{2,1,0:T(8,128)(2,1)}, f32[1,4096]{1,0:T(1,128)S(1)}) custom-call(s32[1]{0:T(128)} %bitcast.place_ref, s32[4]{0:T(128)S(1)} %get-tuple-element.147.lo_ref, s32[4]{0:T(128)S(1)} %get-tuple-element.148.full_ref, s32[4,1,1024]{2,1,0:T(1,128)S(1)} %broadcast_in_dim.28.start_ref, ...), custom_call_target="tpu_custom_call" | custom-call | flops 8589934592 | bytes 4194304 | tf_op jit(solution)/shard_map/attend/pallas_call | solution.py:484
  305.4 10.1 %fusion.133 = f32[1024,1024]{1,0:T(8,128)} fusion(bf16[1024,2048]{1,0:T(8,128)(2,1)} %constant_dynamic-update-slice_fusion.31, bf16[1024,2048]{1,0:T(8,128)(2,1)} %constant_dynamic-update-slice_fusion.26), kind=kOutput, calls=%fused_computation.336 | convolution fusion | flops 4294967296 | bytes 12582912 | tf_op jit(solution)/shard_map/dot_general | solution.py:69
  338.8 25.2 %collective-permute-done.17 = bf16[128,2048]{1,0:T(8,128)(2,1)} collective-permute-done((bf16[128,2048]{1,0:T(8,128)(2,1)}, bf16[128,2048]{1,0:T(8,128)(2,1)}, u32[]{:S(2)}, u32[]{:S(2)}) %collective-permute-start.17) | collective-permute-done | bytes 524320 | tf_op jit(solution)/shard_map/ppermute | solution.py:553
  379.8 8.6 fusion.132
  388.5 9.9 %multiply_convert_fusion.1 = (bf16[1024,1024]{1,0:T(8,128)(2,1)S(1)}, bf16[1024,1024]{1,0:T(8,128)(2,1)S(1)}, bf16[1024,1024]{1,0:T(8,128)(2,1)S(1)}) fusion(f32[1024,1024]{1,0:T(8,128)} %fusion.133, f32[1024,1024]{1,0:T(8,128)} %fusion.132, bf16[1024,2048]{1,0:T(8,128)(2,1)S(1)} %copy-done.5, bf16[1024,2048]{1,0:T(8,128)(2,1)} %constant_dynamic-update-slice_fusion.16), kind=kOutput, calls=%fused_computation.5 | convolution fusion | flops 4310695936 | bytes 23068672 | tf_op jit(solution)/shard_map/dot_general | solution.py:69
  434.8 10.8 %fusion.125 = (bf16[1024,2048]{1,0:T(8,128)(2,1)}, f32[1024,2048]{1,0:T(8,128)}) fusion(f32[1024,2048]{1,0:T(8,128)} %fusion.134, bf16[1024,1024]{1,0:T(8,128)(2,1)S(1)} %get-tuple-element.45, bf16[1024,2048]{1,0:T(8,128)(2,1)} %constant_dynamic-update-slice_fusion.16), kind=kOutput, calls=%fused_computation.328 | convolution fusion | flops 4299161600 | bytes 27262976 | tf_op jit(solution)/shard_map/dot_general | solution.py:326
  453.2 11.1 %collective-permute-done.86 = bf16[128,2048]{1,0:T(8,128)(2,1)S(1)} collective-permute-done((bf16[128,2048]{1,0:T(8,128)(2,1)S(1)}, bf16[128,2048]{1,0:T(8,128)(2,1)S(1)}, u32[]{:S(2)}, u32[]{:S(2)}) %collective-permute-start.86) | collective-permute-done | bytes 524320 | tf_op jit(solution)/shard_map/ppermute | solution.py:557
  504.8 20.6 %collective-permute-done.53 = bf16[128,2048]{1,0:T(8,128)(2,1)S(1)} collective-permute-done((bf16[128,2048]{1,0:T(8,128)(2,1)S(1)}, bf16[128,2048]{1,0:T(8,128)(2,1)S(1)}, u32[]{:S(2)}, u32[]{:S(2)}) %collective-permute-start.53) | collective-permute-done | bytes 524320 | tf_op jit(solution)/shard_map/ppermute | solution.py:553
  525.4 11.1 %collective-permute-done.51 = bf16[128,2048]{1,0:T(8,128)(2,1)S(1)} collective-permute-done((bf16[128,2048]{1,0:T(8,128)(2,1)S(1)}, bf16[128,2048]{1,0:T(8,128)(2,1)S(1)}, u32[]{:S(2)}, u32[]{:S(2)}) %collective-permute-start.51) | collective-permute-done | bytes 524320 | tf_op jit(solution)/shard_map/ppermute | solution.py:553
  578.1 25.5 %collective-permute-done.73 = bf16[128,2048]{1,0:T(8,128)(2,1)} collective-permute-done((bf16[128,2048]{1,0:T(8,128)(2,1)}, bf16[128,2048]{1,0:T(8,128)(2,1)}, u32[]{:S(2)}, u32[]{:S(2)}) %collective-permute-start.73) | collective-permute-done | bytes 524320 | tf_op jit(solution)/shard_map/ppermute | solution.py:553
  608.9 33.0 %attend_back.1 = (f32[64,4096]{1,0:T(8,128)S(1)}, f32[64,4096]{1,0:T(8,128)S(1)}, f32[64,4096]{1,0:T(8,128)S(1)}) custom-call(s32[1]{0:T(128)} %bitcast.place_ref, s32[4]{0:T(128)S(1)} %and_select_fusion.hi_ref, s32[4]{0:T(128)S(1)} %get-tuple-element.148.full_ref, s32[4,1,1024]{2,1,0:T(1,128)S(1)} %broadcast_in_dim.28.start_ref, ...), custom_call_target="tpu_custom_call" | custom-call | flops 21474836480 | bytes 8388608 | tf_op jit(solution)/shard_map/attend_back/pallas_call | solution.py:518
  673.5 8.8 collective-permute-done.67
  688.1 13.8 %collective-permute-done.93 = bf16[256,2048]{1,0:T(8,128)(2,1)S(1)} collective-permute-done((bf16[256,2048]{1,0:T(8,128)(2,1)}, bf16[256,2048]{1,0:T(8,128)(2,1)S(1)}, u32[]{:S(2)}, u32[]{:S(2)}) %collective-permute-start.93) | collective-permute-done | bytes 1048608 | tf_op jit(solution)/shard_map/ppermute | solution.py:557
  708.1 18.0 %collective-permute-done.77 = bf16[32,2048]{1,0:T(8,128)(2,1)S(1)} collective-permute-done((bf16[32,2048]{1,0:T(8,128)(2,1)S(1)}, bf16[32,2048]{1,0:T(8,128)(2,1)S(1)}, u32[]{:S(2)}, u32[]{:S(2)}) %collective-permute-start.77) | collective-permute-done | bytes 131104 | tf_op jit(solution)/shard_map/ppermute | solution.py:557
  796.6 18.3 %collective-permute-start.37 = (bf16[128,2048]{1,0:T(8,128)(2,1)}, bf16[128,2048]{1,0:T(8,128)(2,1)S(1)}, u32[]{:S(2)}, u32[]{:S(2)}) collective-permute-start(bf16[128,2048]{1,0:T(8,128)(2,1)} %get-tuple-element.48), channel_id=1, source_target_pairs={{6,0},{7,1},{0,2},{1,3},{2,4},{3,5},{4,6},{5,7},{14,8},{15,9},{8,1... | collective-permute-start | bytes 1572872 | tf_op jit(solution)/shard_map/ppermute | solution.py:553
  816.9 20.6 %collective-permute-done.58 = bf16[128,2048]{1,0:T(8,128)(2,1)} collective-permute-done((bf16[128,2048]{1,0:T(8,128)(2,1)}, bf16[128,2048]{1,0:T(8,128)(2,1)}, u32[]{:S(2)}, u32[]{:S(2)}) %collective-permute-start.58) | collective-permute-done | bytes 524320 | tf_op jit(solution)/shard_map/ppermute | solution.py:553
  839.9 17.2 %collective-permute-done.41 = bf16[128,2048]{1,0:T(8,128)(2,1)S(1)} collective-permute-done((bf16[128,2048]{1,0:T(8,128)(2,1)}, bf16[128,2048]{1,0:T(8,128)(2,1)S(1)}, u32[]{:S(2)}, u32[]{:S(2)}) %collective-permute-start.41) | collective-permute-done | bytes 524320 | tf_op jit(solution)/shard_map/ppermute | solution.py:553
  857.2 11.1 %collective-permute-done.37 = bf16[128,2048]{1,0:T(8,128)(2,1)S(1)} collective-permute-done((bf16[128,2048]{1,0:T(8,128)(2,1)}, bf16[128,2048]{1,0:T(8,128)(2,1)S(1)}, u32[]{:S(2)}, u32[]{:S(2)}) %collective-permute-start.37) | collective-permute-done | bytes 524320 | tf_op jit(solution)/shard_map/ppermute | solution.py:553
  (492 shorter events, 472.2 us)
Async XLA Ops:
  7.2 312.1 %all-gather.2.cloned.1.call-start = ((), (), s32[]{:S(2)}) async-start(), calls=%async_computation.6 | async-start | bytes 8650752 | tf_op jit(solution)/shard_map/all_gather | solution.py:705
  7.2 94.5 %collective-permute-start.4 = (bf16[128,2048]{1,0:T(8,128)(2,1)}, bf16[128,2048]{1,0:T(8,128)(2,1)}, u32[]{:S(2)}, u32[]{:S(2)}) collective-permute-start(bf16[128,2048]{1,0:T(8,128)(2,1)} %param.12), channel_id=1, source_target_pairs={{0,1},{1,0},{2,3},{3,2},{4,5},{5,4},{6,7},{7,6},{8,9},{9,8},{10,11... | collective-permute-start | bytes 1572872 | tf_op jit(solution)/shard_map/ppermute | solution.py:548
  7.3 94.6 %collective-permute-start.5 = (bf16[128,2048]{1,0:T(8,128)(2,1)}, bf16[128,2048]{1,0:T(8,128)(2,1)}, u32[]{:S(2)}, u32[]{:S(2)}) collective-permute-start(bf16[128,2048]{1,0:T(8,128)(2,1)} %param.12), channel_id=1, source_target_pairs={{2,0},{3,1},{4,2},{5,3},{6,4},{7,5},{0,6},{1,7},{10,8},{11,9},{12,... | collective-permute-start | bytes 1572872 | tf_op jit(solution)/shard_map/ppermute | solution.py:553
  7.4 102.1 %collective-permute-start.7 = (bf16[128,2048]{1,0:T(8,128)(2,1)}, bf16[128,2048]{1,0:T(8,128)(2,1)}, u32[]{:S(2)}, u32[]{:S(2)}) collective-permute-start(bf16[128,2048]{1,0:T(8,128)(2,1)} %param.12), channel_id=1, source_target_pairs={{4,0},{5,1},{6,2},{7,3},{0,4},{1,5},{2,6},{3,7},{12,8},{13,9},{14,... | collective-permute-start | bytes 1572872 | tf_op jit(solution)/shard_map/ppermute | solution.py:553
  10.4 120.2 %collective-permute-start.9 = (bf16[128,2048]{1,0:T(8,128)(2,1)}, bf16[128,2048]{1,0:T(8,128)(2,1)}, u32[]{:S(2)}, u32[]{:S(2)}) collective-permute-start(bf16[128,2048]{1,0:T(8,128)(2,1)} %param.12), channel_id=1, source_target_pairs={{6,0},{7,1},{0,2},{1,3},{2,4},{3,5},{4,6},{5,7},{14,8},{15,9},{8,1... | collective-permute-start | bytes 1572872 | tf_op jit(solution)/shard_map/ppermute | solution.py:553
  29.1 153.0 %all-to-all-start = ((bf16[8,64,768]{2,1,0:T(8,128)(2,1)}), bf16[8,64,768]{2,1,0:T(8,128)(2,1)S(1)}, u32[]{:S(2)}, u32[]{:S(2)}) async-start(bf16[8,64,768]{2,1,0:T(8,128)(2,1)} %reshape.402), calls=%async_computation | async-start | bytes 1572864 | tf_op jit(solution)/shard_map/all_to_all | solution.py:681
  157.3 62.2 %collective-permute-start.24 = (bf16[256,2048]{1,0:T(8,128)(2,1)}, bf16[256,2048]{1,0:T(8,128)(2,1)S(1)}, u32[]{:S(2)}, u32[]{:S(2)}) collective-permute-start(bf16[256,2048]{1,0:T(8,128)(2,1)} %param.20), channel_id=1, source_target_pairs={{0,16},{8,24},{16,0},{24,8},{1,17},{9,25},{17,1},{25,9},{2,18},{10... | collective-permute-start | bytes 3145736 | tf_op jit(solution)/shard_map/ppermute | solution.py:557
  166.5 88.2 %collective-permute-start.48 = (bf16[128,2048]{1,0:T(8,128)(2,1)}, bf16[128,2048]{1,0:T(8,128)(2,1)}, u32[]{:S(2)}, u32[]{:S(2)}) collective-permute-start(bf16[128,2048]{1,0:T(8,128)(2,1)} %collective-permute-done.47), channel_id=1, source_target_pairs={{0,1},{1,0},{2,3},{3,2},{4,5},{5,4},{6,7},{7,6},{8,9},{9,8},{10,11... | collective-permute-start | bytes 1572872 | tf_op jit(solution)/shard_map/ppermute | solution.py:548
  237.5 91.4 %collective-permute-start.30 = (bf16[128,2048]{1,0:T(8,128)(2,1)}, bf16[128,2048]{1,0:T(8,128)(2,1)}, u32[]{:S(2)}, u32[]{:S(2)}) collective-permute-start(bf16[128,2048]{1,0:T(8,128)(2,1)} %slice.521), channel_id=1, source_target_pairs={{0,8},{8,0},{16,24},{24,16},{1,9},{9,1},{17,25},{25,17},{2,10},{10... | collective-permute-start | bytes 1572872 | tf_op jit(solution)/shard_map/ppermute | solution.py:557
  254.8 76.0 %collective-permute-start.25 = (bf16[128,2048]{1,0:T(8,128)(2,1)}, bf16[128,2048]{1,0:T(8,128)(2,1)}, u32[]{:S(2)}, u32[]{:S(2)}) collective-permute-start(bf16[128,2048]{1,0:T(8,128)(2,1)} %slice.518), channel_id=1, source_target_pairs={{0,16},{8,24},{16,0},{24,8},{1,17},{9,25},{17,1},{25,9},{2,18},{10... | collective-permute-start | bytes 1572872 | tf_op jit(solution)/shard_map/ppermute | solution.py:557
  266.0 66.7 %collective-permute-start.26 = (bf16[128,2048]{1,0:T(8,128)(2,1)}, bf16[128,2048]{1,0:T(8,128)(2,1)}, u32[]{:S(2)}, u32[]{:S(2)}) collective-permute-start(bf16[128,2048]{1,0:T(8,128)(2,1)} %slice.519), channel_id=1, source_target_pairs={{0,8},{8,0},{16,24},{24,16},{1,9},{9,1},{17,25},{25,17},{2,10},{10... | collective-permute-start | bytes 1572872 | tf_op jit(solution)/shard_map/ppermute | solution.py:557
  501.5 102.9 %collective-permute-start.89 = (bf16[256,2048]{1,0:T(8,128)(2,1)}, bf16[256,2048]{1,0:T(8,128)(2,1)}, u32[]{:S(2)}, u32[]{:S(2)}) collective-permute-start(bf16[256,2048]{1,0:T(8,128)(2,1)} %pad_maximum_fusion.4), channel_id=1, source_target_pairs={{0,16},{8,24},{16,0},{24,8},{1,17},{9,25},{17,1},{25,9},{2,18},{10... | collective-permute-start | bytes 3145736 | tf_op jit(solution)/shard_map/ppermute | solution.py:557
  503.4 101.1 %collective-permute-start.87 = (bf16[256,2048]{1,0:T(8,128)(2,1)}, bf16[256,2048]{1,0:T(8,128)(2,1)}, u32[]{:S(2)}, u32[]{:S(2)}) collective-permute-start(bf16[256,2048]{1,0:T(8,128)(2,1)} %pad_maximum_fusion.3), channel_id=1, source_target_pairs={{0,8},{8,0},{16,24},{24,16},{1,9},{9,1},{17,25},{25,17},{2,10},{10... | collective-permute-start | bytes 3145736 | tf_op jit(solution)/shard_map/ppermute | solution.py:557
  571.4 100.1 %collective-permute-start.69 = (bf16[64,1024]{1,0:T(8,128)(2,1)}, bf16[64,1024]{1,0:T(8,128)(2,1)S(1)}, u32[]{:S(2)}, u32[]{:S(2)}) collective-permute-start(bf16[64,1024]{1,0:T(8,128)(2,1)} %bitcast.163), channel_id=1, source_target_pairs={{0,24},{8,16},{16,8},{24,0},{1,25},{9,17},{17,9},{25,1},{2,26},{10... | collective-permute-start | bytes 393224 | tf_op jit(solution)/shard_map/ppermute | solution.py:557
  575.7 96.0 %collective-permute-start.68 = (bf16[64,1024]{1,0:T(8,128)(2,1)}, bf16[64,1024]{1,0:T(8,128)(2,1)}, u32[]{:S(2)}, u32[]{:S(2)}) collective-permute-start(bf16[64,1024]{1,0:T(8,128)(2,1)} %bitcast.162), channel_id=1, source_target_pairs={{0,16},{8,24},{16,0},{24,8},{1,17},{9,25},{17,1},{25,9},{2,18},{10... | collective-permute-start | bytes 393224 | tf_op jit(solution)/shard_map/ppermute | solution.py:557
  604.4 60.3 %collective-permute-start.74 = (bf16[128,2048]{1,0:T(8,128)(2,1)}, bf16[128,2048]{1,0:T(8,128)(2,1)}, u32[]{:S(2)}, u32[]{:S(2)}) collective-permute-start(bf16[128,2048]{1,0:T(8,128)(2,1)} %collective-permute-done.73), channel_id=1, source_target_pairs={{0,1},{1,0},{2,3},{3,2},{4,5},{5,4},{6,7},{7,6},{8,9},{9,8},{10,11... | collective-permute-start | bytes 1572872 | tf_op jit(solution)/shard_map/ppermute | solution.py:548
  654.8 75.6 %all-to-all-start.4 = ((bf16[4,192,1024]{2,1,0:T(8,128)(2,1)}), bf16[4,192,1024]{2,1,0:T(8,128)(2,1)S(1)}, u32[]{:S(2)}, u32[]{:S(2)}) async-start(bf16[4,192,1024]{2,1,0:T(8,128)(2,1)} %fusion.69), calls=%async_computation.4 | async-start | bytes 3145728 | tf_op jit(solution)/shard_map/all_to_all | solution.py:755
  671.4 84.4 %collective-permute-start.97 = (bf16[256,2048]{1,0:T(8,128)(2,1)S(1)}, bf16[256,2048]{1,0:T(8,128)(2,1)}, u32[]{:S(2)}, u32[]{:S(2)}) collective-permute-start(bf16[256,2048]{1,0:T(8,128)(2,1)S(1)} %copy-done.28), channel_id=1, source_target_pairs={{0,16},{8,24},{16,0},{24,8},{1,17},{9,25},{17,1},{25,9},{2,18},{10... | collective-permute-start | bytes 3145736 | tf_op jit(solution)/shard_map/ppermute | solution.py:557
  671.6 84.8 %collective-permute-start.95 = (bf16[256,2048]{1,0:T(8,128)(2,1)}, bf16[256,2048]{1,0:T(8,128)(2,1)}, u32[]{:S(2)}, u32[]{:S(2)}) collective-permute-start(bf16[256,2048]{1,0:T(8,128)(2,1)} %pad_maximum_fusion.7), channel_id=1, source_target_pairs={{0,8},{8,0},{16,24},{24,16},{1,9},{9,1},{17,25},{25,17},{2,10},{10... | collective-permute-start | bytes 3145736 | tf_op jit(solution)/shard_map/ppermute | solution.py:557
  778.0 59.5 %collective-permute-start.58 = (bf16[128,2048]{1,0:T(8,128)(2,1)}, bf16[128,2048]{1,0:T(8,128)(2,1)}, u32[]{:S(2)}, u32[]{:S(2)}) collective-permute-start(bf16[128,2048]{1,0:T(8,128)(2,1)} %get-tuple-element.39), channel_id=1, source_target_pairs={{6,0},{7,1},{0,2},{1,3},{2,4},{3,5},{4,6},{5,7},{14,8},{15,9},{8,1... | collective-permute-start | bytes 1572872 | tf_op jit(solution)/shard_map/ppermute | solution.py:553
  782.6 90.4 %all-to-all-start.5 = ((bf16[8,64,768]{2,1,0:T(8,128)(2,1)}), bf16[8,64,768]{2,1,0:T(8,128)(2,1)}, u32[]{:S(2)}, u32[]{:S(2)}) async-start(bf16[8,64,768]{2,1,0:T(8,128)(2,1)} %bitcast.150), calls=%async_computation.5 | async-start | bytes 1572864 | tf_op jit(solution)/shard_map/all_to_all | solution.py:775
  787.2 70.0 %collective-permute-start.41 = (bf16[128,2048]{1,0:T(8,128)(2,1)}, bf16[128,2048]{1,0:T(8,128)(2,1)S(1)}, u32[]{:S(2)}, u32[]{:S(2)}) collective-permute-start(bf16[128,2048]{1,0:T(8,128)(2,1)} %get-tuple-element.49), channel_id=1, source_target_pairs={{2,0},{3,1},{4,2},{5,3},{6,4},{7,5},{0,6},{1,7},{10,8},{11,9},{12,... | collective-permute-start | bytes 1572872 | tf_op jit(solution)/shard_map/ppermute | solution.py:553
  787.7 69.5 %collective-permute-start.39 = (bf16[128,2048]{1,0:T(8,128)(2,1)}, bf16[128,2048]{1,0:T(8,128)(2,1)S(1)}, u32[]{:S(2)}, u32[]{:S(2)}) collective-permute-start(bf16[128,2048]{1,0:T(8,128)(2,1)} %get-tuple-element.50), channel_id=1, source_target_pairs={{4,0},{5,1},{6,2},{7,3},{0,4},{1,5},{2,6},{3,7},{12,8},{13,9},{14,... | collective-permute-start | bytes 1572872 | tf_op jit(solution)/shard_map/ppermute | solution.py:553
  796.6 71.7 %collective-permute-start.37 = (bf16[128,2048]{1,0:T(8,128)(2,1)}, bf16[128,2048]{1,0:T(8,128)(2,1)S(1)}, u32[]{:S(2)}, u32[]{:S(2)}) collective-permute-start(bf16[128,2048]{1,0:T(8,128)(2,1)} %get-tuple-element.48), channel_id=1, source_target_pairs={{6,0},{7,1},{0,2},{1,3},{2,4},{3,5},{4,6},{5,7},{14,8},{15,9},{8,1... | collective-permute-start | bytes 1572872 | tf_op jit(solution)/shard_map/ppermute | solution.py:553
  (134 other events, 2958.7 us)
Sparse Core Ops, SparseCore 0:
  13.0 125.5 all-gather.1

commit v2 on v1

--- a/solution.py
+++ b/solution.py
@@ -318,8 +318,16 @@
 
 
 HEADS = 32
+EXTRA = 16
 BF16 = jnp.bfloat16
 F32 = jnp.float32
+
+
+SHORT = pl.CostEstimate(flops=0, bytes_accessed=0, transcendentals=0)
+
+
+def in_hbm(arrays):
+    return [pltpu.with_memory_space_constraint(array, pltpu.HBM) for array in arrays]
 
 
 def dot_nn(lhs_mat, rhs_mat):
@@ -333,7 +341,7 @@
     return ((z + slot // 2) % half) * 2 + (core + slot) % 2
 
 
-def fwd_kernel(tok, place_ref, lo_ref, full_ref, start_ref, qkv_ref, out_ref, blocks_ref, lse_ref,
+def fwd_kernel(tok, place_ref, lo_ref, full_ref, start_ref, qkv_ref, gain_ref, out_ref, low_ref, blocks_ref, lse_ref,
                k_nat, m_s, l_s, acc_s):
     i = pl.program_id(0)
     spans, rows, span = qkv_ref.shape
@@ -351,10 +359,10 @@
     l_s[...] = jnp.zeros_like(l_s)
     acc_s[...] = jnp.zeros_like(acc_s)
 
-    def step(j, masked):
+    def step(j, masked, same=False):
         s_t = dot_nn(k_nat[pl.ds(pl.multiple_of(j * span, span), span), :], q_t) * scale2
         if masked:
-            s_t = jnp.where(allowed_pairs(i, j, place, tok, span, start_ref), s_t, -jnp.inf)
+            s_t = jnp.where(allowed_pairs(i, j, place, tok, span, start_ref, same), s_t, -jnp.inf)
         m_old = m_s[...]
         m_new = jnp.maximum(m_old, jnp.max(s_t, axis=0, keepdims=True))
         alpha = jnp.exp2(m_old - m_new)
@@ -374,14 +382,16 @@
 
     lax.fori_loop(lo_ref[i], full_ref[i], loop_body(True), 0)
     lax.fori_loop(full_ref[i], i, loop_body(False), 0)
-    step(i, True)
+    step(i, True, True)
     out = acc_s[...] / l_s[...]
-    out_ref[...] = out
-    lse_ref[...] = m_s[...] + jnp.log2(l_s[...])
+    out_ref[0] = out
+    low = out.astype(jnp.bfloat16)
+    low_ref[0] = low
+    lse_ref[0] = m_s[...] + jnp.log2(l_s[...])
     for slot in range(slots):
-        blocks_ref[slot_block(slot, place, slots // 2)] = out[
-            :, slot * tok : (slot + 1) * tok
-        ].astype(jnp.bfloat16)
+        at = slot_block(slot, place, slots // 2)
+        blocks_ref[at, :HEAD_DIM] = low[:, slot * tok : (slot + 1) * tok]
+        blocks_ref[at, HEAD_DIM:] = gain_ref[...]
 
 
 def span_positions_of(lane, place, tok, span):
@@ -389,17 +399,19 @@
     return slot_block(lane // tok, place, half) * tok + lane % tok
 
 
-def allowed_pairs(i, j, place, tok, span, start_ref):
+def allowed_pairs(i, j, place, tok, span, start_ref, same):
     k_lane = lax.broadcasted_iota(jnp.int32, (span, 128), 0)
     k_pos = (j * span + span_positions_of(k_lane, place, tok, span))[:, :1]
+    begun = k_pos >= start_ref[i]
+    if not same:
+        return begun
     q_lane = lax.broadcasted_iota(jnp.int32, (8, span), 1)
     q_pos = (i * span + span_positions_of(q_lane, place, tok, span))[:1]
-    start = start_ref[i]
-    return (k_pos <= q_pos) & (k_pos >= start)
+    return (k_pos <= q_pos) & begun
 
 
 def bwd_kernel(tok, place_ref, hi_ref, full_ref, start_ref, qkv_ref, lse_ref, out_ref, dob_ref,
-               dq_ref, dk_ref, dv_ref, dk_s, dv_s, do_s, di_s):
+               cos_ref, sin_ref, back_ref, dq_s, dk_s, dv_s, do_s, di_s):
     j = pl.program_id(0)
     spans, rows, span = qkv_ref.shape
     slots = span // tok
@@ -409,14 +421,13 @@
 
     @pl.when(j == 0)
     def _():
-        dq_ref[...] = jnp.zeros_like(dq_ref)
+        dq_s[...] = jnp.zeros_like(dq_s)
         for s in range(spans):
             for slot in range(slots):
                 do_s[s, :, slot * tok : (slot + 1) * tok] = dob_ref[
-                    s * slots + slot_block(slot, place, slots // 2)
+                    s * slots + slot_block(slot, place, slots // 2), :HEAD_DIM
                 ]
-            cols = slice(s * span, (s + 1) * span)
-            di_s[s] = jnp.sum(do_s[s].astype(jnp.float32) * out_ref[:, cols], axis=0, keepdims=True)
+            di_s[s] = jnp.sum(do_s[s].astype(jnp.float32) * out_ref[s], axis=0, keepdims=True)
 
     k_t = qkv_ref[j, HEAD_DIM : 2 * HEAD_DIM, :]
     k_nat = k_t.T
@@ -424,19 +435,18 @@
     dk_s[...] = jnp.zeros_like(dk_s)
     dv_s[...] = jnp.zeros_like(dv_s)
 
-    def step(i, masked):
-        cols = pl.ds(pl.multiple_of(i * span, span), span)
+    def step(i, masked, same=False):
         q_t = qkv_ref[i, :HEAD_DIM, :]
-        p_t = jnp.exp2(dot_nn(k_nat, q_t) * scale2 - lse_ref[:, cols])
+        p_t = jnp.exp2(dot_nn(k_nat, q_t) * scale2 - lse_ref[i])
         if masked:
-            p_t = jnp.where(allowed_pairs(i, j, place, tok, span, start_ref), p_t, 0.0)
+            p_t = jnp.where(allowed_pairs(i, j, place, tok, span, start_ref, same), p_t, 0.0)
         do_t = do_s[i]
         dv_s[...] += times_trans(do_t, p_t.astype(jnp.bfloat16))
         ds_t = (p_t * (dot_nn(v_nat, do_t) - di_s[i])).astype(jnp.bfloat16)
         dk_s[...] += times_trans(q_t, ds_t)
-        dq_ref[:, cols] += dot_nn(k_t, ds_t)
-
-    step(j, True)
+        dq_s[i] += dot_nn(k_t, ds_t)
+
+    step(j, True, True)
 
     def body(i, carry):
         whole = full_ref[i] <= j
@@ -452,12 +462,17 @@
         return carry
 
     lax.fori_loop(j + 1, hi_ref[j], body, 0)
-    dk_ref[...] = dk_s[...] * scale
-    dv_ref[...] = dv_s[...]
-
-    @pl.when(j == pl.num_programs(0) - 1)
-    def _():
-        dq_ref[...] = dq_ref[...] * scale
+
+    def turned_back(grad):
+        front, back_half = grad[: HEAD_DIM // 2], grad[HEAD_DIM // 2 :]
+        cos_t, sin_t = cos_ref[0], sin_ref[0]
+        return jnp.concatenate(
+            [front * cos_t + back_half * sin_t, back_half * cos_t - front * sin_t], axis=0
+        ).astype(jnp.bfloat16)
+
+    back_ref[0, :HEAD_DIM] = turned_back(dq_s[j] * scale)
+    back_ref[0, HEAD_DIM : 2 * HEAD_DIM] = turned_back(dk_s[...] * scale)
+    back_ref[0, 2 * HEAD_DIM :] = dv_s[...].astype(jnp.bfloat16)
 
 
 def doc_bounds(doc_lengths, positions):
@@ -474,26 +489,32 @@
     return start[:, None, :], first, whole, last
 
 
-def attend(qkv, tok, place, bounds):
+def attend(qkv, gain_rows, tok, place, bounds):
     spans, rows, span = qkv.shape
     stream = spans * span
     slots = span // tok
     start, first, whole, last = bounds
     smem = pl.BlockSpec(memory_space=pltpu.SMEM)
     vmem = pl.BlockSpec(memory_space=pltpu.VMEM)
+
+    def one(*block):
+        return pl.BlockSpec((1,) + block, lambda i: (i, 0, 0))
+
     return pl.pallas_call(
         functools.partial(fwd_kernel, tok),
         grid=(spans,),
-        in_specs=[smem, smem, smem, vmem, vmem],
+        in_specs=[smem, smem, smem, vmem, vmem, vmem],
         out_specs=[
-            pl.BlockSpec((HEAD_DIM, span), lambda i: (0, i)),
-            pl.BlockSpec((slots, HEAD_DIM, tok), lambda i: (i, 0, 0)),
-            pl.BlockSpec((1, span), lambda i: (0, i)),
+            one(HEAD_DIM, span),
+            one(HEAD_DIM, span),
+            pl.BlockSpec((slots, HEAD_DIM + EXTRA, tok), lambda i: (i, 0, 0)),
+            one(1, span),
         ],
         out_shape=[
-            jax.ShapeDtypeStruct((HEAD_DIM, stream), jnp.float32),
-            jax.ShapeDtypeStruct((stream // tok, HEAD_DIM, tok), jnp.bfloat16),
-            jax.ShapeDtypeStruct((1, stream), jnp.float32),
+            jax.ShapeDtypeStruct((spans, HEAD_DIM, span), jnp.float32),
+            jax.ShapeDtypeStruct((spans, HEAD_DIM, span), jnp.bfloat16),
+            pltpu.HBM((stream // tok, HEAD_DIM + EXTRA, tok), jnp.bfloat16),
+            jax.ShapeDtypeStruct((spans, 1, span), jnp.float32),
         ],
         scratch_shapes=[
             pltpu.VMEM((stream, HEAD_DIM), jnp.bfloat16),
@@ -501,46 +522,489 @@
             pltpu.VMEM((1, span), jnp.float32),
             pltpu.VMEM((HEAD_DIM, span), jnp.float32),
         ],
-        compiler_params=pltpu.CompilerParams(vmem_limit_bytes=40 * 2**20),
+        compiler_params=pltpu.CompilerParams(vmem_limit_bytes=24 * 2**20),
         cost_estimate=pl.CostEstimate(
-            flops=stream * stream * 256 * 2, bytes_accessed=stream * 1024, transcendentals=stream * stream // 2
+            flops=stream * stream * 256 * 5, bytes_accessed=stream * 1024, transcendentals=0
         ),
         name="attend",
-    )(place, first, whole, start, qkv)
-
-
-def attend_back(qkv, lse, out, out_grad, tok, place, bounds):
+    )(place, first, whole, start, qkv, gain_rows)
+
+
+def attend_back(qkv, lse, out, out_grad, cos_t, sin_t, tok, place, bounds):
     spans, rows, span = qkv.shape
     stream = spans * span
     start, first, whole, last = bounds
     smem = pl.BlockSpec(memory_space=pltpu.SMEM)
     vmem = pl.BlockSpec(memory_space=pltpu.VMEM)
+
+    def one(*block):
+        return pl.BlockSpec((1,) + block, lambda j: (j, 0, 0))
+
     return pl.pallas_call(
         functools.partial(bwd_kernel, tok),
         grid=(spans,),
-        in_specs=[smem, smem, smem, vmem, vmem, vmem, vmem, vmem],
-        out_specs=[
-            pl.BlockSpec((HEAD_DIM, stream), lambda j: (0, 0)),
-            pl.BlockSpec((HEAD_DIM, span), lambda j: (0, j)),
-            pl.BlockSpec((HEAD_DIM, span), lambda j: (0, j)),
-        ],
-        out_shape=[jax.ShapeDtypeStruct((HEAD_DIM, stream), jnp.float32)] * 3,
+        in_specs=[smem, smem, smem, vmem, vmem, vmem, vmem, vmem]
+        + [one(HEAD_DIM // 2, span)] * 2,
+        out_specs=one(rows, span),
+        out_shape=pltpu.HBM(qkv.shape, jnp.bfloat16),
         scratch_shapes=[
+            pltpu.VMEM((spans, HEAD_DIM, span), jnp.float32),
             pltpu.VMEM((HEAD_DIM, span), jnp.float32),
             pltpu.VMEM((HEAD_DIM, span), jnp.float32),
             pltpu.VMEM((spans, HEAD_DIM, span), jnp.bfloat16),
             pltpu.VMEM((spans, 1, span), jnp.float32),
         ],
-        compiler_params=pltpu.CompilerParams(vmem_limit_bytes=40 * 2**20),
+        compiler_params=pltpu.CompilerParams(vmem_limit_bytes=30 * 2**20),
         cost_estimate=pl.CostEstimate(
-            flops=5 * stream * stream * 256, bytes_accessed=stream * 2048, transcendentals=stream * stream // 2
+            flops=stream * stream * 256 * 7, bytes_accessed=stream * 1024, transcendentals=0
         ),
         name="attend_back",
-    )(place, whole_last(last), whole, start, qkv, lse, out, out_grad)
-
-
-def whole_last(last):
-    return last
+    )(place, last, whole, start, qkv, lse, out, out_grad, *in_hbm([cos_t, sin_t]))
+
+
+def pack_kernel(heads, place_ref, gain_ref, query_ref, key_ref, value_ref, out_ref):
+    steps = out_ref.shape[1]
+    seqs = 2 * steps
+    z, core = place_ref[0] // 2, place_ref[0] % 2
+    for m, ref in enumerate((query_ref, key_ref, value_ref)):
+        rows = (ref[...].astype(jnp.float32) * gain_ref[...]).astype(jnp.bfloat16)
+        for head in range(heads):
+            at = (head // seqs * 3 + m) * HEAD_DIM
+            other = (core + head) % 2
+            step = (head % seqs // 2 + steps - z) % steps
+            out_ref[other, step, :, at : at + HEAD_DIM] = rows[
+                :, head * HEAD_DIM : (head + 1) * HEAD_DIM
+            ]
+
+
+def pack_columns(place, gain_col, weights, seqs):
+    rows, width = weights[0].shape
+    heads = width // HEAD_DIM
+    vmem = pl.BlockSpec(memory_space=pltpu.VMEM)
+    return pl.pallas_call(
+        functools.partial(pack_kernel, heads),
+        in_specs=[pl.BlockSpec(memory_space=pltpu.SMEM)] + [vmem] * 4,
+        out_specs=vmem,
+        out_shape=jax.ShapeDtypeStruct(
+            (2, seqs // 2, rows, heads // seqs * 3 * HEAD_DIM), jnp.bfloat16
+        ),
+        cost_estimate=SHORT,
+        name="pack_columns",
+    )(place, gain_col, *weights)
+
+
+def order_kernel(index_ref, *refs):
+    out_ref = refs[-1]
+    rows = out_ref.shape[1]
+    count = 0
+    for ref in refs[:-1]:
+        for i in range(ref.shape[0] // rows):
+            out_ref[index_ref[count]] = ref[i * rows : (i + 1) * rows]
+            count += 1
+
+
+def order_blocks(pieces, index, rows):
+    vmem = pl.BlockSpec(memory_space=pltpu.VMEM)
+    blocks = sum(piece.shape[0] for piece in pieces) // rows
+    width = pieces[0].shape[1]
+    return pl.pallas_call(
+        order_kernel,
+        in_specs=[pl.BlockSpec(memory_space=pltpu.SMEM)] + [vmem] * len(pieces),
+        out_specs=vmem,
+        out_shape=jax.ShapeDtypeStruct((blocks, rows, width), pieces[0].dtype),
+        compiler_params=pltpu.CompilerParams(vmem_limit_bytes=12 * 2**20),
+        cost_estimate=SHORT,
+        name="order_blocks",
+    )(index, *pieces).reshape(blocks * rows, width)
+
+
+def spread_kernel(place_ref, own_ref, one_ref, two_ref, out_ref):
+    steps, _, rows, _ = out_ref.shape
+    z, core = place_ref[0] // 2, place_ref[0] % 2
+    total = own_ref[...] + one_ref[...].astype(jnp.float32) + two_ref[...].astype(jnp.float32)
+    total = total.astype(jnp.bfloat16)
+    for q in range(2 * steps):
+        out_ref[(q // 2 + steps - z) % steps, (core + q) % 2] = total[q * rows : (q + 1) * rows]
+
+
+def spread_columns(place, own, one, two, steps):
+    rows, width = own.shape
+    vmem = pl.BlockSpec(memory_space=pltpu.VMEM)
+    return pl.pallas_call(
+        spread_kernel,
+        in_specs=[pl.BlockSpec(memory_space=pltpu.SMEM)] + [vmem] * 3,
+        out_specs=vmem,
+        out_shape=jax.ShapeDtypeStruct((steps, 2, rows // (2 * steps), width), jnp.bfloat16),
+        cost_estimate=SHORT,
+        name="spread_columns",
+    )(place, own, one, two)
+
+
+def unpack_kernel(heads, place_ref, gain_ref, query_ref, key_ref, value_ref, other_ref, *refs):
+    steps = other_ref.shape[0]
+    near, out_refs, cols_s = refs[:steps], refs[steps:-1], refs[-1]
+    seqs = 2 * steps
+    z, core = place_ref[0] // 2, place_ref[0] % 2
+    for step in range(steps):
+        cols_s[0, step] = near[step][0]
+    cols_s[1] = other_ref[...]
+    total = jnp.zeros((gain_ref.shape[0], 1), jnp.float32)
+    for m, ref in enumerate((query_ref, key_ref, value_ref)):
+        rows = jnp.concatenate(
+            [
+                cols_s[
+                    (core + head) % 2,
+                    (z + steps - head % seqs // 2) % steps,
+                    :,
+                    (head // seqs * 3 + m) * HEAD_DIM : (head // seqs * 3 + m + 1) * HEAD_DIM,
+                ]
+                for head in range(heads)
+            ],
+            axis=1,
+        ).astype(jnp.float32)
+        total += jnp.sum(rows * ref[...].astype(jnp.float32), axis=1, keepdims=True)
+        out_refs[m][...] = rows * gain_ref[...]
+    out_refs[3][...] = total
+
+
+def unpack_columns(place, gain_col, weights, near, other):
+    rows, width = weights[0].shape
+    vmem = pl.BlockSpec(memory_space=pltpu.VMEM)
+    return pl.pallas_call(
+        functools.partial(unpack_kernel, width // HEAD_DIM),
+        in_specs=[pl.BlockSpec(memory_space=pltpu.SMEM)] + [vmem] * (5 + len(near)),
+        out_specs=[vmem] * 4,
+        out_shape=[jax.ShapeDtypeStruct((rows, width), jnp.float32)] * 3
+        + [jax.ShapeDtypeStruct((rows, 1), jnp.float32)],
+        scratch_shapes=[pltpu.VMEM((2,) + other.shape, other.dtype)],
+        cost_estimate=SHORT,
+        name="unpack_columns",
+    )(place, gain_col, *weights, other, *near)
+
+
+def unit_kernel(*refs):
+    out_ref = refs[-1]
+    tok = refs[0].shape[0]
+    for slot, ref in enumerate(refs[:-1]):
+        rows = ref[...].astype(jnp.float32)
+        scale = lax.rsqrt(jnp.mean(rows * rows, axis=-1, keepdims=True) + NORM_EPS)
+        out_ref[slot * tok : (slot + 1) * tok] = (rows * scale).astype(jnp.bfloat16)
+
+
+def unit_tokens(slots):
+    tok, width = slots[0].shape
+    return pl.pallas_call(
+        unit_kernel,
+        out_shape=jax.ShapeDtypeStruct((len(slots) * tok, width), jnp.bfloat16),
+        compiler_params=pltpu.CompilerParams(vmem_limit_bytes=16 * 2**20),
+        cost_estimate=SHORT,
+        name="unit_tokens",
+    )(*slots)
+
+
+def join_kernel(*refs):
+    rows = refs[0].shape[0]
+    for i, ref in enumerate(refs[:-1]):
+        refs[-1][i * rows : (i + 1) * rows] = ref[...]
+
+
+def join_rows(arrays):
+    rows, width = arrays[0].shape
+    vmem = pl.BlockSpec(memory_space=pltpu.VMEM)
+    return pl.pallas_call(
+        join_kernel,
+        in_specs=[vmem] * len(arrays),
+        out_specs=vmem,
+        out_shape=jax.ShapeDtypeStruct((len(arrays) * rows, width), arrays[0].dtype),
+        cost_estimate=SHORT,
+        name="join_rows",
+    )(*arrays)
+
+
+def load_kernel(layout, *refs):
+    pieces, out_ref, sem = refs[:-2], refs[-2], refs[-1]
+    copies = [
+        pltpu.make_async_copy(ref, out_ref.at[m, pl.ds(row, ref.shape[0])], sem.at[i])
+        for i, (ref, (m, row)) in enumerate(zip(pieces, layout, strict=True))
+    ]
+    for copy in copies:
+        copy.start()
+    for copy in copies:
+        copy.wait()
+
+
+def load_weights(matrices):
+    layout, pieces = [], []
+    for m, matrix in enumerate(matrices):
+        row = 0
+        for piece in matrix:
+            layout.append((m, row))
+            pieces.append(piece)
+            row += piece.shape[0]
+    shape = (len(matrices), row, pieces[0].shape[1])
+    return pl.pallas_call(
+        functools.partial(load_kernel, tuple(layout)),
+        in_specs=[pl.BlockSpec(memory_space=pl.ANY)] * len(pieces),
+        out_specs=pl.BlockSpec(memory_space=pltpu.VMEM),
+        out_shape=pltpu.VMEM(shape, pieces[0].dtype),
+        scratch_shapes=[pltpu.SemaphoreType.DMA((len(pieces),))],
+        cost_estimate=SHORT,
+        compiler_params=pltpu.CompilerParams(vmem_limit_bytes=14 * 2**20),
+        name="load_weights",
+    )(*in_hbm(pieces))
+
+
+def feed_kernel(call, aliased, *refs):
+    shard_ref, tokens, grads, first_ref, down_ref = refs[0], refs[1:3], refs[3:5], refs[5], refs[6]
+    refs = refs[7 + aliased :]
+    part_near, part_other = refs[:2]
+    all_refs = refs[2:9]
+    tok_s, grad_s, hidden_s, gate_s, up_s, hidden_t, gate_t, up_t, down_s, sem = refs[9:]
+    tok, width = tokens[0].shape
+    shards, block = 4, down_ref.shape[1] // 4
+    rows = pl.ds(2 * tok * call, 2 * tok)
+    for c in range(2):
+        tok_s[c * tok : (c + 1) * tok] = tokens[c][...]
+        grad_s[c * tok : (c + 1) * tok] = grads[c][...]
+    copies = [
+        pltpu.make_async_copy(tok_s, all_refs[0].at[rows], sem.at[0]),
+        pltpu.make_async_copy(grad_s, all_refs[1].at[rows], sem.at[1]),
+    ]
+    for copy in copies:
+        copy.start()
+    for b in range(shards):
+        at = slice(b * block, (b + 1) * block)
+        place = pl.ds(pl.multiple_of((shard_ref[0] ^ b) * block, block), block)
+        gate_val = times_trans(tok_s[...], first_ref[0, at])
+        up_val = times_trans(tok_s[...], first_ref[1, at])
+        hidden_grad = times_trans(grad_s[...], down_ref[0, at])
+        sigmoid_val = 1.0 / (1.0 + jnp.exp(-gate_val))
+        silu_val = gate_val * sigmoid_val
+        hidden = (silu_val * up_val).astype(jnp.bfloat16)
+        gate_grad = (
+            hidden_grad * up_val * (sigmoid_val + silu_val * (1.0 - sigmoid_val))
+        ).astype(jnp.bfloat16)
+        up_grad = (hidden_grad * silu_val).astype(jnp.bfloat16)
+        for value, by_unit, by_token in (
+            (hidden, hidden_t, hidden_s), (gate_grad, gate_t, gate_s), (up_grad, up_t, up_s)
+        ):
+            by_unit[place, :] = value.T
+            by_token[:, at] = value
+    late = [
+        pltpu.make_async_copy(src, dst.at[:, rows], sem.at[2 + i])
+        for i, (src, dst) in enumerate(zip((hidden_t, gate_t, up_t), all_refs[2:5], strict=True))
+    ]
+    for copy in late:
+        copy.start()
+    for c in range(4):
+        at = slice(c * (width // 4), (c + 1) * (width // 4))
+        part = dot_nn(gate_s[...], first_ref[0, :, at]) + dot_nn(up_s[...], first_ref[1, :, at])
+        part_near[:, at] = part[:tok]
+        part_other[:, at] = part[tok:].astype(jnp.bfloat16)
+    for c in range(4):
+        at = slice(c * (width // 4), (c + 1) * (width // 4))
+        down = dot_nn(hidden_s[...], down_ref[0, :, at]).astype(jnp.bfloat16)
+        down_s[0, :, at] = down[:tok]
+        down_s[1, :, at] = down[tok:]
+    last = [
+        pltpu.make_async_copy(down_s.at[c], all_refs[5 + c].at[call], sem.at[5 + c])
+        for c in range(2)
+    ]
+    for copy in last:
+        copy.start()
+    for copy in copies + late + last:
+        copy.wait()
+
+
+def feed_blocks(call, slots, shard, tokens, grads, first_two, down, whole):
+    tok, width = tokens[0].shape
+    units = down.shape[1]
+    anywhere = pl.BlockSpec(memory_space=pl.ANY)
+    vmem = pl.BlockSpec(memory_space=pltpu.VMEM)
+    low, full = jnp.bfloat16, jnp.float32
+    shapes = (
+        [(slots * tok, width)] * 2
+        + [(units, slots * tok)] * 3
+        + [(slots // 2, tok, width)] * 2
+    )
+    whole = in_hbm(whole or [])
+    out = pl.pallas_call(
+        functools.partial(feed_kernel, call, len(whole)),
+        in_specs=[pl.BlockSpec(memory_space=pltpu.SMEM)] + [vmem] * 6 + [anywhere] * len(whole),
+        out_specs=[vmem] * 2 + [anywhere] * 7,
+        out_shape=[jax.ShapeDtypeStruct((tok, width), full), jax.ShapeDtypeStruct((tok, width), low)]
+        + [pltpu.HBM(shape, low) for shape in shapes],
+        input_output_aliases={7 + i: 2 + i for i in range(len(whole))},
+        scratch_shapes=[pltpu.VMEM((2 * tok, width), low)] * 2
+        + [pltpu.VMEM((2 * tok, units), low)] * 3
+        + [pltpu.VMEM((units, 2 * tok), low)] * 3
+        + [pltpu.VMEM((2, tok, width), low), pltpu.SemaphoreType.DMA((7,))],
+        compiler_params=pltpu.CompilerParams(vmem_limit_bytes=30 * 2**20),
+        cost_estimate=SHORT,
+        name="feed_blocks",
+    )(
+        shard,
+        *tokens,
+        *grads,
+        *[pltpu.with_memory_space_constraint(weight, pltpu.VMEM) for weight in (first_two, down)],
+        *whole,
+    )
+    return out[:2], out[2:]
+
+
+def start_pieces(pieces, weight_s, sem):
+    places, row = [], 0
+    for i, ref in enumerate(pieces):
+        at = pl.ds(row, ref.shape[0])
+        copy = pltpu.make_async_copy(ref, weight_s.at[at], sem.at[i])
+        copy.start()
+        places.append((row, ref.shape[0], copy))
+        row += ref.shape[0]
+    return places
+
+
+def project_kernel(index_ref, blocks_ref, input_ref, gain_ref, *refs):
+    pieces, (middle_ref, normed_ref, scale_ref, weight_s, sem) = refs[:-5], refs[-5:]
+    places = start_pieces(pieces, weight_s, sem)
+    heads = blocks_ref.shape[0]
+    rows = jnp.concatenate([blocks_ref[index_ref[i], :HEAD_DIM] for i in range(heads)]).T
+    total = input_ref[...].astype(jnp.float32)
+    for row, size, copy in places:
+        copy.wait()
+        total += dot_nn(rows[:, row : row + size], weight_s[row : row + size])
+    scale = lax.rsqrt(jnp.mean(total * total, axis=-1, keepdims=True) + NORM_EPS)
+    middle_ref[...] = total
+    normed_ref[...] = (total * scale * gain_ref[...]).astype(jnp.bfloat16)
+    scale_ref[...] = jnp.broadcast_to(scale, scale_ref.shape)
+
+
+def project(index, blocks, inputs, gain, pieces):
+    tok, width = inputs.shape
+    vmem = pl.BlockSpec(memory_space=pltpu.VMEM)
+    return pl.pallas_call(
+        project_kernel,
+        in_specs=[pl.BlockSpec(memory_space=pltpu.SMEM)]
+        + [vmem] * 3
+        + [pl.BlockSpec(memory_space=pl.ANY)] * len(pieces),
+        out_specs=[vmem] * 3,
+        out_shape=[
+            jax.ShapeDtypeStruct((tok, width), jnp.float32),
+            jax.ShapeDtypeStruct((tok, width), jnp.bfloat16),
+            jax.ShapeDtypeStruct((tok, 128), jnp.float32),
+        ],
+        scratch_shapes=[
+            pltpu.VMEM((HEADS * HEAD_DIM, width), jnp.bfloat16),
+            pltpu.SemaphoreType.DMA((len(pieces),)),
+        ],
+        compiler_params=pltpu.CompilerParams(vmem_limit_bytes=18 * 2**20),
+        cost_estimate=SHORT,
+        name="project",
+    )(index, blocks, inputs, gain, *in_hbm(pieces))
+
+
+def token_grad_kernel(
+    index_ref, own_ref, one_ref, two_ref, three_ref, middle_ref, scale_ref, gain_ref, grad_ref, *refs
+):
+    pieces, (middle_grad_ref, low_ref, out_ref, weight_s, sem) = refs[:-5], refs[-5:]
+    places = start_pieces(pieces, weight_s, sem)
+    normed_grad = own_ref[...]
+    for ref in (one_ref, two_ref, three_ref):
+        normed_grad += ref[...].astype(jnp.float32)
+    tok = normed_grad.shape[0]
+    scale = scale_ref[:, :1]
+    unit = middle_ref[...] * scale
+    gain_part = jnp.sum(normed_grad * unit, axis=0, keepdims=True)
+    unit_grad = normed_grad * gain_ref[...]
+    middle_grad = grad_ref[...].astype(jnp.float32) + scale * (
+        unit_grad - unit * jnp.mean(unit_grad * unit, axis=-1, keepdims=True)
+    )
+    middle_grad_ref[...] = middle_grad
+    low = middle_grad.astype(jnp.bfloat16)
+    low_ref[...] = low
+    grad_t = low.T
+    for row, size, copy in places:
+        copy.wait()
+        out = dot_nn(weight_s[row : row + size], grad_t).astype(jnp.bfloat16)
+        for i in range(size // HEAD_DIM):
+            out_ref[index_ref[row // HEAD_DIM + i], :HEAD_DIM] = out[
+                i * HEAD_DIM : (i + 1) * HEAD_DIM
+            ]
+    coarse = gain_part.astype(jnp.bfloat16)
+    fine = (gain_part - coarse.astype(jnp.float32)).astype(jnp.bfloat16)
+    wide = gain_part.shape[1] // out_ref.shape[0]
+    for head in range(out_ref.shape[0]):
+        at = slice(head * wide, (head + 1) * wide)
+        row = jnp.concatenate([coarse[:, at], fine[:, at]], axis=1)
+        out_ref[head, HEAD_DIM:] = jnp.broadcast_to(row, (EXTRA, tok))
+
+
+def token_grad(index, sums, middle, scale, gain, output_grad, pieces):
+    tok, width = middle.shape
+    vmem = pl.BlockSpec(memory_space=pltpu.VMEM)
+    return pl.pallas_call(
+        token_grad_kernel,
+        in_specs=[pl.BlockSpec(memory_space=pltpu.SMEM)]
+        + [vmem] * 8
+        + [pl.BlockSpec(memory_space=pl.ANY)] * len(pieces),
+        out_specs=[vmem] * 3,
+        out_shape=[
+            jax.ShapeDtypeStruct((tok, width), jnp.float32),
+            jax.ShapeDtypeStruct((tok, width), jnp.bfloat16),
+            pltpu.HBM((HEADS, HEAD_DIM + EXTRA, tok), jnp.bfloat16),
+        ],
+        scratch_shapes=[
+            pltpu.VMEM((HEADS * HEAD_DIM, width), jnp.bfloat16),
+            pltpu.SemaphoreType.DMA((len(pieces),)),
+        ],
+        compiler_params=pltpu.CompilerParams(vmem_limit_bytes=18 * 2**20),
+        cost_estimate=SHORT,
+        name="token_grad",
+    )(index, *sums, middle, scale, gain, output_grad, *in_hbm(pieces))
+
+
+def feed_wgrad_kernel(gate_ref, up_ref, hidden_ref, tokens_ref, grads_ref, out_ref):
+    tokens, grads = tokens_ref[...], grads_ref[...]
+    out_ref[0, 0] = dot_nn(gate_ref[...], tokens).astype(jnp.bfloat16)
+    out_ref[0, 1] = dot_nn(up_ref[...], tokens).astype(jnp.bfloat16)
+    out_ref[0, 2] = dot_nn(hidden_ref[...], grads).astype(jnp.bfloat16)
+
+
+def feed_wgrads(shards, gate_grad, up_grad, hidden, feed_low, span_grad):
+    units, tokens = hidden.shape
+    width = feed_low.shape[1]
+    block = units // shards
+    half = width // 2
+    rows = pl.BlockSpec((block, tokens), lambda c, i: (i, 0))
+    every = pl.BlockSpec((tokens, half), lambda c, i: (0, c))
+    return pl.pallas_call(
+        feed_wgrad_kernel,
+        grid=(2, shards),
+        in_specs=[rows] * 3 + [every] * 2,
+        out_specs=pl.BlockSpec((1, 3, block, half), lambda c, i: (i, 0, 0, c)),
+        out_shape=jax.ShapeDtypeStruct((shards, 3, block, width), jnp.bfloat16),
+        compiler_params=pltpu.CompilerParams(vmem_limit_bytes=24 * 2**20),
+        cost_estimate=SHORT,
+        name="feed_wgrads",
+    )(*in_hbm([gate_grad, up_grad, hidden, feed_low, span_grad]))
+
+
+def output_wgrad_kernel(blocks, *refs):
+    heads, grads, out_ref = refs[:4], refs[4 : 4 + blocks], refs[-1]
+    tok = grads[0].shape[0]
+    grad_rows = jnp.concatenate([ref[...] for ref in grads])
+    for k in range(4):
+        out_ref[k] = dot_nn(heads[k][...], grad_rows).astype(jnp.bfloat16)
+
+
+def output_wgrad_parts(heads, grads):
+    tok, width = grads[0].shape
+    return pl.pallas_call(
+        functools.partial(output_wgrad_kernel, len(grads)),
+        out_shape=jax.ShapeDtypeStruct((4, HEAD_DIM, width), jnp.bfloat16),
+        compiler_params=pltpu.CompilerParams(vmem_limit_bytes=14 * 2**20),
+        cost_estimate=SHORT,
+        name="output_wgrad",
+    )(*heads, *grads)
 
 
 def swap_cores(values):
@@ -557,77 +1021,44 @@
     return lax.ppermute(values, "shard", [(i, i ^ flip) for i in range(4)])
 
 
-def gather_seq(values):
-    half = lax.axis_size("seq") // 2
-    same = [values] + [from_chip(values, step) for step in range(1, half)]
+def both_cores(same):
     return [block for one in same for block in (one, swap_cores(one))]
 
 
-def scatter_seq(parts):
-    half = lax.axis_size("seq") // 2
-    total = None
-    for step in range(half):
-        pair = parts[2 * step].astype(F32) + swap_cores(parts[2 * step + 1].astype(BF16)).astype(F32)
-        if step:
-            pair = from_chip(pair.astype(BF16), -step).astype(F32)
-        total = pair if total is None else total + pair
-    return total
-
-
-def gather_shard(block):
-    rows = block.shape[0] // 2
-    one, two = from_shard(block, 1), from_shard(block, 2)
-    far = [from_shard(one[:rows], 2), from_shard(two[rows:], 1)]
-    return [block, one, two, jnp.concatenate(far)]
-
-
-def scatter_shard(parts):
+def core_sum(near, other):
+    return near.astype(F32) + swap_cores(other.astype(BF16)).astype(F32)
+
+
+def after(token, values):
+    return lax.optimization_barrier((values, token))[0]
+
+
+def join(token, *values):
+    return lax.optimization_barrier((token,) + values)[0]
+
+
+def first_hops(block):
+    return [from_shard(block, 1), from_shard(block, 2)]
+
+
+def second_hops(first):
+    rows = first[0].shape[0] // 2
+    return [from_shard(first[0][:rows], 2), from_shard(first[1][rows:], 1)]
+
+
+def scatter_shard_first(parts):
     rows = parts[3].shape[0] // 2
     low = parts[3].astype(BF16)
-    top, bottom = from_shard(low[:rows], 1), from_shard(low[rows:], 2)
-    one = jnp.concatenate([parts[1][:rows], parts[1][rows:] + bottom.astype(F32)])
-    two = jnp.concatenate([parts[2][:rows] + top.astype(F32), parts[2][rows:]])
-    return (
-        parts[0]
-        + from_shard(one.astype(BF16), 1).astype(F32)
-        + from_shard(two.astype(BF16), 2).astype(F32)
-    )
-
-
-def to_natural_shards(slots):
-    own = lax.axis_index("shard")
-    stacked = jnp.stack(slots)
-    return jnp.concatenate(
-        [lax.dynamic_index_in_dim(stacked, own ^ k, 0, keepdims=False) for k in range(4)]
-    )
-
-
-def bits_of(flat):
-    seq_bits = [("seq", 1 << b) for b in range(lax.axis_size("seq").bit_length() - 1)]
-    return seq_bits + [("shard", 1), ("shard", 2)]
-
-
-def gather_small(row):
-    rows = row
-    for axis, flip in bits_of(row):
-        count = lax.axis_size(axis)
-        other = lax.ppermute(rows, axis, [(i, i ^ flip) for i in range(count)])
-        upper = (lax.axis_index(axis) & flip) != 0
-        rows = jnp.concatenate(
-            [jnp.where(upper, other, rows), jnp.where(upper, rows, other)], axis=0
-        )
-    return rows
-
-
-def scatter_small(rows):
-    for axis, flip in reversed(bits_of(rows)):
-        count = lax.axis_size(axis)
-        upper = (lax.axis_index(axis) & flip) != 0
-        half = rows.shape[0] // 2
-        keep = jnp.where(upper, rows[half:], rows[:half])
-        give = jnp.where(upper, rows[:half], rows[half:])
-        rows = keep + lax.ppermute(give, axis, [(i, i ^ flip) for i in range(count)])
-    return rows
+    return from_shard(low[:rows], 1), from_shard(low[rows:], 2)
+
+
+def scatter_shard_last(parts, first):
+    rows = parts[3].shape[0] // 2
+    top, bottom = first
+    one, two = parts[1].astype(F32), parts[2].astype(F32)
+    one = jnp.concatenate([one[:rows], one[rows:] + bottom.astype(F32)])
+    two = jnp.concatenate([two[:rows] + top.astype(F32), two[rows:]])
+    return from_shard(one.astype(BF16), 1), from_shard(two.astype(BF16), 2)
 
 
 def rotate_rows(front, back, cos_t, sin_t):
@@ -666,26 +1097,42 @@
     cos_own = lax.dynamic_index_in_dim(cos_all, shard, 0, keepdims=False)
     sin_own = lax.dynamic_index_in_dim(sin_all, shard, 0, keepdims=False)
 
-    inputs_slots = gather_seq(layer_input)
+    steps = seqs // 2
+    z, core = seq // 2, seq % 2
+    shard_at = jnp.reshape(shard, (1,)).astype(jnp.int32)
     gain_col = norm_gain.astype(F32)[:, None]
     heads_here = HEADS // seqs
     own_rows = query_weight.shape[0]
-    packed = jnp.stack(
-        [
-            (weight.astype(F32) * gain_col).astype(BF16).reshape(own_rows, shards, seqs, HEAD_DIM)
-            for weight in (query_weight, key_weight, value_weight)
-        ],
-        axis=2,
-    )
-    packed = jnp.transpose(packed, (3, 0, 1, 2, 4)).reshape(seqs, own_rows, heads_here * 3 * HEAD_DIM)
-    columns = lax.all_to_all(packed, "seq", split_axis=0, concat_axis=0, tiled=True)
-    columns = to_natural_shards(
-        gather_shard(columns.reshape(seqs * own_rows, heads_here * 3 * HEAD_DIM))
-    )
-
-    span_inputs = jnp.concatenate(inputs_slots).astype(F32)
-    scale_span = lax.rsqrt(jnp.mean(span_inputs * span_inputs, axis=-1, keepdims=True) + NORM_EPS)
-    unit_low = (span_inputs * scale_span).astype(BF16)
+    attn_weights = (query_weight, key_weight, value_weight)
+    slot = jnp.arange(HEADS, dtype=jnp.int32)
+
+    packed = pack_columns(place, gain_col, attn_weights, seqs)
+    point = join(jnp.zeros((), F32), packed)
+    from_other = swap_cores(packed[1])
+    gate_first = first_hops(after(point, gate_weight))
+    col_blocks = []
+    for step in range(steps):
+        block = jnp.concatenate([packed[0, step], from_other[step]])
+        col_blocks.append(from_chip(block, -step) if step else block)
+    point = join(point, gate_first, col_blocks)
+    col_block = jnp.concatenate(after(point, col_blocks))
+    col_first = first_hops(col_block)
+    own_input = after(point, layer_input)
+    input_one, input_three = from_chip(own_input, 1), from_chip(own_input, -1)
+    point = join(point, col_first, input_one, input_three)
+    col_far = second_hops(after(point, col_first))
+    input_two = from_chip(after(point, input_one), 1)
+    input_slots = both_cores([own_input, after(point, input_one)])
+    input_last = both_cores([after(point, input_three)])
+    point = join(point, col_far, input_two, input_slots, input_last)
+    input_slots += both_cores([after(point, input_two)]) + input_last
+    rel_blocks = (
+        (shard ^ (slot // seqs)) * seqs
+        + (z + steps - slot % seqs // 2) % steps * 2
+        + (core ^ (slot % 2))
+    ).astype(jnp.int32)
+    columns = order_blocks([col_block] + col_first + after(point, col_far), rel_blocks, own_rows)
+    unit_low = unit_tokens(input_slots)
     qkv = lax.dot_general(
         columns, unit_low, (((0,), (1,)), ((), ())), preferred_element_type=F32
     ).reshape(shards, 3, HEAD_DIM, span)
@@ -693,123 +1140,203 @@
         qkv[:, :2, :half_head], qkv[:, :2, half_head:], cos_own[None, None], sin_own[None, None]
     )
     qkv_low = jnp.concatenate([turned, qkv[:, 2:]], axis=1).astype(BF16)
+    qkv_low = qkv_low.reshape(shards, 3 * HEAD_DIM, span)
+    gate_far = second_hops(after(point, gate_first))
+    output_own = after(point, output_weight)
+    output_one, output_three = from_chip(output_own, 1), from_chip(output_own, -1)
+    up_top, up_bottom = up_weight[: up_weight.shape[0] // 2], up_weight[up_weight.shape[0] // 2 :]
+    up_first = [from_shard(after(point, up_top), flip) for flip in (1, 2)]
+    point = join(point, qkv_low, gate_far, output_one, output_three, up_first)
+
     head_qkv = lax.all_to_all(
-        qkv_low.reshape(shards, 3 * HEAD_DIM, span), "shard", split_axis=0, concat_axis=0, tiled=True
-    )
-
-    head_out, out_blocks, lse = attend(head_qkv, tok, place, bounds)
-    token_out = lax.all_to_all(
-        out_blocks, ("shard", "seq"), split_axis=0, concat_axis=0, tiled=True
-    ).reshape(width, tok)
-
-    output_full = lax.all_gather(output_weight, ("shard", "seq"), axis=0, tiled=True)
-    gain_two = gather_small(feed_gain.astype(F32)[None, :]).reshape(1, width)
-    grad_slots = gather_seq(output_grad)
-    span_grad = jnp.concatenate(grad_slots)
-    gate_here = jnp.concatenate(gather_shard(gate_weight))
-    up_here = jnp.concatenate(gather_shard(up_weight))
-    down_here = jnp.concatenate(gather_shard(down_weight))
-
+        after(point, qkv_low), "shard", split_axis=0, concat_axis=0, tiled=True
+    )
+    output_two = from_chip(after(point, output_one), 1)
+    own_grad = after(point, output_grad)
+    grad_one = from_chip(own_grad, 1)
+    up_first += [from_shard(after(point, up_bottom), flip) for flip in (1, 2)]
+    point = join(point, head_qkv, output_two, grad_one, up_first)
+    output_own = jnp.concatenate(after(point, [output_own, output_one, output_two, output_three]))
+    output_first = first_hops(output_own)
+    output_swapped = [swap_cores(output_own)]
+    grad_two, grad_three = from_chip(after(point, grad_one), 1), from_chip(own_grad, -1)
+    gain_rows = jnp.pad(feed_gain[None, :], ((0, EXTRA - 1), (0, tok - own_rows)))
+    head_out, head_low, out_blocks, lse = attend(
+        after(point, head_qkv), gain_rows, tok, place, bounds
+    )
+    point = join(point, out_blocks, output_first, output_swapped, grad_two, grad_three)
+    token_blocks = lax.all_to_all(
+        after(point, out_blocks), ("shard", "seq"), split_axis=0, concat_axis=0, tiled=True
+    )
+    output_far = second_hops(after(point, output_first))
+    up_far = [from_shard(after(point, up_first[0]), 2), from_shard(after(point, up_first[3]), 1)]
+    output_swapped += [swap_cores(piece) for piece in after(point, output_first)]
+    point = join(point, token_blocks, output_far, up_far, output_swapped)
+    gain_two = token_blocks[:, HEAD_DIM, :own_rows].astype(F32).reshape(1, width)
+    output_swapped += [swap_cores(piece) for piece in after(point, output_far)]
+    output_pieces = [output_own] + output_first + output_far + output_swapped
+    rel_heads = (
+        (shard ^ (slot // steps % shards)) * seqs
+        + (z + slot % steps) % steps * 2
+        + (core ^ (slot // (HEADS // 2)))
+    ).astype(jnp.int32)
+    middle, normed_two, scale_two = project(
+        rel_heads, after(point, token_blocks), layer_input, gain_two, output_pieces
+    )
+    point = join(point, normed_two)
+
+    own_tokens = after(point, normed_two)
+    tokens_one, tokens_three = from_chip(own_tokens, 1), from_chip(own_tokens, -1)
+    down_first = first_hops(after(point, down_weight))
+    grad_slots = both_cores(after(point, [output_grad, grad_one, grad_two, grad_three]))
+    first_two = load_weights(
+        [
+            after(point, [gate_weight, *gate_first, *gate_far]),
+            [up_weight, up_first[0], up_first[2], up_first[1], up_first[3], *up_far],
+        ]
+    )
+    point = join(point, tokens_one, tokens_three, down_first, grad_slots, first_two)
+    tokens_two = from_chip(after(point, tokens_one), 1)
+    down_far = second_hops(after(point, down_first))
+    feed_slots = both_cores([own_tokens, after(point, tokens_one)])
+    feed_last = both_cores([after(point, tokens_three)])
+    point = join(point, tokens_two, down_far, feed_slots, feed_last)
+    feed_slots += both_cores([after(point, tokens_two)]) + feed_last
+    down_here = load_weights([[down_weight, *down_first, *after(point, down_far)]])
+    order = (2, 1, 3, 0)
+
+    def feed(step, tokens, whole):
+        here = slice(2 * step, 2 * step + 2)
+        return feed_blocks(
+            order.index(step), seqs, shard_at, tokens, grad_slots[here], first_two, down_here, whole
+        )
+
+    parts_two, whole = feed(2, feed_slots[4:6], None)
+    sum_two = core_sum(*parts_two).astype(BF16)
+    point = join(point, sum_two)
+    arrived_two = from_chip(after(point, sum_two), -2)
+    parts_one, whole = feed(1, after(point, feed_slots[2:4]), whole)
+    parts_three, whole = feed(3, feed_slots[6:8], whole)
+    point = join(point, arrived_two, parts_one, parts_three)
+    sum_one = core_sum(*after(point, parts_one)).astype(BF16)
+    sum_three = core_sum(*after(point, parts_three)).astype(BF16)
+    point = join(point, sum_one, sum_three)
+    arrived_one = from_chip(after(point, sum_one), -1)
+    arrived_three = from_chip(after(point, sum_three), 1)
+    parts_own, whole = feed(0, after(point, feed_slots[0:2]), whole)
+    feed_low, span_grad, hidden, gate_grad, up_grad, down_near, down_other = whole
+    feed_wparts = feed_wgrads(shards, gate_grad, up_grad, hidden, feed_low, span_grad)
+    head_slots = [
+        lax.dynamic_index_in_dim(after(point, head_low), shard ^ k, 0, keepdims=False)
+        for k in range(4)
+    ]
+    head_slots = head_slots[:1] + [from_shard(head_slots[k], k) for k in range(1, 4)]
+    point = join(point, parts_own, feed_wparts, arrived_one, arrived_three, head_slots)
+    sum_own = core_sum(*after(point, parts_own))
+    middle_grad, attend_grad, head_grad = token_grad(
+        rel_heads,
+        [sum_own, arrived_one, arrived_two, arrived_three],
+        middle,
+        scale_two,
+        gain_two,
+        output_grad,
+        output_pieces,
+    )
+    point = join(point, head_grad)
+
+    out_grad_blocks = lax.all_to_all(
+        after(point, head_grad), ("shard", "seq"), split_axis=0, concat_axis=0, tiled=True
+    )
+    feed_wsum = lax.psum_scatter(
+        after(point, feed_wparts).reshape(-1, width), "shard", scatter_dimension=0, tiled=True
+    ).reshape(3, -1, width)
+    own_agrad = after(point, attend_grad)
+    agrad_one = from_chip(own_agrad, 1)
+    down_all = core_sum(after(point, down_near), down_other).astype(BF16)
+    down_sums = [down_all[order.index(step)] for step in range(steps)]
+    point = join(point, out_grad_blocks, agrad_one, down_sums)
+    agrad_three = from_chip(after(point, own_agrad), -1)
+    down_two = from_chip(after(point, down_sums[2]), -1)
+    down_three = from_chip(after(point, down_sums[3]), 1)
+    back = attend_back(
+        head_qkv, lse, head_out, after(point, out_grad_blocks), cos_all, sin_all, tok, place, bounds
+    )
+    point = join(point, back, agrad_three, down_two, down_three)
+    span_back = lax.all_to_all(
+        after(point, back), "shard", split_axis=0, concat_axis=0, tiled=True
+    ).reshape(heads_here * 3 * HEAD_DIM, span)
+    agrad_two = from_chip(after(point, agrad_one), 1)
+    down_one = from_chip(
+        (down_sums[1].astype(F32) + after(point, down_two).astype(F32)).astype(BF16), -1
+    )
+    agrad_slots = both_cores([after(point, own_agrad), agrad_one, agrad_two, agrad_three])
+    out_part = output_wgrad_parts(head_slots, agrad_slots)
+    point = join(point, span_back, down_one, out_part)
+    layer_output = (
+        middle
+        + down_sums[0].astype(F32)
+        + after(point, down_one).astype(F32)
+        + down_three.astype(F32)
+    ).astype(BF16)
+
+    span_back = after(point, span_back)
+    cols_part = lax.dot_general(
+        unit_low, span_back, (((0,), (1,)), ((), ())), preferred_element_type=F32
+    ).reshape(shards, seqs * own_rows, heads_here * 3 * HEAD_DIM)
+    cols_parts = [
+        lax.dynamic_index_in_dim(cols_part, shard ^ k, 0, keepdims=False) for k in range(4)
+    ]
+    cols_first = scatter_shard_first(cols_parts)
+    unit_sums = []
+    for step in range(steps):
+        lanes_here = after(cols_part, span_back)[:, 2 * step * tok : 2 * (step + 1) * tok]
+        part = lax.dot_general(
+            lanes_here, columns, (((0,), (1,)), ((), ())), preferred_element_type=F32
+        )
+        unit_sums.append(core_sum(part[:tok], part[tok:]))
+    point = join(point, cols_first, unit_sums, layer_output)
+    unit_two = from_chip(after(point, unit_sums[2]).astype(BF16), -1)
+    unit_three = from_chip(after(point, unit_sums[3]).astype(BF16), 1)
+    cols_last = scatter_shard_last(cols_parts, after(point, cols_first))
+    point = join(point, unit_two, unit_three, cols_last)
+    unit_one = from_chip((unit_sums[1] + after(point, unit_two).astype(F32)).astype(BF16), -1)
+    out_parts = [after(point, out_part)[k] for k in range(4)]
+    out_first = scatter_shard_first(out_parts)
+    cols_spread = spread_columns(place, cols_parts[0], *after(point, cols_last), steps)
+    point = join(point, unit_one, cols_spread, out_first)
+    cols_same = [cols_spread[0]] + [
+        from_chip(after(point, cols_spread)[step], -step) for step in range(1, steps)
+    ]
+    out_last = scatter_shard_last(out_parts, after(point, out_first))
+    unit_grad = unit_sums[0] + after(point, unit_one).astype(F32) + unit_three.astype(F32)
     inputs = layer_input.astype(F32)
-    middle = inputs + trans_times(token_out, output_full)
-    normed_two, scale_two = normalize(middle, gain_two)
-    feed_low = jnp.concatenate(gather_seq(normed_two.astype(BF16)))
-
-    gate_val = times_trans(feed_low, gate_here)
-    up_val = times_trans(feed_low, up_here)
-    hidden_grad = times_trans(span_grad, down_here)
-    sigmoid_val = jax.nn.sigmoid(gate_val)
-    hidden = (gate_val * sigmoid_val * up_val).astype(BF16)
-    gate_grad = (
-        hidden_grad * up_val * (sigmoid_val * (1.0 + gate_val * (1.0 - sigmoid_val)))
-    ).astype(BF16)
-    up_grad = (hidden_grad * (gate_val * sigmoid_val)).astype(BF16)
-    feed_part = dot_nn(gate_grad, gate_here) + dot_nn(up_grad, up_here)
-    feed_grad = scatter_seq(feed_part.reshape(seqs, tok, width))
-
-    middle_norm_grad, gain_two_part = norm_back(feed_grad, middle, scale_two, gain_two)
-    middle_grad = output_grad.astype(F32) + middle_norm_grad
-    attend_grad = middle_grad.astype(BF16)
-    token_out_grad = times_trans(output_full, attend_grad).astype(BF16)
-    out_grad_blocks = lax.all_to_all(
-        token_out_grad.reshape(HEADS, HEAD_DIM, tok),
-        ("shard", "seq"),
-        split_axis=0,
-        concat_axis=0,
-        tiled=True,
-    )
-    query_grad, key_grad, value_grad = attend_back(
-        head_qkv, lse, head_out, out_grad_blocks, tok, place, bounds
-    )
-
-    def by_span(grad):
-        return jnp.transpose(grad.reshape(HEAD_DIM, shards, span), (1, 0, 2))
-
-    def turn_back(grad):
-        rows = by_span(grad)
-        return rotate_rows(rows[:, :half_head], rows[:, half_head:], cos_all, -sin_all)
-
-    back = jnp.concatenate(
-        [turn_back(query_grad), turn_back(key_grad), by_span(value_grad)], axis=1
-    ).astype(BF16)
-    span_back = lax.all_to_all(back, "shard", split_axis=0, concat_axis=0, tiled=True).reshape(
-        heads_here * 3 * HEAD_DIM, span
-    )
-    unit_part = lax.dot_general(
-        span_back, columns, (((0,), (1,)), ((), ())), preferred_element_type=F32
-    )
-    unit_grad = scatter_seq(unit_part.reshape(seqs, tok, width))
     scale_one = lax.rsqrt(jnp.mean(inputs * inputs, axis=-1, keepdims=True) + NORM_EPS)
     unit_rows = inputs * scale_one
     input_grad = (
         middle_grad
         + scale_one * (unit_grad - unit_rows * jnp.mean(unit_grad * unit_rows, axis=-1, keepdims=True))
     ).astype(BF16)
-
-    cols_part = lax.dot_general(
-        unit_low, span_back, (((0,), (1,)), ((), ())), preferred_element_type=F32
-    ).reshape(shards, seqs * own_rows, heads_here * 3 * HEAD_DIM)
-    cols_sum = scatter_shard(
-        [lax.dynamic_index_in_dim(cols_part, shard ^ k, 0, keepdims=False) for k in range(4)]
-    )
-    cols_all = lax.all_to_all(
-        cols_sum.astype(BF16).reshape(seqs, own_rows, -1), "seq", split_axis=0, concat_axis=0, tiled=True
-    ).reshape(seqs, own_rows, shards, 3, HEAD_DIM)
-    unit_wgrads = jnp.transpose(cols_all, (3, 1, 2, 0, 4)).reshape(3, own_rows, width).astype(F32)
-    query_wgrad, key_wgrad, value_wgrad = [unit_wgrads[i] * gain_col for i in range(3)]
-    gain_one_out = sum(
-        jnp.sum(unit_wgrads[i] * weight.astype(F32), axis=1)
-        for i, weight in enumerate((query_weight, key_weight, value_weight))
-    )
-
-    out_low = by_span(head_out).astype(BF16)
-    out_slots = jnp.concatenate(
-        [
-            from_shard(lax.dynamic_index_in_dim(out_low, shard ^ k, 0, keepdims=False), k)
-            if k
-            else lax.dynamic_index_in_dim(out_low, shard, 0, keepdims=False)
-            for k in range(4)
-        ]
-    )
-    span_attend_grad = jnp.concatenate(gather_seq(attend_grad))
-    out_part = dot_nn(out_slots, span_attend_grad).reshape(shards, HEAD_DIM, width)
-    output_wgrad = scatter_shard([out_part[k] for k in range(4)])
-    gain_two_out = scatter_small(gain_two_part.reshape(shards * seqs, -1)).reshape(-1)
-
-    down_part = dot_nn(hidden, down_here)
-    layer_output = (middle + scatter_seq(down_part.reshape(seqs, tok, width))).astype(BF16)
-
-    def feed_wgrad(lhs_mat, rhs_mat):
-        part = trans_times(lhs_mat, rhs_mat).reshape(shards, -1, width)
-        return scatter_shard([part[k] for k in range(4)])
-
-    down_wgrad = feed_wgrad(hidden, span_grad)
-    gate_wgrad = feed_wgrad(gate_grad, feed_low)
-    up_wgrad = feed_wgrad(up_grad, feed_low)
+    gate_wgrad, up_wgrad, down_wgrad = [
+        after(point, feed_wsum)[m].astype(F32) for m in range(3)
+    ]
+    gain_rows_back = out_grad_blocks[:, HEAD_DIM].astype(F32)
+    gain_two_out = jnp.sum(
+        gain_rows_back[:, :own_rows] + gain_rows_back[:, own_rows : 2 * own_rows], axis=0
+    )
+    point = join(
+        point, cols_same, out_last, input_grad, gate_wgrad, up_wgrad, down_wgrad, gain_two_out
+    )
+    cols_same = after(point, cols_same)
+    cols_other = swap_cores(jnp.stack([block[1] for block in cols_same]))
+    query_wgrad, key_wgrad, value_wgrad, gain_one_out = unpack_columns(
+        place, gain_col, attn_weights, cols_same, cols_other
+    )
+    out_one, out_two = after(point, out_last)
+    output_wgrad = out_parts[0].astype(F32) + out_one.astype(F32) + out_two.astype(F32)
     return (
         layer_output,
         input_grad,
-        gain_one_out,
+        gain_one_out.reshape(-1),
         query_wgrad,
         key_wgrad,
         value_wgrad,

time: 912 us -> 622 us (0.68)
  the two profiles are of different devices: /device:TPU:8 before, /device:TPU:1 now
where the time goes in v2:
time: 622 us; the launch traced here: 612 us
  waiting for transfers between devices  204 us (33%)
  Pallas kernels  157 us (25%)
  starting transfers between devices  127 us (20%)
  local copies, waits for them, and re-layouts  54.8 us (9%)
  other arithmetic  34.7 us (6%)
  matrix products  17.7 us (3%)
  between operations  15.6 us (3%)
    ppermute x30, waiting for transfers between devices, from_chip(): lax.ppermute(values, 'seq', [((i + 2 * step) % count, i) for i in range(c...  128 us
    ppermute x33, waiting for transfers between devices, from_shard(): return lax.ppermute(values, 'shard', [(i, i ^ flip) for i in range(4)])  67.9 us
    ppermute x30, starting transfers between devices, from_chip(): lax.ppermute(values, 'seq', [((i + 2 * step) % count, i) for i in range(c...  50.7 us
    pallas_call x4, Pallas kernels, feed_blocks(): pl.pallas_call(functools.partial(feed_kernel, call, len(whole)), in_specs...  37.3 us
    pallas_call x1, Pallas kernels, attend_back(): pl.pallas_call(functools.partial(bwd_kernel, tok), grid=(spans,), in_spec...  35.1 us
    ppermute x32, starting transfers between devices, swap_cores(): return lax.ppermute(values, 'seq', [(i, i ^ 1) for i in range(count)])  30.8 us
    unnamed x170, local copies, waits for them, and re-layouts  30.1 us
    ppermute x33, starting transfers between devices, from_shard(): return lax.ppermute(values, 'shard', [(i, i ^ flip) for i in range(4)])  29.6 us
  transfers between devices with their start and end apart: 100, of which 33 were waited for; matrix products, arithmetic and copies ran while one was open for 12% of the time, Pallas kernels for 21%

profile of v2, /device:TPU:1, one launch (start us, length us, event | category | flops | bytes accessed | tf_op | source)
XLA Modules:
  0.0 611.6 jit_solution(387607362963768756)
XLA Ops:
  25.3 9.3 %collective-permute-done.2 = bf16[128,768]{1,0:T(8,128)(2,1)S(1)} collective-permute-done((bf16[128,768]{1,0:T(8,128)(2,1)S(1)}, bf16[128,768]{1,0:T(8,128)(2,1)S(1)}, u32[]{:S(2)}, u32[]{:S(2)}) %collective-permute-start.2) | collective-permute-done | bytes 196640 | tf_op jit(solution)/shard_map/ppermute | solution.py:1017
  47.6 8.8 %collective-permute-done.9.refs_6_ = bf16[128,2048]{1,0:T(8,128)(2,1)} collective-permute-done((bf16[128,2048]{1,0:T(8,128)(2,1)S(1)}, bf16[128,2048]{1,0:T(8,128)(2,1)}, u32[]{:S(2)}, u32[]{:S(2)}) %collective-permute-start.9) | collective-permute-done | bytes 524320 | tf_op jit(solution)/shard_map/ppermute | solution.py:1017
  56.4 11.7 %collective-permute-done.8.refs_2_ = bf16[128,2048]{1,0:T(8,128)(2,1)} collective-permute-done((bf16[128,2048]{1,0:T(8,128)(2,1)S(1)}, bf16[128,2048]{1,0:T(8,128)(2,1)}, u32[]{:S(2)}, u32[]{:S(2)}) %collective-permute-start.8) | collective-permute-done | bytes 524320 | tf_op jit(solution)/shard_map/ppermute | solution.py:1017
  76.6 7.6 %collective-permute-done.11.refs_4_ = bf16[256,768]{1,0:T(8,128)(2,1)S(1)} collective-permute-done((bf16[256,768]{1,0:T(8,128)(2,1)}, bf16[256,768]{1,0:T(8,128)(2,1)S(1)}, u32[]{:S(2)}, u32[]{:S(2)}) %collective-permute-start.11) | collective-permute-done | bytes 393248 | tf_op jit(solution)/shard_map/ppermute | solution.py:1021
  126.9 11.2 %collective-permute-done.23 = bf16[64,2048]{1,0:T(8,128)(2,1)} collective-permute-done((bf16[64,2048]{1,0:T(8,128)(2,1)S(1)}, bf16[64,2048]{1,0:T(8,128)(2,1)}, u32[]{:S(2)}, u32[]{:S(2)}) %collective-permute-start.23) | collective-permute-done | bytes 262176 | tf_op jit(solution)/shard_map/ppermute | solution.py:1017
  138.1 9.2 %collective-permute-done.26.refs_9_ = bf16[128,2048]{1,0:T(8,128)(2,1)} collective-permute-done((bf16[128,2048]{1,0:T(8,128)(2,1)}, bf16[128,2048]{1,0:T(8,128)(2,1)}, u32[]{:S(2)}, u32[]{:S(2)}) %collective-permute-start.26) | collective-permute-done | bytes 524320 | tf_op jit(solution)/shard_map/ppermute | solution.py:1021
  157.2 26.5 %attend.1 = (f32[4,64,1024]{2,1,0:T(8,128)S(1)}, bf16[4,64,1024]{2,1,0:T(8,128)(2,1)S(1)}, bf16[32,80,128]{2,1,0:T(8,128)(2,1)}, f32[4,1,1024]{2,1,0:T(1,128)S(1)}) custom-call(s32[1]{0:T(128)} %bitcast.place_ref, s32[4]{0:T(128)S(1)} %and_select_fusion.7.lo_ref, s32[4]{0:T(128)S(1)} %iota_minimum_fusion.full_ref, ...), custom_call_target="tpu_custom_call" | custom-call | flops 21474836480 | bytes 4194304 | tf_op jit(solution)/shard_map/attend/pallas_call | solution.py:503
  196.7 14.7 %collective-permute-done.33.refs_4_ = bf16[128,2048]{1,0:T(8,128)(2,1)} collective-permute-done((bf16[128,2048]{1,0:T(8,128)(2,1)S(1)}, bf16[128,2048]{1,0:T(8,128)(2,1)}, u32[]{:S(2)}, u32[]{:S(2)}) %collective-permute-start.33) | collective-permute-done | bytes 524320 | tf_op jit(solution)/shard_map/ppermute | solution.py:1021
  212.7 11.2 %collective-permute-done.34.refs_10_ = bf16[128,2048]{1,0:T(8,128)(2,1)} collective-permute-done((bf16[128,2048]{1,0:T(8,128)(2,1)}, bf16[128,2048]{1,0:T(8,128)(2,1)}, u32[]{:S(2)}, u32[]{:S(2)}) %collective-permute-start.34) | collective-permute-done | bytes 524320 | tf_op jit(solution)/shard_map/ppermute | solution.py:1021
  241.6 9.2 %collective-permute-done.42.refs_1_ = bf16[128,2048]{1,0:T(8,128)(2,1)S(1)} collective-permute-done((bf16[128,2048]{1,0:T(8,128)(2,1)S(1)}, bf16[128,2048]{1,0:T(8,128)(2,1)S(1)}, u32[]{:S(2)}, u32[]{:S(2)}) %collective-permute-start.42) | collective-permute-done | bytes 524320 | tf_op jit(solution)/shard_map/ppermute | solution.py:1017
  252.8 8.8 %collective-permute-done.41.refs_1_ = bf16[128,2048]{1,0:T(8,128)(2,1)S(1)} collective-permute-done((bf16[128,2048]{1,0:T(8,128)(2,1)S(1)}, bf16[128,2048]{1,0:T(8,128)(2,1)S(1)}, u32[]{:S(2)}, u32[]{:S(2)}) %collective-permute-start.41) | collective-permute-done | bytes 524320 | tf_op jit(solution)/shard_map/ppermute | solution.py:1017
  272.3 9.8 %collective-permute-done.51.refs_4_ = bf16[128,2048]{1,0:T(8,128)(2,1)S(1)} collective-permute-done((bf16[128,2048]{1,0:T(8,128)(2,1)S(1)}, bf16[128,2048]{1,0:T(8,128)(2,1)S(1)}, u32[]{:S(2)}, u32[]{:S(2)}) %collective-permute-start.51) | collective-permute-done | bytes 524320 | tf_op jit(solution)/shard_map/ppermute | solution.py:1021
  286.5 9.8 %feed_blocks.4 = (f32[128,2048]{1,0:T(8,128)S(1)}, bf16[128,2048]{1,0:T(8,128)(2,1)S(1)}, bf16[1024,2048]{1,0:T(8,128)(2,1)}, bf16[1024,2048]{1,0:T(8,128)(2,1)}...) custom-call(s32[1]{0:T(128)} %bitcast.21.refs_0_, ...), custom_call_target="tpu_custom_call" | custom-call | tf_op jit(solution)/shard_map/feed_blocks/pallas_call | solution.py:831
  299.4 9.6 %feed_blocks.5 = (f32[128,2048]{1,0:T(8,128)S(1)}, bf16[128,2048]{1,0:T(8,128)(2,1)S(1)}, bf16[1024,2048]{1,0:T(8,128)(2,1)}, bf16[1024,2048]{1,0:T(8,128)(2,1)}...) custom-call(s32[1]{0:T(128)} %bitcast.21.refs_0_, ...), custom_call_target="tpu_custom_call", output_to_operand_aliasing={{2}: (7, {}), {3}: (8, {}), {4}: (9, {}), {5}: (10, {}), {6... | custom-call | tf_op jit(solution)/shard_map/feed_blocks/pallas_call | solution.py:831
  309.1 9.4 %feed_blocks.6 = (f32[128,2048]{1,0:T(8,128)S(1)}, bf16[128,2048]{1,0:T(8,128)(2,1)S(1)}, bf16[1024,2048]{1,0:T(8,128)(2,1)}, bf16[1024,2048]{1,0:T(8,128)(2,1)}...) custom-call(s32[1]{0:T(128)} %bitcast.21.refs_0_, ...), custom_call_target="tpu_custom_call", output_to_operand_aliasing={{2}: (7, {}), {3}: (8, {}), {4}: (9, {}), {5}: (10, {}), {6... | custom-call | tf_op jit(solution)/shard_map/feed_blocks/pallas_call | solution.py:831
  344.9 8.5 %feed_blocks.7 = (f32[128,2048]{1,0:T(8,128)S(1)}, bf16[128,2048]{1,0:T(8,128)(2,1)S(1)}, bf16[1024,2048]{1,0:T(8,128)(2,1)}, bf16[1024,2048]{1,0:T(8,128)(2,1)}...) custom-call(s32[1]{0:T(128)} %bitcast.21.refs_0_, ...), custom_call_target="tpu_custom_call", output_to_operand_aliasing={{2}: (7, {}), {3}: (8, {}), {4}: (9, {}), {5}: (10, {}), {6... | custom-call | tf_op jit(solution)/shard_map/feed_blocks/pallas_call | solution.py:831
  353.5 18.9 %feed_wgrads.1 = bf16[4,3,256,2048]{3,2,1,0:T(8,128)(2,1)S(1)} custom-call(bf16[1024,1024]{1,0:T(8,128)(2,1)} %get-tuple-element.294.gate_ref, bf16[1024,1024]{1,0:T(8,128)(2,1)} %get-tuple-element.295.up_ref, bf16[1024,1024]{1,0:T(8,128)(2,1)} %get-tuple-element.296.hidden_ref, bf16[1024,2048]{1,0:T(8,128)(2,1)} %get-tuple-element.297.tokens_ref, ...), custom_call_target="tpu_custom_call" | custom-call | tf_op jit(solution)/shard_map/feed_wgrads/pallas_call | solution.py:979
  376.1 10.3 %token_grad.1 = (f32[128,2048]{1,0:T(8,128)S(1)}, bf16[128,2048]{1,0:T(8,128)(2,1)S(1)}, bf16[32,80,128]{2,1,0:T(8,128)(2,1)}) custom-call(s32[32]{0:T(128)S(1)} %fusion.55.index_ref, f32[128,2048]{1,0:T(8,128)S(1)} %convert_add_fusion.1.own_ref, bf16[128,2048]{1,0:T(8,128)(2,1)} %collective-permute-done.59.one_ref, bf16[128,2048]{1,0:T(8,128)(2,1)S(1)} %copy-done.32, ...), custom_call_target="tpu_custom_call" | custom-call | tf_op jit(solution)/shard_map/token_grad/pallas_call | solution.py:944
  403.7 13.8 %collective-permute-done.66.refs_6_ = bf16[128,2048]{1,0:T(8,128)(2,1)} collective-permute-done((bf16[128,2048]{1,0:T(8,128)(2,1)}, bf16[128,2048]{1,0:T(8,128)(2,1)}, u32[]{:S(2)}, u32[]{:S(2)}) %collective-permute-start.66) | collective-permute-done | bytes 524320 | tf_op jit(solution)/shard_map/ppermute | solution.py:1017
  428.8 35.1 %attend_back.1 = bf16[4,192,1024]{2,1,0:T(8,128)(2,1)} custom-call(s32[1]{0:T(128)} %bitcast.place_ref, s32[4]{0:T(128)S(1)} %copy-done.46, s32[4]{0:T(128)S(1)} %copy-done.45, s32[4,1,1024]{2,1,0:T(1,128)S(1)} %copy-done.43, bf16[4,192,1024]{2,1,0:T(8,128)(2,1)} %all-to-all-done.qkv_ref, f32[4,1,1024]{2,1,0:T(1,128)S(1)} %copy-done.50, ...), custom_call_target="tpu_custom_call" | custom-call | flops 30064771072 | bytes 4194304 | tf_op jit(solution)/shard_map/attend_back/pallas_call | solution.py:543
  488.9 7.7 %collective-permute-done.70 = bf16[128,2048]{1,0:T(8,128)(2,1)} collective-permute-done((bf16[128,2048]{1,0:T(8,128)(2,1)}, bf16[128,2048]{1,0:T(8,128)(2,1)}, u32[]{:S(2)}, u32[]{:S(2)}) %collective-permute-start.70) | collective-permute-done | bytes 524320 | tf_op jit(solution)/shard_map/ppermute | solution.py:1017
  521.6 8.5 %collective-permute-done.80 = bf16[256,768]{1,0:T(8,128)(2,1)S(1)} collective-permute-done((bf16[256,768]{1,0:T(8,128)(2,1)S(1)}, bf16[256,768]{1,0:T(8,128)(2,1)S(1)}, u32[]{:S(2)}, u32[]{:S(2)}) %collective-permute-start.80) | collective-permute-done | bytes 393248 | tf_op jit(solution)/shard_map/ppermute | solution.py:1021
  538.1 8.2 %collective-permute-done.82 = bf16[128,2048]{1,0:T(8,128)(2,1)S(1)} collective-permute-done((bf16[128,2048]{1,0:T(8,128)(2,1)S(1)}, bf16[128,2048]{1,0:T(8,128)(2,1)S(1)}, u32[]{:S(2)}, u32[]{:S(2)}) %collective-permute-start.82) | collective-permute-done | bytes 524320 | tf_op jit(solution)/shard_map/ppermute | solution.py:1017
  546.3 11.0 %collective-permute-done.83 = bf16[128,2048]{1,0:T(8,128)(2,1)S(1)} collective-permute-done((bf16[128,2048]{1,0:T(8,128)(2,1)S(1)}, bf16[128,2048]{1,0:T(8,128)(2,1)S(1)}, u32[]{:S(2)}, u32[]{:S(2)}) %collective-permute-start.83) | collective-permute-done | bytes 524320 | tf_op jit(solution)/shard_map/ppermute | solution.py:1017
  (461 shorter events, 306.9 us)
Async XLA Ops:
  39.8 28.3 %collective-permute-start.7 = (bf16[512,768]{1,0:T(8,128)(2,1)S(1)}, bf16[512,768]{1,0:T(8,128)(2,1)S(1)}, u32[]{:S(2)}, u32[]{:S(2)}) collective-permute-start(bf16[512,768]{1,0:T(8,128)(2,1)S(1)} %constant_dynamic-update-slice_fusion.refs_0_), channel_id=1, source_target_pairs={{0,16},{8,24},{16,0},{24,8},{1,17},{9,25},{17,1},{25,9},{2,18},{10... | collective-permute-start | bytes 2359304 | tf_op jit(solution)/shard_map/ppermute | solution.py:1021
  45.7 27.9 %collective-permute-start.13 = (bf16[128,2048]{1,0:T(8,128)(2,1)S(1)}, bf16[128,2048]{1,0:T(8,128)(2,1)}, u32[]{:S(2)}, u32[]{:S(2)}) collective-permute-start(bf16[128,2048]{1,0:T(8,128)(2,1)S(1)} %copy-done.5), channel_id=1, source_target_pairs={{0,1},{1,0},{2,3},{3,2},{4,5},{5,4},{6,7},{7,6},{8,9},{9,8},{10,11... | collective-permute-start | bytes 1572872 | tf_op jit(solution)/shard_map/ppermute | solution.py:1012
  112.9 34.4 %all-to-all-start = ((bf16[4,192,1024]{2,1,0:T(8,128)(2,1)}), bf16[4,192,1024]{2,1,0:T(8,128)(2,1)}, u32[]{:S(2)}, u32[]{:S(2)}) async-start(bf16[4,192,1024]{2,1,0:T(8,128)(2,1)} %bitcast.133), calls=%async_computation | async-start | bytes 3145728 | tf_op jit(solution)/shard_map/all_to_all | solution.py:1151
  117.6 29.7 %collective-permute-start.26 = (bf16[128,2048]{1,0:T(8,128)(2,1)}, bf16[128,2048]{1,0:T(8,128)(2,1)}, u32[]{:S(2)}, u32[]{:S(2)}) collective-permute-start(bf16[128,2048]{1,0:T(8,128)(2,1)} %get-tuple-element.210), channel_id=1, source_target_pairs={{0,16},{8,24},{16,0},{24,8},{1,17},{9,25},{17,1},{25,9},{2,18},{10... | collective-permute-start | bytes 1572872 | tf_op jit(solution)/shard_map/ppermute | solution.py:1021
  119.0 28.3 %collective-permute-start.25 = (bf16[128,2048]{1,0:T(8,128)(2,1)}, bf16[128,2048]{1,0:T(8,128)(2,1)}, u32[]{:S(2)}, u32[]{:S(2)}) collective-permute-start(bf16[128,2048]{1,0:T(8,128)(2,1)} %get-tuple-element.210), channel_id=1, source_target_pairs={{0,8},{8,0},{16,24},{24,16},{1,9},{9,1},{17,25},{25,17},{2,10},{10... | collective-permute-start | bytes 1572872 | tf_op jit(solution)/shard_map/ppermute | solution.py:1021
  125.2 61.0 %collective-permute-start.31 = (bf16[128,2048]{1,0:T(8,128)(2,1)}, bf16[128,2048]{1,0:T(8,128)(2,1)}, u32[]{:S(2)}, u32[]{:S(2)}) collective-permute-start(bf16[128,2048]{1,0:T(8,128)(2,1)} %grad_ref.1), channel_id=1, source_target_pairs={{6,0},{7,1},{0,2},{1,3},{2,4},{3,5},{4,6},{5,7},{14,8},{15,9},{8,1... | collective-permute-start | bytes 1572872 | tf_op jit(solution)/shard_map/ppermute | solution.py:1017
  150.3 35.9 %collective-permute-start.29 = (bf16[256,2048]{1,0:T(8,128)(2,1)S(1)}, bf16[256,2048]{1,0:T(8,128)(2,1)S(1)}, u32[]{:S(2)}, u32[]{:S(2)}) collective-permute-start(bf16[256,2048]{1,0:T(8,128)(2,1)S(1)} %constant_dynamic-update-slice_fusion.4.refs_0_), channel_id=1, source_target_pairs={{0,1},{1,0},{2,3},{3,2},{4,5},{5,4},{6,7},{7,6},{8,9},{9,8},{10,11... | collective-permute-start | bytes 3145736 | tf_op jit(solution)/shard_map/ppermute | solution.py:1012
  151.8 34.3 %collective-permute-start.28 = (bf16[256,2048]{1,0:T(8,128)(2,1)S(1)}, bf16[256,2048]{1,0:T(8,128)(2,1)}, u32[]{:S(2)}, u32[]{:S(2)}) collective-permute-start(bf16[256,2048]{1,0:T(8,128)(2,1)S(1)} %constant_dynamic-update-slice_fusion.4.refs_0_), channel_id=1, source_target_pairs={{0,16},{8,24},{16,0},{24,8},{1,17},{9,25},{17,1},{25,9},{2,18},{10... | collective-permute-start | bytes 3145736 | tf_op jit(solution)/shard_map/ppermute | solution.py:1021
  153.0 33.1 %collective-permute-start.27 = (bf16[256,2048]{1,0:T(8,128)(2,1)S(1)}, bf16[256,2048]{1,0:T(8,128)(2,1)}, u32[]{:S(2)}, u32[]{:S(2)}) collective-permute-start(bf16[256,2048]{1,0:T(8,128)(2,1)S(1)} %constant_dynamic-update-slice_fusion.4.refs_0_), channel_id=1, source_target_pairs={{0,8},{8,0},{16,24},{24,16},{1,9},{9,1},{17,25},{25,17},{2,10},{10... | collective-permute-start | bytes 3145736 | tf_op jit(solution)/shard_map/ppermute | solution.py:1021
  153.3 32.8 %collective-permute-start.30 = (bf16[128,2048]{1,0:T(8,128)(2,1)}, bf16[128,2048]{1,0:T(8,128)(2,1)}, u32[]{:S(2)}, u32[]{:S(2)}) collective-permute-start(bf16[128,2048]{1,0:T(8,128)(2,1)} %collective-permute-done.24.refs_3_), channel_id=1, source_target_pairs={{2,0},{3,1},{4,2},{5,3},{6,4},{7,5},{0,6},{1,7},{10,8},{11,9},{12,... | collective-permute-start | bytes 1572872 | tf_op jit(solution)/shard_map/ppermute | solution.py:1017
  187.1 37.3 %all-to-all-start.1 = ((bf16[32,80,128]{2,1,0:T(8,128)(2,1)}), bf16[32,80,128]{2,1,0:T(8,128)(2,1)}, u32[]{:S(2)}, u32[]{:S(2)}) async-start(bf16[32,80,128]{2,1,0:T(8,128)(2,1)} %get-tuple-element.220), calls=%async_computation.1 | async-start | bytes 1310720 | tf_op jit(solution)/shard_map/all_to_all | solution.py:1168
  190.9 391.1 %reduce-scatter.2.cloned.1.call-start = ((), (), s32[]{:S(2)}) async-start(), calls=%async_computation.5 | async-start | bytes 15728640 | tf_op jit(solution)/shard_map/reduce_scatter | solution.py:1250
  193.5 30.9 %collective-permute-start.36 = (bf16[256,2048]{1,0:T(8,128)(2,1)}, bf16[256,2048]{1,0:T(8,128)(2,1)}, u32[]{:S(2)}, u32[]{:S(2)}) collective-permute-start(bf16[256,2048]{1,0:T(8,128)(2,1)} %collective-permute-done.27.refs_1_), channel_id=1, source_target_pairs={{0,1},{1,0},{2,3},{3,2},{4,5},{5,4},{6,7},{7,6},{8,9},{9,8},{10,11... | collective-permute-start | bytes 3145736 | tf_op jit(solution)/shard_map/ppermute | solution.py:1012
  194.1 30.2 %collective-permute-start.37 = (bf16[256,2048]{1,0:T(8,128)(2,1)}, bf16[256,2048]{1,0:T(8,128)(2,1)}, u32[]{:S(2)}, u32[]{:S(2)}) collective-permute-start(bf16[256,2048]{1,0:T(8,128)(2,1)} %collective-permute-done.28.refs_2_), channel_id=1, source_target_pairs={{0,1},{1,0},{2,3},{3,2},{4,5},{5,4},{6,7},{7,6},{8,9},{9,8},{10,11... | collective-permute-start | bytes 3145736 | tf_op jit(solution)/shard_map/ppermute | solution.py:1012
  328.1 44.4 %collective-permute-start.59 = (bf16[128,2048]{1,0:T(8,128)(2,1)}, bf16[128,2048]{1,0:T(8,128)(2,1)}, u32[]{:S(2)}, u32[]{:S(2)}) collective-permute-start(bf16[128,2048]{1,0:T(8,128)(2,1)} %add_convert_fusion.5), channel_id=1, source_target_pairs={{6,0},{7,1},{0,2},{1,3},{2,4},{3,5},{4,6},{5,7},{14,8},{15,9},{8,1... | collective-permute-start | bytes 1572872 | tf_op jit(solution)/shard_map/ppermute | solution.py:1017
  328.1 44.5 %collective-permute-start.60 = (bf16[128,2048]{1,0:T(8,128)(2,1)}, bf16[128,2048]{1,0:T(8,128)(2,1)}, u32[]{:S(2)}, u32[]{:S(2)}) collective-permute-start(bf16[128,2048]{1,0:T(8,128)(2,1)} %add_convert_fusion.4), channel_id=1, source_target_pairs={{2,0},{3,1},{4,2},{5,3},{6,4},{7,5},{0,6},{1,7},{10,8},{11,9},{12,... | collective-permute-start | bytes 1572872 | tf_op jit(solution)/shard_map/ppermute | solution.py:1017
  332.5 40.0 %collective-permute-start.63 = (bf16[64,1024]{1,0:T(8,128)(2,1)S(1)}, bf16[64,1024]{1,0:T(8,128)(2,1)S(1)}, u32[]{:S(2)}, u32[]{:S(2)}) collective-permute-start(bf16[64,1024]{1,0:T(8,128)(2,1)S(1)} %get-tuple-element.390), channel_id=1, source_target_pairs={{0,24},{8,16},{16,8},{24,0},{1,25},{9,17},{17,9},{25,1},{2,26},{10... | collective-permute-start | bytes 393224 | tf_op jit(solution)/shard_map/ppermute | solution.py:1021
  334.8 37.7 %collective-permute-start.62 = (bf16[64,1024]{1,0:T(8,128)(2,1)S(1)}, bf16[64,1024]{1,0:T(8,128)(2,1)S(1)}, u32[]{:S(2)}, u32[]{:S(2)}) collective-permute-start(bf16[64,1024]{1,0:T(8,128)(2,1)S(1)} %get-tuple-element.391), channel_id=1, source_target_pairs={{0,16},{8,24},{16,0},{24,8},{1,17},{9,25},{17,1},{25,9},{2,18},{10... | collective-permute-start | bytes 393224 | tf_op jit(solution)/shard_map/ppermute | solution.py:1021
  335.0 37.5 %collective-permute-start.61 = (bf16[64,1024]{1,0:T(8,128)(2,1)S(1)}, bf16[64,1024]{1,0:T(8,128)(2,1)S(1)}, u32[]{:S(2)}, u32[]{:S(2)}) collective-permute-start(bf16[64,1024]{1,0:T(8,128)(2,1)S(1)} %get-tuple-element.392), channel_id=1, source_target_pairs={{0,8},{8,0},{16,24},{24,16},{1,9},{9,1},{17,25},{25,17},{2,10},{10... | collective-permute-start | bytes 393224 | tf_op jit(solution)/shard_map/ppermute | solution.py:1021
  389.9 27.6 %all-to-all-start.2 = ((bf16[32,80,128]{2,1,0:T(8,128)(2,1)}), bf16[32,80,128]{2,1,0:T(8,128)(2,1)}, u32[]{:S(2)}, u32[]{:S(2)}) async-start(bf16[32,80,128]{2,1,0:T(8,128)(2,1)} %get-tuple-element.311), calls=%async_computation.2 | async-start | bytes 1310720 | tf_op jit(solution)/shard_map/all_to_all | solution.py:1247
  417.5 46.3 %collective-permute-start.67 = (bf16[128,2048]{1,0:T(8,128)(2,1)}, bf16[128,2048]{1,0:T(8,128)(2,1)}, u32[]{:S(2)}, u32[]{:S(2)}) collective-permute-start(bf16[128,2048]{1,0:T(8,128)(2,1)} %get-tuple-element.315), channel_id=1, source_target_pairs={{6,0},{7,1},{0,2},{1,3},{2,4},{3,5},{4,6},{5,7},{14,8},{15,9},{8,1... | collective-permute-start | bytes 1572872 | tf_op jit(solution)/shard_map/ppermute | solution.py:1017
  422.3 41.6 %collective-permute-start.68 = (bf16[128,2048]{1,0:T(8,128)(2,1)}, bf16[128,2048]{1,0:T(8,128)(2,1)}, u32[]{:S(2)}, u32[]{:S(2)}) collective-permute-start(bf16[128,2048]{1,0:T(8,128)(2,1)} %copy-done.34), channel_id=1, source_target_pairs={{6,0},{7,1},{0,2},{1,3},{2,4},{3,5},{4,6},{5,7},{14,8},{15,9},{8,1... | collective-permute-start | bytes 1572872 | tf_op jit(solution)/shard_map/ppermute | solution.py:1017
  423.1 40.8 %collective-permute-start.69 = (bf16[128,2048]{1,0:T(8,128)(2,1)}, bf16[128,2048]{1,0:T(8,128)(2,1)}, u32[]{:S(2)}, u32[]{:S(2)}) collective-permute-start(bf16[128,2048]{1,0:T(8,128)(2,1)} %get-tuple-element.320), channel_id=1, source_target_pairs={{2,0},{3,1},{4,2},{5,3},{6,4},{7,5},{0,6},{1,7},{10,8},{11,9},{12,... | collective-permute-start | bytes 1572872 | tf_op jit(solution)/shard_map/ppermute | solution.py:1017
  463.9 32.6 %all-to-all-start.3 = ((bf16[4,192,1024]{2,1,0:T(8,128)(2,1)}), bf16[4,192,1024]{2,1,0:T(8,128)(2,1)}, u32[]{:S(2)}, u32[]{:S(2)}) async-start(bf16[4,192,1024]{2,1,0:T(8,128)(2,1)} %attend_back.1), calls=%async_computation.3 | async-start | bytes 3145728 | tf_op jit(solution)/shard_map/all_to_all | solution.py:1265
  (158 other events, 1859.9 us)
Sparse Core Ops, SparseCore 0:
  388.4 141.3 reduce-scatter.1

commit v3 on v2

--- a/solution.py
+++ b/solution.py
@@ -336,17 +336,26 @@
     )
 
 
-def slot_block(slot, place, half):
-    z, core = place // 2, place % 2
-    return ((z + slot // 2) % half) * 2 + (core + slot) % 2
-
-
-def fwd_kernel(tok, place_ref, lo_ref, full_ref, start_ref, qkv_ref, gain_ref, out_ref, low_ref, blocks_ref, lse_ref,
-               k_nat, m_s, l_s, acc_s):
+def allowed_pairs(i, j, keys, cols, span, start_ref, same):
+    shape = (keys.stop - keys.start, cols.stop - cols.start)
+    k_pos = j * span + keys.start + lax.broadcasted_iota(jnp.int32, shape, 0)
+    begun = k_pos >= start_ref[i][:, cols]
+    if not same:
+        return begun
+    q_pos = i * span + cols.start + lax.broadcasted_iota(jnp.int32, shape, 1)
+    return (k_pos <= q_pos) & begun
+
+
+def own_span_parts(span):
+    half = span // 2
+    return (slice(0, half), slice(0, half)), (slice(0, span), slice(half, span))
+
+
+def fwd_kernel(tok, shard_ref, lo_ref, full_ref, start_ref, qkv_ref, gain_ref, out_ref, low_ref, blocks_ref,
+               lse_ref, k_nat, m_s, l_s, acc_s):
     i = pl.program_id(0)
     spans, rows, span = qkv_ref.shape
     slots = span // tok
-    place = place_ref[0]
     scale2 = HEAD_DIM ** -0.5 * math.log2(math.e)
 
     @pl.when(i == 0)
@@ -354,23 +363,23 @@
         for s in range(spans):
             k_nat[pl.ds(s * span, span), :] = qkv_ref[s, HEAD_DIM : 2 * HEAD_DIM, :].T
 
-    q_t = qkv_ref[i, :HEAD_DIM, :]
     m_s[...] = jnp.full_like(m_s, -1e30)
     l_s[...] = jnp.zeros_like(l_s)
     acc_s[...] = jnp.zeros_like(acc_s)
 
-    def step(j, masked, same=False):
-        s_t = dot_nn(k_nat[pl.ds(pl.multiple_of(j * span, span), span), :], q_t) * scale2
+    def step(j, masked, same=False, keys=slice(0, span), cols=slice(0, span)):
+        k_rows = pl.ds(pl.multiple_of(j * span + keys.start, 128), keys.stop - keys.start)
+        s_t = dot_nn(k_nat[k_rows, :], qkv_ref[i, :HEAD_DIM, cols]) * scale2
         if masked:
-            s_t = jnp.where(allowed_pairs(i, j, place, tok, span, start_ref, same), s_t, -jnp.inf)
-        m_old = m_s[...]
+            s_t = jnp.where(allowed_pairs(i, j, keys, cols, span, start_ref, same), s_t, -jnp.inf)
+        m_old = m_s[:, cols]
         m_new = jnp.maximum(m_old, jnp.max(s_t, axis=0, keepdims=True))
         alpha = jnp.exp2(m_old - m_new)
         p_t = jnp.exp2(s_t - m_new)
-        l_s[...] = l_s[...] * alpha + jnp.sum(p_t, axis=0, keepdims=True)
-        m_s[...] = m_new
-        acc_s[...] = acc_s[...] * alpha + dot_nn(
-            qkv_ref[j, 2 * HEAD_DIM :, :], p_t.astype(jnp.bfloat16)
+        l_s[:, cols] = l_s[:, cols] * alpha + jnp.sum(p_t, axis=0, keepdims=True)
+        m_s[:, cols] = m_new
+        acc_s[:, cols] = acc_s[:, cols] * alpha + dot_nn(
+            qkv_ref[j, 2 * HEAD_DIM :, keys], p_t.astype(jnp.bfloat16)
         )
 
     def loop_body(masked):
@@ -382,71 +391,56 @@
 
     lax.fori_loop(lo_ref[i], full_ref[i], loop_body(True), 0)
     lax.fori_loop(full_ref[i], i, loop_body(False), 0)
-    step(i, True, True)
+    for keys, cols in own_span_parts(span):
+        step(i, True, True, keys, cols)
     out = acc_s[...] / l_s[...]
     out_ref[0] = out
     low = out.astype(jnp.bfloat16)
-    low_ref[0] = low
+    low_ref[i ^ shard_ref[0]] = low
     lse_ref[0] = m_s[...] + jnp.log2(l_s[...])
     for slot in range(slots):
-        at = slot_block(slot, place, slots // 2)
-        blocks_ref[at, :HEAD_DIM] = low[:, slot * tok : (slot + 1) * tok]
-        blocks_ref[at, HEAD_DIM:] = gain_ref[...]
-
-
-def span_positions_of(lane, place, tok, span):
-    half = span // tok // 2
-    return slot_block(lane // tok, place, half) * tok + lane % tok
-
-
-def allowed_pairs(i, j, place, tok, span, start_ref, same):
-    k_lane = lax.broadcasted_iota(jnp.int32, (span, 128), 0)
-    k_pos = (j * span + span_positions_of(k_lane, place, tok, span))[:, :1]
-    begun = k_pos >= start_ref[i]
-    if not same:
-        return begun
-    q_lane = lax.broadcasted_iota(jnp.int32, (8, span), 1)
-    q_pos = (i * span + span_positions_of(q_lane, place, tok, span))[:1]
-    return (k_pos <= q_pos) & begun
-
-
-def bwd_kernel(tok, place_ref, hi_ref, full_ref, start_ref, qkv_ref, lse_ref, out_ref, dob_ref,
-               cos_ref, sin_ref, back_ref, dq_s, dk_s, dv_s, do_s, di_s):
+        blocks_ref[slot, :HEAD_DIM] = low[:, slot * tok : (slot + 1) * tok]
+        blocks_ref[slot, HEAD_DIM:] = gain_ref[...]
+
+
+def bwd_kernel(tok, hi_ref, full_ref, start_ref, qkv_ref, lse_ref, out_hbm, dob_ref,
+               cos_ref, sin_ref, back_ref, dq_s, dk_s, dv_s, do_s, di_s, out_ref, sem):
     j = pl.program_id(0)
     spans, rows, span = qkv_ref.shape
     slots = span // tok
-    place = place_ref[0]
     scale = HEAD_DIM ** -0.5
     scale2 = scale * math.log2(math.e)
 
     @pl.when(j == 0)
     def _():
+        copy = pltpu.make_async_copy(out_hbm, out_ref, sem)
+        copy.start()
         dq_s[...] = jnp.zeros_like(dq_s)
         for s in range(spans):
             for slot in range(slots):
-                do_s[s, :, slot * tok : (slot + 1) * tok] = dob_ref[
-                    s * slots + slot_block(slot, place, slots // 2), :HEAD_DIM
-                ]
+                do_s[s, :, slot * tok : (slot + 1) * tok] = dob_ref[s * slots + slot, :HEAD_DIM]
+        copy.wait()
+        for s in range(spans):
             di_s[s] = jnp.sum(do_s[s].astype(jnp.float32) * out_ref[s], axis=0, keepdims=True)
 
-    k_t = qkv_ref[j, HEAD_DIM : 2 * HEAD_DIM, :]
-    k_nat = k_t.T
+    k_nat = qkv_ref[j, HEAD_DIM : 2 * HEAD_DIM, :].T
     v_nat = qkv_ref[j, 2 * HEAD_DIM :, :].T
     dk_s[...] = jnp.zeros_like(dk_s)
     dv_s[...] = jnp.zeros_like(dv_s)
 
-    def step(i, masked, same=False):
-        q_t = qkv_ref[i, :HEAD_DIM, :]
-        p_t = jnp.exp2(dot_nn(k_nat, q_t) * scale2 - lse_ref[i])
+    def step(i, masked, same=False, keys=slice(0, span), cols=slice(0, span)):
+        q_t = qkv_ref[i, :HEAD_DIM, cols]
+        p_t = jnp.exp2(dot_nn(k_nat[keys], q_t) * scale2 - lse_ref[i][:, cols])
         if masked:
-            p_t = jnp.where(allowed_pairs(i, j, place, tok, span, start_ref, same), p_t, 0.0)
-        do_t = do_s[i]
-        dv_s[...] += times_trans(do_t, p_t.astype(jnp.bfloat16))
-        ds_t = (p_t * (dot_nn(v_nat, do_t) - di_s[i])).astype(jnp.bfloat16)
-        dk_s[...] += times_trans(q_t, ds_t)
-        dq_s[i] += dot_nn(k_t, ds_t)
-
-    step(j, True, True)
+            p_t = jnp.where(allowed_pairs(i, j, keys, cols, span, start_ref, same), p_t, 0.0)
+        do_t = do_s[i, :, cols]
+        dv_s[:, keys] += times_trans(do_t, p_t.astype(jnp.bfloat16))
+        ds_t = (p_t * (dot_nn(v_nat[keys], do_t) - di_s[i][:, cols])).astype(jnp.bfloat16)
+        dk_s[:, keys] += times_trans(q_t, ds_t)
+        dq_s[i, :, cols] += dot_nn(qkv_ref[j, HEAD_DIM : 2 * HEAD_DIM, keys], ds_t)
+
+    for keys, cols in own_span_parts(span):
+        step(j, True, True, keys, cols)
 
     def body(i, carry):
         whole = full_ref[i] <= j
@@ -489,7 +483,7 @@
     return start[:, None, :], first, whole, last
 
 
-def attend(qkv, gain_rows, tok, place, bounds):
+def attend(qkv, gain_rows, tok, shard, bounds):
     spans, rows, span = qkv.shape
     stream = spans * span
     slots = span // tok
@@ -506,13 +500,13 @@
         in_specs=[smem, smem, smem, vmem, vmem, vmem],
         out_specs=[
             one(HEAD_DIM, span),
-            one(HEAD_DIM, span),
+            pl.BlockSpec((spans, HEAD_DIM, span), lambda i: (0, 0, 0)),
             pl.BlockSpec((slots, HEAD_DIM + EXTRA, tok), lambda i: (i, 0, 0)),
             one(1, span),
         ],
         out_shape=[
-            jax.ShapeDtypeStruct((spans, HEAD_DIM, span), jnp.float32),
-            jax.ShapeDtypeStruct((spans, HEAD_DIM, span), jnp.bfloat16),
+            pltpu.HBM((spans, HEAD_DIM, span), jnp.float32),
+            pltpu.HBM((spans, HEAD_DIM, span), jnp.bfloat16),
             pltpu.HBM((stream // tok, HEAD_DIM + EXTRA, tok), jnp.bfloat16),
             jax.ShapeDtypeStruct((spans, 1, span), jnp.float32),
         ],
@@ -527,10 +521,10 @@
             flops=stream * stream * 256 * 5, bytes_accessed=stream * 1024, transcendentals=0
         ),
         name="attend",
-    )(place, first, whole, start, qkv, gain_rows)
-
-
-def attend_back(qkv, lse, out, out_grad, cos_t, sin_t, tok, place, bounds):
+    )(shard, first, whole, start, qkv, gain_rows)
+
+
+def attend_back(qkv, lse, out, out_grad, cos_t, sin_t, tok, bounds):
     spans, rows, span = qkv.shape
     stream = spans * span
     start, first, whole, last = bounds
@@ -543,7 +537,7 @@
     return pl.pallas_call(
         functools.partial(bwd_kernel, tok),
         grid=(spans,),
-        in_specs=[smem, smem, smem, vmem, vmem, vmem, vmem, vmem]
+        in_specs=[smem, smem, vmem, vmem, vmem, pl.BlockSpec(memory_space=pl.ANY), vmem]
         + [one(HEAD_DIM // 2, span)] * 2,
         out_specs=one(rows, span),
         out_shape=pltpu.HBM(qkv.shape, jnp.bfloat16),
@@ -553,21 +547,30 @@
             pltpu.VMEM((HEAD_DIM, span), jnp.float32),
             pltpu.VMEM((spans, HEAD_DIM, span), jnp.bfloat16),
             pltpu.VMEM((spans, 1, span), jnp.float32),
+            pltpu.VMEM((spans, HEAD_DIM, span), jnp.float32),
+            pltpu.SemaphoreType.DMA,
         ],
-        compiler_params=pltpu.CompilerParams(vmem_limit_bytes=30 * 2**20),
+        compiler_params=pltpu.CompilerParams(vmem_limit_bytes=32 * 2**20),
         cost_estimate=pl.CostEstimate(
             flops=stream * stream * 256 * 7, bytes_accessed=stream * 1024, transcendentals=0
         ),
         name="attend_back",
-    )(place, last, whole, start, qkv, lse, out, out_grad, *in_hbm([cos_t, sin_t]))
+    )(last, whole, start, qkv, lse, *in_hbm([out]), out_grad, *in_hbm([cos_t, sin_t]))
+
+
+def as_column(row):
+    shape = (row.shape[1], row.shape[1])
+    same = lax.broadcasted_iota(jnp.int32, shape, 0) == lax.broadcasted_iota(jnp.int32, shape, 1)
+    return jnp.sum(jnp.where(same, row.astype(jnp.float32), 0.0), axis=1, keepdims=True)
 
 
 def pack_kernel(heads, place_ref, gain_ref, query_ref, key_ref, value_ref, out_ref):
     steps = out_ref.shape[1]
     seqs = 2 * steps
     z, core = place_ref[0] // 2, place_ref[0] % 2
+    gain_col = as_column(gain_ref[...])
     for m, ref in enumerate((query_ref, key_ref, value_ref)):
-        rows = (ref[...].astype(jnp.float32) * gain_ref[...]).astype(jnp.bfloat16)
+        rows = (ref[...].astype(jnp.float32) * gain_col).astype(jnp.bfloat16)
         for head in range(heads):
             at = (head // seqs * 3 + m) * HEAD_DIM
             other = (core + head) % 2
@@ -577,7 +580,7 @@
             ]
 
 
-def pack_columns(place, gain_col, weights, seqs):
+def pack_columns(place, gain_row, weights, seqs):
     rows, width = weights[0].shape
     heads = width // HEAD_DIM
     vmem = pl.BlockSpec(memory_space=pltpu.VMEM)
@@ -590,7 +593,7 @@
         ),
         cost_estimate=SHORT,
         name="pack_columns",
-    )(place, gain_col, *weights)
+    )(place, gain_row, *weights)
 
 
 def order_kernel(index_ref, *refs):
@@ -618,39 +621,113 @@
     )(index, *pieces).reshape(blocks * rows, width)
 
 
+def cols_kernel(shard_ref, back_ref, unit_ref, out_ref):
+    slots, _, width = out_ref.shape
+    back = back_ref[...]
+    for k in range(slots):
+        at = pl.ds(pl.multiple_of((shard_ref[0] ^ k) * width, width), width)
+        out_ref[k] = dot_nn(back, unit_ref[:, at]).astype(jnp.bfloat16)
+
+
+def cols_parts_of(shard, back, unit_low, slots):
+    rows = back.shape[0]
+    width = unit_low.shape[1] // slots
+    vmem = pl.BlockSpec(memory_space=pltpu.VMEM)
+    return pl.pallas_call(
+        cols_kernel,
+        in_specs=[pl.BlockSpec(memory_space=pltpu.SMEM)] + [vmem] * 2,
+        out_specs=vmem,
+        out_shape=jax.ShapeDtypeStruct((slots, rows, width), jnp.bfloat16),
+        compiler_params=pltpu.CompilerParams(vmem_limit_bytes=24 * 2**20),
+        cost_estimate=SHORT,
+        name="cols_parts",
+    )(shard, back, unit_low)
+
+
+def unit_back_kernel(index_ref, back_ref, columns_ref, near_ref, other_ref):
+    steps, tok, _ = near_ref.shape
+    for step in range(steps):
+        lanes = [
+            back_ref[:, pl.ds(pl.multiple_of(index_ref[2 * step + c] * tok, tok), tok)]
+            for c in range(2)
+        ]
+        part = times_trans(jnp.concatenate(lanes, axis=1).T, columns_ref[...])
+        near_ref[step] = part[:tok]
+        other_ref[step] = part[tok:].astype(jnp.bfloat16)
+
+
+def unit_back(index, back, columns, tok):
+    steps = back.shape[1] // (2 * tok)
+    width = columns.shape[0]
+    vmem = pl.BlockSpec(memory_space=pltpu.VMEM)
+    return pl.pallas_call(
+        unit_back_kernel,
+        in_specs=[pl.BlockSpec(memory_space=pltpu.SMEM)] + [vmem] * 2,
+        out_specs=[vmem] * 2,
+        out_shape=[
+            jax.ShapeDtypeStruct((steps, tok, width), jnp.float32),
+            jax.ShapeDtypeStruct((steps, tok, width), jnp.bfloat16),
+        ],
+        compiler_params=pltpu.CompilerParams(vmem_limit_bytes=24 * 2**20),
+        cost_estimate=SHORT,
+        name="unit_back",
+    )(index, back, columns)
+
+
 def spread_kernel(place_ref, own_ref, one_ref, two_ref, out_ref):
-    steps, _, rows, _ = out_ref.shape
+    _, steps, rows, _ = out_ref.shape
     z, core = place_ref[0] // 2, place_ref[0] % 2
-    total = own_ref[...] + one_ref[...].astype(jnp.float32) + two_ref[...].astype(jnp.float32)
-    total = total.astype(jnp.bfloat16)
+    total = own_ref[...].astype(jnp.float32)
+    total += one_ref[...].astype(jnp.float32) + two_ref[...].astype(jnp.float32)
+    total = total.T.astype(jnp.bfloat16)
     for q in range(2 * steps):
-        out_ref[(q // 2 + steps - z) % steps, (core + q) % 2] = total[q * rows : (q + 1) * rows]
+        out_ref[(core + q) % 2, (q // 2 + steps - z) % steps] = total[q * rows : (q + 1) * rows]
 
 
 def spread_columns(place, own, one, two, steps):
-    rows, width = own.shape
+    columns, rows = own.shape
     vmem = pl.BlockSpec(memory_space=pltpu.VMEM)
     return pl.pallas_call(
         spread_kernel,
         in_specs=[pl.BlockSpec(memory_space=pltpu.SMEM)] + [vmem] * 3,
         out_specs=vmem,
-        out_shape=jax.ShapeDtypeStruct((steps, 2, rows // (2 * steps), width), jnp.bfloat16),
+        out_shape=jax.ShapeDtypeStruct((2, steps, rows // (2 * steps), columns), jnp.bfloat16),
         cost_estimate=SHORT,
         name="spread_columns",
     )(place, own, one, two)
 
 
-def unpack_kernel(heads, place_ref, gain_ref, query_ref, key_ref, value_ref, other_ref, *refs):
-    steps = other_ref.shape[0]
-    near, out_refs, cols_s = refs[:steps], refs[steps:-1], refs[-1]
+def pair_kernel(spread_ref, other_ref, *out_refs):
+    for step, out_ref in enumerate(out_refs):
+        out_ref[...] = jnp.concatenate([spread_ref[0, step], other_ref[step]])
+
+
+def pair_columns(spread, other):
+    steps, rows, columns = other.shape
+    vmem = pl.BlockSpec(memory_space=pltpu.VMEM)
+    return pl.pallas_call(
+        pair_kernel,
+        in_specs=[vmem] * 2,
+        out_specs=[vmem] * steps,
+        out_shape=[jax.ShapeDtypeStruct((2 * rows, columns), other.dtype)] * steps,
+        cost_estimate=SHORT,
+        name="pair_columns",
+    )(spread, other)
+
+
+def unpack_kernel(heads, place_ref, gain_ref, query_ref, key_ref, value_ref, *refs):
+    out_refs, cols_s = refs[-5:-1], refs[-1]
+    steps = len(refs) - 5
+    rows = query_ref.shape[0]
     seqs = 2 * steps
     z, core = place_ref[0] // 2, place_ref[0] % 2
     for step in range(steps):
-        cols_s[0, step] = near[step][0]
-    cols_s[1] = other_ref[...]
-    total = jnp.zeros((gain_ref.shape[0], 1), jnp.float32)
+        cols_s[0, step] = refs[step][:rows]
+        cols_s[1, step] = refs[step][rows:]
+    gain_col = as_column(gain_ref[...])
+    total = jnp.zeros((rows, 1), jnp.float32)
     for m, ref in enumerate((query_ref, key_ref, value_ref)):
-        rows = jnp.concatenate(
+        grads = jnp.concatenate(
             [
                 cols_s[
                     (core + head) % 2,
@@ -662,44 +739,48 @@
             ],
             axis=1,
         ).astype(jnp.float32)
-        total += jnp.sum(rows * ref[...].astype(jnp.float32), axis=1, keepdims=True)
-        out_refs[m][...] = rows * gain_ref[...]
-    out_refs[3][...] = total
-
-
-def unpack_columns(place, gain_col, weights, near, other):
+        total += jnp.sum(grads * ref[...].astype(jnp.float32), axis=1, keepdims=True)
+        out_refs[m][...] = grads * gain_col
+    out_refs[3][...] = jnp.broadcast_to(total, (rows, 128)).T[:8]
+
+
+def unpack_columns(place, gain_row, weights, cols):
     rows, width = weights[0].shape
     vmem = pl.BlockSpec(memory_space=pltpu.VMEM)
     return pl.pallas_call(
         functools.partial(unpack_kernel, width // HEAD_DIM),
-        in_specs=[pl.BlockSpec(memory_space=pltpu.SMEM)] + [vmem] * (5 + len(near)),
+        in_specs=[pl.BlockSpec(memory_space=pltpu.SMEM)] + [vmem] * (4 + len(cols)),
         out_specs=[vmem] * 4,
         out_shape=[jax.ShapeDtypeStruct((rows, width), jnp.float32)] * 3
-        + [jax.ShapeDtypeStruct((rows, 1), jnp.float32)],
-        scratch_shapes=[pltpu.VMEM((2,) + other.shape, other.dtype)],
+        + [jax.ShapeDtypeStruct((8, rows), jnp.float32)],
+        scratch_shapes=[pltpu.VMEM((2, len(cols), rows, cols[0].shape[1]), cols[0].dtype)],
         cost_estimate=SHORT,
         name="unpack_columns",
-    )(place, gain_col, *weights, other, *near)
-
-
-def unit_kernel(*refs):
+    )(place, gain_row, *weights, *cols)
+
+
+def unit_kernel(index_ref, *refs):
     out_ref = refs[-1]
     tok = refs[0].shape[0]
     for slot, ref in enumerate(refs[:-1]):
         rows = ref[...].astype(jnp.float32)
         scale = lax.rsqrt(jnp.mean(rows * rows, axis=-1, keepdims=True) + NORM_EPS)
-        out_ref[slot * tok : (slot + 1) * tok] = (rows * scale).astype(jnp.bfloat16)
-
-
-def unit_tokens(slots):
+        at = pl.ds(pl.multiple_of(index_ref[slot] * tok, tok), tok)
+        out_ref[at, :] = (rows * scale).astype(jnp.bfloat16)
+
+
+def unit_tokens(index, slots):
     tok, width = slots[0].shape
+    vmem = pl.BlockSpec(memory_space=pltpu.VMEM)
     return pl.pallas_call(
         unit_kernel,
+        in_specs=[pl.BlockSpec(memory_space=pltpu.SMEM)] + [vmem] * len(slots),
+        out_specs=vmem,
         out_shape=jax.ShapeDtypeStruct((len(slots) * tok, width), jnp.bfloat16),
         compiler_params=pltpu.CompilerParams(vmem_limit_bytes=16 * 2**20),
         cost_estimate=SHORT,
         name="unit_tokens",
-    )(*slots)
+    )(index, *slots)
 
 
 def join_kernel(*refs):
@@ -905,8 +986,7 @@
 def token_grad_kernel(
     index_ref, own_ref, one_ref, two_ref, three_ref, middle_ref, scale_ref, gain_ref, grad_ref, *refs
 ):
-    pieces, (middle_grad_ref, low_ref, out_ref, weight_s, sem) = refs[:-5], refs[-5:]
-    places = start_pieces(pieces, weight_s, sem)
+    weight_ref, middle_grad_ref, low_ref, out_ref = refs
     normed_grad = own_ref[...]
     for ref in (one_ref, two_ref, three_ref):
         normed_grad += ref[...].astype(jnp.float32)
@@ -922,9 +1002,9 @@
     low = middle_grad.astype(jnp.bfloat16)
     low_ref[...] = low
     grad_t = low.T
-    for row, size, copy in places:
-        copy.wait()
-        out = dot_nn(weight_s[row : row + size], grad_t).astype(jnp.bfloat16)
+    size = weight_ref.shape[1] // 8
+    for row in range(0, weight_ref.shape[1], size):
+        out = dot_nn(weight_ref[0, row : row + size], grad_t).astype(jnp.bfloat16)
         for i in range(size // HEAD_DIM):
             out_ref[index_ref[row // HEAD_DIM + i], :HEAD_DIM] = out[
                 i * HEAD_DIM : (i + 1) * HEAD_DIM
@@ -938,28 +1018,31 @@
         out_ref[head, HEAD_DIM:] = jnp.broadcast_to(row, (EXTRA, tok))
 
 
-def token_grad(index, sums, middle, scale, gain, output_grad, pieces):
+def token_grad(index, sums, middle, scale, gain, output_grad, weight):
     tok, width = middle.shape
     vmem = pl.BlockSpec(memory_space=pltpu.VMEM)
     return pl.pallas_call(
         token_grad_kernel,
         in_specs=[pl.BlockSpec(memory_space=pltpu.SMEM)]
-        + [vmem] * 8
-        + [pl.BlockSpec(memory_space=pl.ANY)] * len(pieces),
+        + [vmem] * 9,
         out_specs=[vmem] * 3,
         out_shape=[
             jax.ShapeDtypeStruct((tok, width), jnp.float32),
             jax.ShapeDtypeStruct((tok, width), jnp.bfloat16),
             pltpu.HBM((HEADS, HEAD_DIM + EXTRA, tok), jnp.bfloat16),
         ],
-        scratch_shapes=[
-            pltpu.VMEM((HEADS * HEAD_DIM, width), jnp.bfloat16),
-            pltpu.SemaphoreType.DMA((len(pieces),)),
-        ],
-        compiler_params=pltpu.CompilerParams(vmem_limit_bytes=18 * 2**20),
+        compiler_params=pltpu.CompilerParams(vmem_limit_bytes=20 * 2**20),
         cost_estimate=SHORT,
         name="token_grad",
-    )(index, *sums, middle, scale, gain, output_grad, *in_hbm(pieces))
+    )(
+        index,
+        *sums,
+        middle,
+        scale,
+        gain,
+        output_grad,
+        pltpu.with_memory_space_constraint(weight, pltpu.VMEM),
+    )
 
 
 def feed_wgrad_kernel(gate_ref, up_ref, hidden_ref, tokens_ref, grads_ref, out_ref):
@@ -973,38 +1056,44 @@
     units, tokens = hidden.shape
     width = feed_low.shape[1]
     block = units // shards
-    half = width // 2
+    cuts = 2
+    half = width // cuts
     rows = pl.BlockSpec((block, tokens), lambda c, i: (i, 0))
     every = pl.BlockSpec((tokens, half), lambda c, i: (0, c))
     return pl.pallas_call(
         feed_wgrad_kernel,
-        grid=(2, shards),
+        grid=(cuts, shards),
         in_specs=[rows] * 3 + [every] * 2,
         out_specs=pl.BlockSpec((1, 3, block, half), lambda c, i: (i, 0, 0, c)),
-        out_shape=jax.ShapeDtypeStruct((shards, 3, block, width), jnp.bfloat16),
+        out_shape=pltpu.HBM((shards, 3, block, width), jnp.bfloat16),
         compiler_params=pltpu.CompilerParams(vmem_limit_bytes=24 * 2**20),
         cost_estimate=SHORT,
         name="feed_wgrads",
     )(*in_hbm([gate_grad, up_grad, hidden, feed_low, span_grad]))
 
 
-def output_wgrad_kernel(blocks, *refs):
-    heads, grads, out_ref = refs[:4], refs[4 : 4 + blocks], refs[-1]
+def output_wgrad_kernel(index_ref, heads_ref, *refs):
+    grads, (out_ref, grads_s) = refs[:-2], refs[-2:]
     tok = grads[0].shape[0]
-    grad_rows = jnp.concatenate([ref[...] for ref in grads])
-    for k in range(4):
-        out_ref[k] = dot_nn(heads[k][...], grad_rows).astype(jnp.bfloat16)
-
-
-def output_wgrad_parts(heads, grads):
+    for slot, ref in enumerate(grads):
+        grads_s[pl.ds(pl.multiple_of(index_ref[slot] * tok, tok), tok), :] = ref[...]
+    for k in range(heads_ref.shape[0]):
+        out_ref[k] = dot_nn(heads_ref[k], grads_s[...]).astype(jnp.bfloat16)
+
+
+def output_wgrad_parts(index, heads, grads):
     tok, width = grads[0].shape
-    return pl.pallas_call(
-        functools.partial(output_wgrad_kernel, len(grads)),
-        out_shape=jax.ShapeDtypeStruct((4, HEAD_DIM, width), jnp.bfloat16),
-        compiler_params=pltpu.CompilerParams(vmem_limit_bytes=14 * 2**20),
+    vmem = pl.BlockSpec(memory_space=pltpu.VMEM)
+    return pl.pallas_call(
+        output_wgrad_kernel,
+        in_specs=[pl.BlockSpec(memory_space=pltpu.SMEM)] + [vmem] * (1 + len(grads)),
+        out_specs=vmem,
+        out_shape=jax.ShapeDtypeStruct((heads.shape[0], HEAD_DIM, width), jnp.bfloat16),
+        scratch_shapes=[pltpu.VMEM((len(grads) * tok, width), jnp.bfloat16)],
+        compiler_params=pltpu.CompilerParams(vmem_limit_bytes=18 * 2**20),
         cost_estimate=SHORT,
         name="output_wgrad",
-    )(*heads, *grads)
+    )(index, heads, *grads)
 
 
 def swap_cores(values):
@@ -1059,6 +1148,11 @@
     one = jnp.concatenate([one[:rows], one[rows:] + bottom.astype(F32)])
     two = jnp.concatenate([two[:rows] + top.astype(F32), two[rows:]])
     return from_shard(one.astype(BF16), 1), from_shard(two.astype(BF16), 2)
+
+
+def slot_block(slot, place, half):
+    z, core = place // 2, place % 2
+    return ((z + slot // 2) % half) * 2 + (core + slot) % 2
 
 
 def rotate_rows(front, back, cos_t, sin_t):
@@ -1086,9 +1180,8 @@
     half_head = HEAD_DIM // 2
     place = jnp.reshape(seq, (1,)).astype(jnp.int32)
 
-    lanes = jnp.arange(span, dtype=jnp.int32)
-    in_span = slot_block(lanes // tok, seq.astype(jnp.int32), seqs // 2) * tok + lanes % tok
-    positions = jnp.arange(shards, dtype=jnp.int32)[:, None] * span + in_span[None]
+    positions = jnp.arange(shards * span, dtype=jnp.int32).reshape(shards, span)
+    span_blocks = slot_block(jnp.arange(seqs, dtype=jnp.int32), seq.astype(jnp.int32), seqs // 2)
     bounds = doc_bounds(doc_lengths, positions)
     exponent = -2.0 * jnp.arange(half_head, dtype=jnp.float32) / HEAD_DIM
     inverse = jnp.power(jnp.float32(ROPE_BASE), exponent)
@@ -1100,13 +1193,13 @@
     steps = seqs // 2
     z, core = seq // 2, seq % 2
     shard_at = jnp.reshape(shard, (1,)).astype(jnp.int32)
-    gain_col = norm_gain.astype(F32)[:, None]
+    gain_row = norm_gain[None, :]
     heads_here = HEADS // seqs
     own_rows = query_weight.shape[0]
     attn_weights = (query_weight, key_weight, value_weight)
     slot = jnp.arange(HEADS, dtype=jnp.int32)
 
-    packed = pack_columns(place, gain_col, attn_weights, seqs)
+    packed = pack_columns(place, gain_row, attn_weights, seqs)
     point = join(jnp.zeros((), F32), packed)
     from_other = swap_cores(packed[1])
     gate_first = first_hops(after(point, gate_weight))
@@ -1114,17 +1207,19 @@
     for step in range(steps):
         block = jnp.concatenate([packed[0, step], from_other[step]])
         col_blocks.append(from_chip(block, -step) if step else block)
-    point = join(point, gate_first, col_blocks)
+    point = join(point, col_blocks)
     col_block = jnp.concatenate(after(point, col_blocks))
     col_first = first_hops(col_block)
     own_input = after(point, layer_input)
     input_one, input_three = from_chip(own_input, 1), from_chip(own_input, -1)
-    point = join(point, col_first, input_one, input_three)
+    point = join(point, col_first, input_one, input_three, gate_first)
     col_far = second_hops(after(point, col_first))
     input_two = from_chip(after(point, input_one), 1)
     input_slots = both_cores([own_input, after(point, input_one)])
     input_last = both_cores([after(point, input_three)])
-    point = join(point, col_far, input_two, input_slots, input_last)
+    output_own = after(point, output_weight)
+    output_three = from_chip(output_own, -1)
+    point = join(point, col_far, input_two, input_slots, input_last, output_three)
     input_slots += both_cores([after(point, input_two)]) + input_last
     rel_blocks = (
         (shard ^ (slot // seqs)) * seqs
@@ -1132,7 +1227,7 @@
         + (core ^ (slot % 2))
     ).astype(jnp.int32)
     columns = order_blocks([col_block] + col_first + after(point, col_far), rel_blocks, own_rows)
-    unit_low = unit_tokens(input_slots)
+    unit_low = unit_tokens(span_blocks, input_slots)
     qkv = lax.dot_general(
         columns, unit_low, (((0,), (1,)), ((), ())), preferred_element_type=F32
     ).reshape(shards, 3, HEAD_DIM, span)
@@ -1142,11 +1237,10 @@
     qkv_low = jnp.concatenate([turned, qkv[:, 2:]], axis=1).astype(BF16)
     qkv_low = qkv_low.reshape(shards, 3 * HEAD_DIM, span)
     gate_far = second_hops(after(point, gate_first))
-    output_own = after(point, output_weight)
-    output_one, output_three = from_chip(output_own, 1), from_chip(output_own, -1)
+    output_one = from_chip(after(point, output_weight), 1)
     up_top, up_bottom = up_weight[: up_weight.shape[0] // 2], up_weight[up_weight.shape[0] // 2 :]
     up_first = [from_shard(after(point, up_top), flip) for flip in (1, 2)]
-    point = join(point, qkv_low, gate_far, output_one, output_three, up_first)
+    point = join(point, qkv_low, gate_far, output_one, up_first)
 
     head_qkv = lax.all_to_all(
         after(point, qkv_low), "shard", split_axis=0, concat_axis=0, tiled=True
@@ -1162,18 +1256,18 @@
     grad_two, grad_three = from_chip(after(point, grad_one), 1), from_chip(own_grad, -1)
     gain_rows = jnp.pad(feed_gain[None, :], ((0, EXTRA - 1), (0, tok - own_rows)))
     head_out, head_low, out_blocks, lse = attend(
-        after(point, head_qkv), gain_rows, tok, place, bounds
+        after(point, head_qkv), gain_rows, tok, shard_at, bounds
     )
     point = join(point, out_blocks, output_first, output_swapped, grad_two, grad_three)
     token_blocks = lax.all_to_all(
         after(point, out_blocks), ("shard", "seq"), split_axis=0, concat_axis=0, tiled=True
     )
     output_far = second_hops(after(point, output_first))
-    up_far = [from_shard(after(point, up_first[0]), 2), from_shard(after(point, up_first[3]), 1)]
     output_swapped += [swap_cores(piece) for piece in after(point, output_first)]
-    point = join(point, token_blocks, output_far, up_far, output_swapped)
+    point = join(point, token_blocks, output_far, output_swapped)
     gain_two = token_blocks[:, HEAD_DIM, :own_rows].astype(F32).reshape(1, width)
     output_swapped += [swap_cores(piece) for piece in after(point, output_far)]
+    up_far = [from_shard(after(point, up_first[0]), 2), from_shard(after(point, up_first[3]), 1)]
     output_pieces = [output_own] + output_first + output_far + output_swapped
     rel_heads = (
         (shard ^ (slot // steps % shards)) * seqs
@@ -1183,7 +1277,7 @@
     middle, normed_two, scale_two = project(
         rel_heads, after(point, token_blocks), layer_input, gain_two, output_pieces
     )
-    point = join(point, normed_two)
+    point = join(point, normed_two, up_far)
 
     own_tokens = after(point, normed_two)
     tokens_one, tokens_three = from_chip(own_tokens, 1), from_chip(own_tokens, -1)
@@ -1199,8 +1293,9 @@
     tokens_two = from_chip(after(point, tokens_one), 1)
     down_far = second_hops(after(point, down_first))
     feed_slots = both_cores([own_tokens, after(point, tokens_one)])
+    output_here = load_weights([after(point, output_pieces)])
     feed_last = both_cores([after(point, tokens_three)])
-    point = join(point, tokens_two, down_far, feed_slots, feed_last)
+    point = join(point, tokens_two, down_far, feed_slots, feed_last, output_here)
     feed_slots += both_cores([after(point, tokens_two)]) + feed_last
     down_here = load_weights([[down_weight, *down_first, *after(point, down_far)]])
     order = (2, 1, 3, 0)
@@ -1217,30 +1312,25 @@
     arrived_two = from_chip(after(point, sum_two), -2)
     parts_one, whole = feed(1, after(point, feed_slots[2:4]), whole)
     parts_three, whole = feed(3, feed_slots[6:8], whole)
-    point = join(point, arrived_two, parts_one, parts_three)
+    parts_own, whole = feed(0, feed_slots[0:2], whole)
+    point = join(point, arrived_two, parts_one, parts_three, parts_own)
     sum_one = core_sum(*after(point, parts_one)).astype(BF16)
     sum_three = core_sum(*after(point, parts_three)).astype(BF16)
     point = join(point, sum_one, sum_three)
     arrived_one = from_chip(after(point, sum_one), -1)
     arrived_three = from_chip(after(point, sum_three), 1)
-    parts_own, whole = feed(0, after(point, feed_slots[0:2]), whole)
-    feed_low, span_grad, hidden, gate_grad, up_grad, down_near, down_other = whole
+    sum_own = core_sum(*after(point, parts_own))
+    feed_low, span_grad, hidden, gate_grad, up_grad, down_near, down_other = after(point, whole)
     feed_wparts = feed_wgrads(shards, gate_grad, up_grad, hidden, feed_low, span_grad)
-    head_slots = [
-        lax.dynamic_index_in_dim(after(point, head_low), shard ^ k, 0, keepdims=False)
-        for k in range(4)
-    ]
-    head_slots = head_slots[:1] + [from_shard(head_slots[k], k) for k in range(1, 4)]
-    point = join(point, parts_own, feed_wparts, arrived_one, arrived_three, head_slots)
-    sum_own = core_sum(*after(point, parts_own))
+    point = join(point, sum_own, feed_wparts, arrived_one, arrived_three)
     middle_grad, attend_grad, head_grad = token_grad(
         rel_heads,
-        [sum_own, arrived_one, arrived_two, arrived_three],
+        [sum_own, *after(point, [arrived_one, arrived_two, arrived_three])],
         middle,
         scale_two,
         gain_two,
         output_grad,
-        output_pieces,
+        output_here,
     )
     point = join(point, head_grad)
 
@@ -1254,14 +1344,15 @@
     agrad_one = from_chip(own_agrad, 1)
     down_all = core_sum(after(point, down_near), down_other).astype(BF16)
     down_sums = [down_all[order.index(step)] for step in range(steps)]
-    point = join(point, out_grad_blocks, agrad_one, down_sums)
-    agrad_three = from_chip(after(point, own_agrad), -1)
-    down_two = from_chip(after(point, down_sums[2]), -1)
+    head_slots = [head_low[0]] + [from_shard(after(point, head_low[k]), k) for k in range(1, 4)]
+    point = join(point, out_grad_blocks, agrad_one, down_sums, head_slots)
+    both = from_chip(jnp.concatenate([own_agrad, after(point, down_sums[2])]), -1)
     down_three = from_chip(after(point, down_sums[3]), 1)
     back = attend_back(
-        head_qkv, lse, head_out, after(point, out_grad_blocks), cos_all, sin_all, tok, place, bounds
-    )
-    point = join(point, back, agrad_three, down_two, down_three)
+        head_qkv, lse, head_out, after(point, out_grad_blocks), cos_all, sin_all, tok, bounds
+    )
+    point = join(point, back, both, down_three)
+    agrad_three, down_two = both[:tok], both[tok:]
     span_back = lax.all_to_all(
         after(point, back), "shard", split_axis=0, concat_axis=0, tiled=True
     ).reshape(heads_here * 3 * HEAD_DIM, span)
@@ -1270,44 +1361,43 @@
         (down_sums[1].astype(F32) + after(point, down_two).astype(F32)).astype(BF16), -1
     )
     agrad_slots = both_cores([after(point, own_agrad), agrad_one, agrad_two, agrad_three])
-    out_part = output_wgrad_parts(head_slots, agrad_slots)
-    point = join(point, span_back, down_one, out_part)
+    out_part = output_wgrad_parts(span_blocks, jnp.stack(head_slots), agrad_slots)
+    out_parts = [out_part[k] for k in range(4)]
+    out_first = scatter_shard_first(out_parts)
+    point = join(point, span_back, down_one, out_first)
+
+    span_back = after(point, span_back)
+    cols_part = cols_parts_of(shard_at, span_back, unit_low, shards)
+    point = join(point, cols_part)
+    cols_parts = [after(point, cols_part)[k] for k in range(4)]
+    cols_first = scatter_shard_first(cols_parts)
+    unit_near, unit_other = unit_back(span_blocks, after(point, span_back), columns, tok)
+    unit_swapped = swap_cores(unit_other)
+    point = join(point, unit_near, unit_swapped)
+    unit_sums = unit_near + after(point, unit_swapped).astype(F32)
+    unit_two = from_chip(unit_sums[2].astype(BF16), -1)
+    unit_three = from_chip(unit_sums[3].astype(BF16), 1)
+    out_last = scatter_shard_last(out_parts, after(point, out_first))
     layer_output = (
         middle
         + down_sums[0].astype(F32)
         + after(point, down_one).astype(F32)
         + down_three.astype(F32)
     ).astype(BF16)
-
-    span_back = after(point, span_back)
-    cols_part = lax.dot_general(
-        unit_low, span_back, (((0,), (1,)), ((), ())), preferred_element_type=F32
-    ).reshape(shards, seqs * own_rows, heads_here * 3 * HEAD_DIM)
-    cols_parts = [
-        lax.dynamic_index_in_dim(cols_part, shard ^ k, 0, keepdims=False) for k in range(4)
-    ]
-    cols_first = scatter_shard_first(cols_parts)
-    unit_sums = []
-    for step in range(steps):
-        lanes_here = after(cols_part, span_back)[:, 2 * step * tok : 2 * (step + 1) * tok]
-        part = lax.dot_general(
-            lanes_here, columns, (((0,), (1,)), ((), ())), preferred_element_type=F32
-        )
-        unit_sums.append(core_sum(part[:tok], part[tok:]))
-    point = join(point, cols_first, unit_sums, layer_output)
-    unit_two = from_chip(after(point, unit_sums[2]).astype(BF16), -1)
-    unit_three = from_chip(after(point, unit_sums[3]).astype(BF16), 1)
+    point, layer_output = lax.optimization_barrier(
+        (join(point, unit_two, unit_three, cols_first, out_last), layer_output)
+    )
+    unit_one = from_chip((unit_sums[1] + after(point, unit_two).astype(F32)).astype(BF16), -1)
     cols_last = scatter_shard_last(cols_parts, after(point, cols_first))
-    point = join(point, unit_two, unit_three, cols_last)
-    unit_one = from_chip((unit_sums[1] + after(point, unit_two).astype(F32)).astype(BF16), -1)
-    out_parts = [after(point, out_part)[k] for k in range(4)]
-    out_first = scatter_shard_first(out_parts)
+    point = join(point, unit_one, cols_last)
     cols_spread = spread_columns(place, cols_parts[0], *after(point, cols_last), steps)
-    point = join(point, unit_one, cols_spread, out_first)
-    cols_same = [cols_spread[0]] + [
-        from_chip(after(point, cols_spread)[step], -step) for step in range(1, steps)
-    ]
-    out_last = scatter_shard_last(out_parts, after(point, out_first))
+    cols_other = swap_cores(cols_spread[1])
+    cols_blocks = pair_columns(cols_spread, cols_other)
+    point = join(point, cols_blocks)
+    cols_same = list(after(point, cols_blocks))
+    cols_same = cols_same[:1] + [from_chip(cols_same[step], -step) for step in range(1, steps)]
+    out_one, out_two = after(point, out_last)
+    output_wgrad = out_parts[0].astype(F32) + out_one.astype(F32) + out_two.astype(F32)
     unit_grad = unit_sums[0] + after(point, unit_one).astype(F32) + unit_three.astype(F32)
     inputs = layer_input.astype(F32)
     scale_one = lax.rsqrt(jnp.mean(inputs * inputs, axis=-1, keepdims=True) + NORM_EPS)
@@ -1323,20 +1413,21 @@
     gain_two_out = jnp.sum(
         gain_rows_back[:, :own_rows] + gain_rows_back[:, own_rows : 2 * own_rows], axis=0
     )
-    point = join(
-        point, cols_same, out_last, input_grad, gate_wgrad, up_wgrad, down_wgrad, gain_two_out
-    )
-    cols_same = after(point, cols_same)
-    cols_other = swap_cores(jnp.stack([block[1] for block in cols_same]))
+    point, output_wgrad, input_grad, gate_wgrad, up_wgrad, down_wgrad, gain_two_out, cols_same = (
+        lax.optimization_barrier(
+            (
+                *(point, output_wgrad, input_grad, gate_wgrad, up_wgrad, down_wgrad, gain_two_out),
+                cols_same,
+            )
+        )
+    )
     query_wgrad, key_wgrad, value_wgrad, gain_one_out = unpack_columns(
-        place, gain_col, attn_weights, cols_same, cols_other
-    )
-    out_one, out_two = after(point, out_last)
-    output_wgrad = out_parts[0].astype(F32) + out_one.astype(F32) + out_two.astype(F32)
+        place, gain_row, attn_weights, after(point, cols_same)
+    )
     return (
         layer_output,
         input_grad,
-        gain_one_out.reshape(-1),
+        gain_one_out[0],
         query_wgrad,
         key_wgrad,
         value_wgrad,

time: 622 us -> 571 us (0.918)
  the two profiles are of different devices: /device:TPU:1 before, /device:TPU:8 now
where the time goes in v3:
time: 571 us; the launch traced here: 561 us
  waiting for transfers between devices  230 us (40%)
  Pallas kernels  151 us (26%)
  starting transfers between devices  93.1 us (16%)
  local copies, waits for them, and re-layouts  38 us (7%)
  other arithmetic  30.2 us (5%)
  between operations  15.4 us (3%)
    ppermute x29, waiting for transfers between devices, from_chip(): lax.ppermute(values, 'seq', [((i + 2 * step) % count, i) for i in range(c...  116 us
    ppermute x33, waiting for transfers between devices, from_shard(): return lax.ppermute(values, 'shard', [(i, i ^ flip) for i in range(4)])  105 us
    ppermute x33, starting transfers between devices, from_shard(): return lax.ppermute(values, 'shard', [(i, i ^ flip) for i in range(4)])  39.3 us
    pallas_call x4, Pallas kernels, feed_blocks(): pl.pallas_call(functools.partial(feed_kernel, call, len(whole)), in_specs...  35.6 us
    ppermute x29, starting transfers between devices, from_chip(): lax.ppermute(values, 'seq', [((i + 2 * step) % count, i) for i in range(c...  33.8 us
    pallas_call x1, Pallas kernels, attend_back(): pl.pallas_call(functools.partial(bwd_kernel, tok), grid=(spans,), in_spec...  30.1 us
    pallas_call x1, Pallas kernels, feed_wgrads(): pl.pallas_call(feed_wgrad_kernel, grid=(cuts, shards), in_specs=[rows] *...  20.7 us
    pallas_call x1, Pallas kernels, attend(): pl.pallas_call(functools.partial(fwd_kernel, tok), grid=(spans,), in_spec...  19.9 us
  transfers between devices with their start and end apart: 96, of which 45 were waited for; matrix products, arithmetic and copies ran while one was open for 10% of the time, Pallas kernels for 24%

profile of v3, /device:TPU:8, one launch (start us, length us, event | category | flops | bytes accessed | tf_op | source)
XLA Modules:
  0.0 561.1 jit_solution(343980074395519290)
XLA Ops:
  19.9 8.8 %collective-permute-done.1 = bf16[128,768]{1,0:T(8,128)(2,1)S(1)} collective-permute-done((bf16[128,768]{1,0:T(8,128)(2,1)S(1)}, bf16[128,768]{1,0:T(8,128)(2,1)S(1)}, u32[]{:S(2)}, u32[]{:S(2)}) %collective-permute-start.1) | collective-permute-done | bytes 196640 | tf_op jit(solution)/shard_map/ppermute | solution.py:1106
  44.7 7.3 %collective-permute-done.7.refs_6_ = bf16[128,2048]{1,0:T(8,128)(2,1)S(1)} collective-permute-done((bf16[128,2048]{1,0:T(8,128)(2,1)S(1)}, bf16[128,2048]{1,0:T(8,128)(2,1)S(1)}, u32[]{:S(2)}, u32[]{:S(2)}) %collective-permute-start.7) | collective-permute-done | bytes 524320 | tf_op jit(solution)/shard_map/ppermute | solution.py:1106
  52.0 8.8 %collective-permute-done.6.refs_2_ = bf16[128,2048]{1,0:T(8,128)(2,1)S(1)} collective-permute-done((bf16[128,2048]{1,0:T(8,128)(2,1)S(1)}, bf16[128,2048]{1,0:T(8,128)(2,1)S(1)}, u32[]{:S(2)}, u32[]{:S(2)}) %collective-permute-start.6) | collective-permute-done | bytes 524320 | tf_op jit(solution)/shard_map/ppermute | solution.py:1106
  123.0 16.3 %collective-permute-done.23 = bf16[64,2048]{1,0:T(8,128)(2,1)S(1)} collective-permute-done((bf16[64,2048]{1,0:T(8,128)(2,1)}, bf16[64,2048]{1,0:T(8,128)(2,1)S(1)}, u32[]{:S(2)}, u32[]{:S(2)}) %collective-permute-start.23) | collective-permute-done | bytes 262176 | tf_op jit(solution)/shard_map/ppermute | solution.py:1106
  139.3 6.2 %collective-permute-done.26.refs_9_ = bf16[128,2048]{1,0:T(8,128)(2,1)} collective-permute-done((bf16[128,2048]{1,0:T(8,128)(2,1)}, bf16[128,2048]{1,0:T(8,128)(2,1)}, u32[]{:S(2)}, u32[]{:S(2)}) %collective-permute-start.26) | collective-permute-done | bytes 524320 | tf_op jit(solution)/shard_map/ppermute | solution.py:1110
  152.1 19.9 %attend.1 = (f32[4,64,1024]{2,1,0:T(8,128)}, bf16[4,64,1024]{2,1,0:T(8,128)(2,1)}, bf16[32,80,128]{2,1,0:T(8,128)(2,1)}, f32[4,1,1024]{2,1,0:T(1,128)S(1)}) custom-call(s32[1]{0:T(128)} %bitcast.19.shard_ref.refs_0_, s32[4]{0:T(128)S(1)} %and_select_fusion.7.lo_ref, s32[4]{0:T(128)S(1)} %iota_minimum_fusion.full_ref, ...), custom_call_target="tpu_custom_call" | custom-call | flops 21474836480 | bytes 4194304 | tf_op jit(solution)/shard_map/attend/pallas_call | solution.py:497
  185.0 15.2 %collective-permute-done.33.refs_4_ = bf16[128,2048]{1,0:T(8,128)(2,1)S(1)} collective-permute-done((bf16[128,2048]{1,0:T(8,128)(2,1)S(1)}, bf16[128,2048]{1,0:T(8,128)(2,1)S(1)}, u32[]{:S(2)}, u32[]{:S(2)}) %collective-permute-start.33) | collective-permute-done | bytes 524320 | tf_op jit(solution)/shard_map/ppermute | solution.py:1110
  209.3 6.9 %collective-permute-done.38.refs_10_ = bf16[128,2048]{1,0:T(8,128)(2,1)} collective-permute-done((bf16[128,2048]{1,0:T(8,128)(2,1)}, bf16[128,2048]{1,0:T(8,128)(2,1)}, u32[]{:S(2)}, u32[]{:S(2)}) %collective-permute-start.38) | collective-permute-done | bytes 524320 | tf_op jit(solution)/shard_map/ppermute | solution.py:1110
  221.4 10.7 %collective-permute-done.41.refs_1_ = bf16[128,2048]{1,0:T(8,128)(2,1)S(1)} collective-permute-done((bf16[128,2048]{1,0:T(8,128)(2,1)S(1)}, bf16[128,2048]{1,0:T(8,128)(2,1)S(1)}, u32[]{:S(2)}, u32[]{:S(2)}) %collective-permute-start.41) | collective-permute-done | bytes 524320 | tf_op jit(solution)/shard_map/ppermute | solution.py:1106
  232.2 10.0 %collective-permute-done.40.refs_1_ = bf16[128,2048]{1,0:T(8,128)(2,1)S(1)} collective-permute-done((bf16[128,2048]{1,0:T(8,128)(2,1)S(1)}, bf16[128,2048]{1,0:T(8,128)(2,1)S(1)}, u32[]{:S(2)}, u32[]{:S(2)}) %collective-permute-start.40) | collective-permute-done | bytes 524320 | tf_op jit(solution)/shard_map/ppermute | solution.py:1106
  254.1 8.5 %collective-permute-done.50.refs_4_ = bf16[128,2048]{1,0:T(8,128)(2,1)S(1)} collective-permute-done((bf16[128,2048]{1,0:T(8,128)(2,1)S(1)}, bf16[128,2048]{1,0:T(8,128)(2,1)S(1)}, u32[]{:S(2)}, u32[]{:S(2)}) %collective-permute-start.50) | collective-permute-done | bytes 524320 | tf_op jit(solution)/shard_map/ppermute | solution.py:1110
  266.0 8.5 %feed_blocks.4 = (f32[128,2048]{1,0:T(8,128)S(1)}, bf16[128,2048]{1,0:T(8,128)(2,1)S(1)}, bf16[1024,2048]{1,0:T(8,128)(2,1)}, bf16[1024,2048]{1,0:T(8,128)(2,1)}...) custom-call(s32[1]{0:T(128)} %bitcast.19.shard_ref.refs_0_, ...), custom_call_target="tpu_custom_call" | custom-call | tf_op jit(solution)/shard_map/feed_blocks/pallas_call | solution.py:912
  278.4 8.9 %feed_blocks.5 = (f32[128,2048]{1,0:T(8,128)S(1)}, bf16[128,2048]{1,0:T(8,128)(2,1)S(1)}, bf16[1024,2048]{1,0:T(8,128)(2,1)}, bf16[1024,2048]{1,0:T(8,128)(2,1)}...) custom-call(s32[1]{0:T(128)} %bitcast.19.shard_ref.refs_0_, ...), custom_call_target="tpu_custom_call", output_to_operand_aliasing={{2}: (7, {}), {3}: (8, {}), {4}: (9, {}), {5}: (10, {}), {6... | custom-call | tf_op jit(solution)/shard_map/feed_blocks/pallas_call | solution.py:912
  287.3 9.5 %feed_blocks.6 = (f32[128,2048]{1,0:T(8,128)S(1)}, bf16[128,2048]{1,0:T(8,128)(2,1)S(1)}, bf16[1024,2048]{1,0:T(8,128)(2,1)}, bf16[1024,2048]{1,0:T(8,128)(2,1)}...) custom-call(s32[1]{0:T(128)} %bitcast.19.shard_ref.refs_0_, ...), custom_call_target="tpu_custom_call", output_to_operand_aliasing={{2}: (7, {}), {3}: (8, {}), {4}: (9, {}), {5}: (10, {}), {6... | custom-call | tf_op jit(solution)/shard_map/feed_blocks/pallas_call | solution.py:912
  296.9 8.7 %feed_blocks.7 = (f32[128,2048]{1,0:T(8,128)S(1)}, bf16[128,2048]{1,0:T(8,128)(2,1)S(1)}, bf16[1024,2048]{1,0:T(8,128)(2,1)}, bf16[1024,2048]{1,0:T(8,128)(2,1)}...) custom-call(s32[1]{0:T(128)} %bitcast.19.shard_ref.refs_0_, ...), custom_call_target="tpu_custom_call", output_to_operand_aliasing={{2}: (7, {}), {3}: (8, {}), {4}: (9, {}), {5}: (10, {}), {6... | custom-call | tf_op jit(solution)/shard_map/feed_blocks/pallas_call | solution.py:912
  310.7 20.7 %feed_wgrads.1 = bf16[4,3,256,2048]{3,2,1,0:T(8,128)(2,1)} custom-call(bf16[1024,1024]{1,0:T(8,128)(2,1)} %get-tuple-element.351.gate_ref, bf16[1024,1024]{1,0:T(8,128)(2,1)} %get-tuple-element.352.up_ref, bf16[1024,1024]{1,0:T(8,128)(2,1)} %get-tuple-element.353.hidden_ref, bf16[1024,2048]{1,0:T(8,128)(2,1)} %get-tuple-element.354.tokens_ref, ...), custom_call_target="tpu_custom_call" | custom-call | tf_op jit(solution)/shard_map/feed_wgrads/pallas_call | solution.py:1063
  352.8 9.1 %collective-permute-done.64 = bf16[64,1024]{1,0:T(8,128)(2,1)S(1)} collective-permute-done((bf16[64,1024]{1,0:T(8,128)(2,1)S(1)}, bf16[64,1024]{1,0:T(8,128)(2,1)S(1)}, u32[]{:S(2)}, u32[]{:S(2)}) %collective-permute-start.64) | collective-permute-done | bytes 131104 | tf_op jit(solution)/shard_map/ppermute | solution.py:1110
  361.8 6.0 %collective-permute-done.66 = bf16[64,1024]{1,0:T(8,128)(2,1)S(1)} collective-permute-done((bf16[64,1024]{1,0:T(8,128)(2,1)S(1)}, bf16[64,1024]{1,0:T(8,128)(2,1)S(1)}, u32[]{:S(2)}, u32[]{:S(2)}) %collective-permute-start.66) | collective-permute-done | bytes 131104 | tf_op jit(solution)/shard_map/ppermute | solution.py:1110
  376.0 30.1 %attend_back.1 = bf16[4,192,1024]{2,1,0:T(8,128)(2,1)} custom-call(s32[4]{0:T(128)S(1)} %and_select_fusion.hi_ref, s32[4]{0:T(128)S(1)} %iota_minimum_fusion.full_ref, s32[4,1,1024]{2,1,0:T(1,128)S(1)} %broadcast_in_dim.40.start_ref, bf16[4,192,1024]{2,1,0:T(8,128)(2,1)S(1)} %copy-done.17, f32[4,1,1024]{2,1,0:T(1,128)S(1)} %get-tuple-element.377.lse_ref, ...), custom_call_target="tpu_custom_call" | custom-call | flops 30064771072 | bytes 4194304 | tf_op jit(solution)/shard_map/attend_back/pallas_call | solution.py:537
  416.6 7.9 %collective-permute-done.72.refs_4_ = bf16[128,2048]{1,0:T(8,128)(2,1)S(1)} collective-permute-done((bf16[128,2048]{1,0:T(8,128)(2,1)}, bf16[128,2048]{1,0:T(8,128)(2,1)S(1)}, u32[]{:S(2)}, u32[]{:S(2)}) %collective-permute-start.72) | collective-permute-done | bytes 524320 | tf_op jit(solution)/shard_map/ppermute | solution.py:1106
  466.0 11.6 %collective-permute-done.81 = bf16[384,512]{1,0:T(8,128)(2,1)S(1)} collective-permute-done((bf16[384,512]{1,0:T(8,128)(2,1)S(1)}, bf16[384,512]{1,0:T(8,128)(2,1)S(1)}, u32[]{:S(2)}, u32[]{:S(2)}) %collective-permute-start.81) | collective-permute-done | bytes 393248 | tf_op jit(solution)/shard_map/ppermute | solution.py:1110
  481.4 8.6 %collective-permute-done.82 = bf16[64,2048]{1,0:T(8,128)(2,1)S(1)} collective-permute-done((bf16[64,2048]{1,0:T(8,128)(2,1)S(1)}, bf16[64,2048]{1,0:T(8,128)(2,1)S(1)}, u32[]{:S(2)}, u32[]{:S(2)}) %collective-permute-start.82) | collective-permute-done | bytes 262176 | tf_op jit(solution)/shard_map/ppermute | solution.py:1110
  497.3 10.0 %collective-permute-done.84 = bf16[128,2048]{1,0:T(8,128)(2,1)S(1)} collective-permute-done((bf16[128,2048]{1,0:T(8,128)(2,1)S(1)}, bf16[128,2048]{1,0:T(8,128)(2,1)S(1)}, u32[]{:S(2)}, u32[]{:S(2)}) %collective-permute-start.84) | collective-permute-done | bytes 524320 | tf_op jit(solution)/shard_map/ppermute | solution.py:1106
  507.2 11.6 %collective-permute-done.85.one_ref = bf16[768,512]{1,0:T(8,128)(2,1)S(1)} collective-permute-done((bf16[768,512]{1,0:T(8,128)(2,1)S(1)}, bf16[768,512]{1,0:T(8,128)(2,1)S(1)}, u32[]{:S(2)}, u32[]{:S(2)}) %collective-permute-start.85) | collective-permute-done | bytes 786464 | tf_op jit(solution)/shard_map/ppermute | solution.py:1110
  (423 shorter events, 275.7 us)
Async XLA Ops:
  10.9 26.3 %collective-permute-start.9 = (bf16[256,2048]{1,0:T(8,128)(2,1)}, bf16[256,2048]{1,0:T(8,128)(2,1)S(1)}, u32[]{:S(2)}, u32[]{:S(2)}) collective-permute-start(bf16[256,2048]{1,0:T(8,128)(2,1)} %refs_0_.2), channel_id=1, source_target_pairs={{0,16},{8,24},{16,0},{24,8},{1,17},{9,25},{17,1},{25,9},{2,18},{10... | collective-permute-start | bytes 3145736 | tf_op jit(solution)/shard_map/ppermute | solution.py:1110
  18.4 26.3 %collective-permute-start.8 = (bf16[256,2048]{1,0:T(8,128)(2,1)}, bf16[256,2048]{1,0:T(8,128)(2,1)S(1)}, u32[]{:S(2)}, u32[]{:S(2)}) collective-permute-start(bf16[256,2048]{1,0:T(8,128)(2,1)} %refs_0_.2), channel_id=1, source_target_pairs={{0,8},{8,0},{16,24},{24,16},{1,9},{9,1},{17,25},{25,17},{2,10},{10... | collective-permute-start | bytes 3145736 | tf_op jit(solution)/shard_map/ppermute | solution.py:1110
  34.2 26.6 %collective-permute-start.5 = (bf16[512,768]{1,0:T(8,128)(2,1)S(1)}, bf16[512,768]{1,0:T(8,128)(2,1)S(1)}, u32[]{:S(2)}, u32[]{:S(2)}) collective-permute-start(bf16[512,768]{1,0:T(8,128)(2,1)S(1)} %constant_dynamic-update-slice_fusion.refs_0_), channel_id=1, source_target_pairs={{0,16},{8,24},{16,0},{24,8},{1,17},{9,25},{17,1},{25,9},{2,18},{10... | collective-permute-start | bytes 2359304 | tf_op jit(solution)/shard_map/ppermute | solution.py:1110
  34.8 26.1 %collective-permute-start.4 = (bf16[512,768]{1,0:T(8,128)(2,1)S(1)}, bf16[512,768]{1,0:T(8,128)(2,1)S(1)}, u32[]{:S(2)}, u32[]{:S(2)}) collective-permute-start(bf16[512,768]{1,0:T(8,128)(2,1)S(1)} %constant_dynamic-update-slice_fusion.refs_0_), channel_id=1, source_target_pairs={{0,8},{8,0},{16,24},{24,16},{1,9},{9,1},{17,25},{25,17},{2,10},{10... | collective-permute-start | bytes 2359304 | tf_op jit(solution)/shard_map/ppermute | solution.py:1110
  83.8 27.1 %collective-permute-start.22 = (bf16[128,2048]{1,0:T(8,128)(2,1)}, bf16[128,2048]{1,0:T(8,128)(2,1)}, u32[]{:S(2)}, u32[]{:S(2)}) collective-permute-start(bf16[128,2048]{1,0:T(8,128)(2,1)} %get-tuple-element.247), channel_id=1, source_target_pairs={{0,16},{8,24},{16,0},{24,8},{1,17},{9,25},{17,1},{25,9},{2,18},{10... | collective-permute-start | bytes 1572872 | tf_op jit(solution)/shard_map/ppermute | solution.py:1110
  85.4 25.5 %collective-permute-start.21 = (bf16[128,2048]{1,0:T(8,128)(2,1)}, bf16[128,2048]{1,0:T(8,128)(2,1)}, u32[]{:S(2)}, u32[]{:S(2)}) collective-permute-start(bf16[128,2048]{1,0:T(8,128)(2,1)} %get-tuple-element.247), channel_id=1, source_target_pairs={{0,8},{8,0},{16,24},{24,16},{1,9},{9,1},{17,25},{25,17},{2,10},{10... | collective-permute-start | bytes 1572872 | tf_op jit(solution)/shard_map/ppermute | solution.py:1110
  111.7 33.9 %all-to-all-start = ((bf16[4,192,1024]{2,1,0:T(8,128)(2,1)}), bf16[4,192,1024]{2,1,0:T(8,128)(2,1)S(1)}, u32[]{:S(2)}, u32[]{:S(2)}) async-start(bf16[4,192,1024]{2,1,0:T(8,128)(2,1)} %bitcast.140), calls=%async_computation | async-start | bytes 3145728 | tf_op jit(solution)/shard_map/all_to_all | solution.py:1245
  115.5 30.0 %collective-permute-start.26 = (bf16[128,2048]{1,0:T(8,128)(2,1)}, bf16[128,2048]{1,0:T(8,128)(2,1)}, u32[]{:S(2)}, u32[]{:S(2)}) collective-permute-start(bf16[128,2048]{1,0:T(8,128)(2,1)} %get-tuple-element.252), channel_id=1, source_target_pairs={{0,16},{8,24},{16,0},{24,8},{1,17},{9,25},{17,1},{25,9},{2,18},{10... | collective-permute-start | bytes 1572872 | tf_op jit(solution)/shard_map/ppermute | solution.py:1110
  117.6 28.0 %collective-permute-start.25 = (bf16[128,2048]{1,0:T(8,128)(2,1)}, bf16[128,2048]{1,0:T(8,128)(2,1)}, u32[]{:S(2)}, u32[]{:S(2)}) collective-permute-start(bf16[128,2048]{1,0:T(8,128)(2,1)} %get-tuple-element.252), channel_id=1, source_target_pairs={{0,8},{8,0},{16,24},{24,16},{1,9},{9,1},{17,25},{25,17},{2,10},{10... | collective-permute-start | bytes 1572872 | tf_op jit(solution)/shard_map/ppermute | solution.py:1110
  121.5 50.5 %collective-permute-start.31 = (bf16[128,2048]{1,0:T(8,128)(2,1)S(1)}, bf16[128,2048]{1,0:T(8,128)(2,1)}, u32[]{:S(2)}, u32[]{:S(2)}) collective-permute-start(bf16[128,2048]{1,0:T(8,128)(2,1)S(1)} %copy-done.9), channel_id=1, source_target_pairs={{6,0},{7,1},{0,2},{1,3},{2,4},{3,5},{4,6},{5,7},{14,8},{15,9},{8,1... | collective-permute-start | bytes 1572872 | tf_op jit(solution)/shard_map/ppermute | solution.py:1106
  148.8 25.7 %collective-permute-start.28 = (bf16[256,2048]{1,0:T(8,128)(2,1)S(1)}, bf16[256,2048]{1,0:T(8,128)(2,1)}, u32[]{:S(2)}, u32[]{:S(2)}) collective-permute-start(bf16[256,2048]{1,0:T(8,128)(2,1)S(1)} %constant_dynamic-update-slice_fusion.4.refs_0_), channel_id=1, source_target_pairs={{0,16},{8,24},{16,0},{24,8},{1,17},{9,25},{17,1},{25,9},{2,18},{10... | collective-permute-start | bytes 3145736 | tf_op jit(solution)/shard_map/ppermute | solution.py:1110
  175.7 25.8 %all-to-all-start.1 = ((bf16[32,80,128]{2,1,0:T(8,128)(2,1)}), bf16[32,80,128]{2,1,0:T(8,128)(2,1)S(1)}, u32[]{:S(2)}, u32[]{:S(2)}) async-start(bf16[32,80,128]{2,1,0:T(8,128)(2,1)} %get-tuple-element.262), calls=%async_computation.1 | async-start | bytes 1310720 | tf_op jit(solution)/shard_map/all_to_all | solution.py:1262
  179.2 359.6 %reduce-scatter.2.cloned.1.call-start = ((), (), s32[]{:S(2)}) async-start(), calls=%async_computation.5 | async-start | bytes 15728640 | tf_op jit(solution)/shard_map/reduce_scatter | solution.py:1340
  219.3 27.0 %collective-permute-start.43 = (bf16[256,2048]{1,0:T(8,128)(2,1)S(1)}, bf16[256,2048]{1,0:T(8,128)(2,1)S(1)}, u32[]{:S(2)}, u32[]{:S(2)}) collective-permute-start(bf16[256,2048]{1,0:T(8,128)(2,1)S(1)} %copy-done.50), channel_id=1, source_target_pairs={{0,16},{8,24},{16,0},{24,8},{1,17},{9,25},{17,1},{25,9},{2,18},{10... | collective-permute-start | bytes 3145736 | tf_op jit(solution)/shard_map/ppermute | solution.py:1110
  220.0 26.3 %collective-permute-start.42 = (bf16[256,2048]{1,0:T(8,128)(2,1)S(1)}, bf16[256,2048]{1,0:T(8,128)(2,1)S(1)}, u32[]{:S(2)}, u32[]{:S(2)}) collective-permute-start(bf16[256,2048]{1,0:T(8,128)(2,1)S(1)} %copy-done.50), channel_id=1, source_target_pairs={{0,8},{8,0},{16,24},{24,16},{1,9},{9,1},{17,25},{25,17},{2,10},{10... | collective-permute-start | bytes 3145736 | tf_op jit(solution)/shard_map/ppermute | solution.py:1110
  276.6 29.0 %collective-permute-start.56 = (bf16[128,2048]{1,0:T(8,128)(2,1)S(1)}, bf16[128,2048]{1,0:T(8,128)(2,1)S(1)}, u32[]{:S(2)}, u32[]{:S(2)}) collective-permute-start(bf16[128,2048]{1,0:T(8,128)(2,1)S(1)} %add_convert_fusion.5), channel_id=1, source_target_pairs={{4,0},{5,1},{6,2},{7,3},{0,4},{1,5},{2,6},{3,7},{12,8},{13,9},{14,... | collective-permute-start | bytes 1572872 | tf_op jit(solution)/shard_map/ppermute | solution.py:1106
  340.4 32.3 %all-to-all-start.2 = ((bf16[32,80,128]{2,1,0:T(8,128)(2,1)}), bf16[32,80,128]{2,1,0:T(8,128)(2,1)S(1)}, u32[]{:S(2)}, u32[]{:S(2)}) async-start(bf16[32,80,128]{2,1,0:T(8,128)(2,1)} %get-tuple-element.366), calls=%async_computation.2 | async-start | bytes 1310720 | tf_op jit(solution)/shard_map/all_to_all | solution.py:1337
  372.8 33.3 %collective-permute-start.68 = (bf16[128,2048]{1,0:T(8,128)(2,1)}, bf16[128,2048]{1,0:T(8,128)(2,1)S(1)}, u32[]{:S(2)}, u32[]{:S(2)}) collective-permute-start(bf16[128,2048]{1,0:T(8,128)(2,1)} %get-tuple-element.381), channel_id=1, source_target_pairs={{2,0},{3,1},{4,2},{5,3},{6,4},{7,5},{0,6},{1,7},{10,8},{11,9},{12,... | collective-permute-start | bytes 1572872 | tf_op jit(solution)/shard_map/ppermute | solution.py:1106
  374.1 36.5 %collective-permute-start.67 = (bf16[256,2048]{1,0:T(8,128)(2,1)S(1)}, bf16[256,2048]{1,0:T(8,128)(2,1)}, u32[]{:S(2)}, u32[]{:S(2)}) collective-permute-start(bf16[256,2048]{1,0:T(8,128)(2,1)S(1)} %pad_maximum_fusion.1), channel_id=1, source_target_pairs={{6,0},{7,1},{0,2},{1,3},{2,4},{3,5},{4,6},{5,7},{14,8},{15,9},{8,1... | collective-permute-start | bytes 3145736 | tf_op jit(solution)/shard_map/ppermute | solution.py:1106
  411.0 33.4 %all-to-all-start.3 = ((bf16[4,192,1024]{2,1,0:T(8,128)(2,1)}), bf16[4,192,1024]{2,1,0:T(8,128)(2,1)S(1)}, u32[]{:S(2)}, u32[]{:S(2)}) async-start(bf16[4,192,1024]{2,1,0:T(8,128)(2,1)} %attend_back.1), calls=%async_computation.3 | async-start | bytes 3145728 | tf_op jit(solution)/shard_map/all_to_all | solution.py:1356
  462.1 27.9 %collective-permute-start.82 = (bf16[64,2048]{1,0:T(8,128)(2,1)S(1)}, bf16[64,2048]{1,0:T(8,128)(2,1)S(1)}, u32[]{:S(2)}, u32[]{:S(2)}) collective-permute-start(bf16[64,2048]{1,0:T(8,128)(2,1)S(1)} %pad_maximum_fusion.5), channel_id=1, source_target_pairs={{0,8},{8,0},{16,24},{24,16},{1,9},{9,1},{17,25},{25,17},{2,10},{10... | collective-permute-start | bytes 786440 | tf_op jit(solution)/shard_map/ppermute | solution.py:1110
  463.6 26.4 %collective-permute-start.83 = (bf16[64,2048]{1,0:T(8,128)(2,1)S(1)}, bf16[64,2048]{1,0:T(8,128)(2,1)S(1)}, u32[]{:S(2)}, u32[]{:S(2)}) collective-permute-start(bf16[64,2048]{1,0:T(8,128)(2,1)S(1)} %pad_maximum_fusion.6), channel_id=1, source_target_pairs={{0,16},{8,24},{16,0},{24,8},{1,17},{9,25},{17,1},{25,9},{2,18},{10... | collective-permute-start | bytes 786440 | tf_op jit(solution)/shard_map/ppermute | solution.py:1110
  492.1 26.7 %collective-permute-start.85 = (bf16[768,512]{1,0:T(8,128)(2,1)S(1)}, bf16[768,512]{1,0:T(8,128)(2,1)S(1)}, u32[]{:S(2)}, u32[]{:S(2)}) collective-permute-start(bf16[768,512]{1,0:T(8,128)(2,1)S(1)} %pad_maximum_fusion.2), channel_id=1, source_target_pairs={{0,8},{8,0},{16,24},{24,16},{1,9},{9,1},{17,25},{25,17},{2,10},{10... | collective-permute-start | bytes 2359304 | tf_op jit(solution)/shard_map/ppermute | solution.py:1110
  493.7 26.0 %collective-permute-start.86 = (bf16[768,512]{1,0:T(8,128)(2,1)S(1)}, bf16[768,512]{1,0:T(8,128)(2,1)}, u32[]{:S(2)}, u32[]{:S(2)}) collective-permute-start(bf16[768,512]{1,0:T(8,128)(2,1)S(1)} %pad_maximum_fusion.3), channel_id=1, source_target_pairs={{0,16},{8,24},{16,0},{24,8},{1,17},{9,25},{17,1},{25,9},{2,18},{10... | collective-permute-start | bytes 2359304 | tf_op jit(solution)/shard_map/ppermute | solution.py:1110
  (146 other events, 1999.0 us)
Sparse Core Ops, SparseCore 0:
  340.3 170.9 reduce-scatter.1

commit v4 on v3

--- a/solution.py
+++ b/solution.py
@@ -621,27 +621,43 @@
     )(index, *pieces).reshape(blocks * rows, width)
 
 
-def cols_kernel(shard_ref, back_ref, unit_ref, out_ref):
+def cols_kernel(shard_ref, back_ref, unit_hbm, out_ref, unit_s, sem):
     slots, _, width = out_ref.shape
-    back = back_ref[...]
+    copies = [
+        pltpu.make_async_copy(
+            unit_hbm.at[:, pl.ds(pl.multiple_of((shard_ref[0] ^ k) * width, width), width)],
+            unit_s.at[k],
+            sem.at[k],
+        )
+        for k in range(slots)
+    ]
+    for copy in copies:
+        copy.start()
     for k in range(slots):
-        at = pl.ds(pl.multiple_of((shard_ref[0] ^ k) * width, width), width)
-        out_ref[k] = dot_nn(back, unit_ref[:, at]).astype(jnp.bfloat16)
+        copies[k].wait()
+        out_ref[k] = dot_nn(back_ref[...], unit_s[k]).astype(jnp.bfloat16)
 
 
 def cols_parts_of(shard, back, unit_low, slots):
     rows = back.shape[0]
+    tokens = unit_low.shape[0]
     width = unit_low.shape[1] // slots
     vmem = pl.BlockSpec(memory_space=pltpu.VMEM)
     return pl.pallas_call(
         cols_kernel,
-        in_specs=[pl.BlockSpec(memory_space=pltpu.SMEM)] + [vmem] * 2,
+        in_specs=[
+            pl.BlockSpec(memory_space=pltpu.SMEM), vmem, pl.BlockSpec(memory_space=pl.ANY)
+        ],
         out_specs=vmem,
         out_shape=jax.ShapeDtypeStruct((slots, rows, width), jnp.bfloat16),
+        scratch_shapes=[
+            pltpu.VMEM((slots, tokens, width), unit_low.dtype),
+            pltpu.SemaphoreType.DMA((slots,)),
+        ],
         compiler_params=pltpu.CompilerParams(vmem_limit_bytes=24 * 2**20),
         cost_estimate=SHORT,
         name="cols_parts",
-    )(shard, back, unit_low)
+    )(shard, back, *in_hbm([unit_low]))
 
 
 def unit_back_kernel(index_ref, back_ref, columns_ref, near_ref, other_ref):
@@ -674,24 +690,28 @@
     )(index, back, columns)
 
 
-def spread_kernel(place_ref, own_ref, one_ref, two_ref, out_ref):
-    _, steps, rows, _ = out_ref.shape
+def spread_kernel(place_ref, own_ref, one_ref, two_ref, near_ref, other_ref, both_s):
+    steps, rows, _ = near_ref.shape
     z, core = place_ref[0] // 2, place_ref[0] % 2
     total = own_ref[...].astype(jnp.float32)
     total += one_ref[...].astype(jnp.float32) + two_ref[...].astype(jnp.float32)
     total = total.T.astype(jnp.bfloat16)
     for q in range(2 * steps):
-        out_ref[(core + q) % 2, (q // 2 + steps - z) % steps] = total[q * rows : (q + 1) * rows]
+        both_s[(core + q) % 2, (q // 2 + steps - z) % steps] = total[q * rows : (q + 1) * rows]
+    near_ref[...] = both_s[0]
+    other_ref[...] = both_s[1]
 
 
 def spread_columns(place, own, one, two, steps):
     columns, rows = own.shape
     vmem = pl.BlockSpec(memory_space=pltpu.VMEM)
+    shape = (steps, rows // (2 * steps), columns)
     return pl.pallas_call(
         spread_kernel,
         in_specs=[pl.BlockSpec(memory_space=pltpu.SMEM)] + [vmem] * 3,
-        out_specs=vmem,
-        out_shape=jax.ShapeDtypeStruct((2, steps, rows // (2 * steps), columns), jnp.bfloat16),
+        out_specs=[vmem] * 2,
+        out_shape=[jax.ShapeDtypeStruct(shape, jnp.bfloat16)] * 2,
+        scratch_shapes=[pltpu.VMEM((2,) + shape, jnp.bfloat16)],
         cost_estimate=SHORT,
         name="spread_columns",
     )(place, own, one, two)
@@ -699,7 +719,7 @@
 
 def pair_kernel(spread_ref, other_ref, *out_refs):
     for step, out_ref in enumerate(out_refs):
-        out_ref[...] = jnp.concatenate([spread_ref[0, step], other_ref[step]])
+        out_ref[...] = jnp.concatenate([spread_ref[step], other_ref[step]])
 
 
 def pair_columns(spread, other):
@@ -741,7 +761,7 @@
         ).astype(jnp.float32)
         total += jnp.sum(grads * ref[...].astype(jnp.float32), axis=1, keepdims=True)
         out_refs[m][...] = grads * gain_col
-    out_refs[3][...] = jnp.broadcast_to(total, (rows, 128)).T[:8]
+    out_refs[3][...] = jnp.broadcast_to(total, (rows, 128)).T[:1]
 
 
 def unpack_columns(place, gain_row, weights, cols):
@@ -752,7 +772,7 @@
         in_specs=[pl.BlockSpec(memory_space=pltpu.SMEM)] + [vmem] * (4 + len(cols)),
         out_specs=[vmem] * 4,
         out_shape=[jax.ShapeDtypeStruct((rows, width), jnp.float32)] * 3
-        + [jax.ShapeDtypeStruct((8, rows), jnp.float32)],
+        + [jax.ShapeDtypeStruct((1, rows), jnp.float32)],
         scratch_shapes=[pltpu.VMEM((2, len(cols), rows, cols[0].shape[1]), cols[0].dtype)],
         cost_estimate=SHORT,
         name="unpack_columns",
@@ -879,11 +899,6 @@
         copy.start()
     for c in range(4):
         at = slice(c * (width // 4), (c + 1) * (width // 4))
-        part = dot_nn(gate_s[...], first_ref[0, :, at]) + dot_nn(up_s[...], first_ref[1, :, at])
-        part_near[:, at] = part[:tok]
-        part_other[:, at] = part[tok:].astype(jnp.bfloat16)
-    for c in range(4):
-        at = slice(c * (width // 4), (c + 1) * (width // 4))
         down = dot_nn(hidden_s[...], down_ref[0, :, at]).astype(jnp.bfloat16)
         down_s[0, :, at] = down[:tok]
         down_s[1, :, at] = down[tok:]
@@ -893,6 +908,11 @@
     ]
     for copy in last:
         copy.start()
+    for c in range(4):
+        at = slice(c * (width // 4), (c + 1) * (width // 4))
+        part = dot_nn(gate_s[...], first_ref[0, :, at]) + dot_nn(up_s[...], first_ref[1, :, at])
+        part_near[:, at] = part[:tok]
+        part_other[:, at] = part[tok:].astype(jnp.bfloat16)
     for copy in copies + late + last:
         copy.wait()
 
@@ -1217,9 +1237,8 @@
     input_two = from_chip(after(point, input_one), 1)
     input_slots = both_cores([own_input, after(point, input_one)])
     input_last = both_cores([after(point, input_three)])
-    output_own = after(point, output_weight)
-    output_three = from_chip(output_own, -1)
-    point = join(point, col_far, input_two, input_slots, input_last, output_three)
+    gate_far = second_hops(after(point, gate_first))
+    point = join(point, col_far, input_two, input_slots, input_last)
     input_slots += both_cores([after(point, input_two)]) + input_last
     rel_blocks = (
         (shard ^ (slot // seqs)) * seqs
@@ -1236,11 +1255,13 @@
     )
     qkv_low = jnp.concatenate([turned, qkv[:, 2:]], axis=1).astype(BF16)
     qkv_low = qkv_low.reshape(shards, 3 * HEAD_DIM, span)
-    gate_far = second_hops(after(point, gate_first))
-    output_one = from_chip(after(point, output_weight), 1)
+    output_own = after(point, output_weight)
+    output_one, output_three = from_chip(output_own, 1), from_chip(output_own, -1)
     up_top, up_bottom = up_weight[: up_weight.shape[0] // 2], up_weight[up_weight.shape[0] // 2 :]
-    up_first = [from_shard(after(point, up_top), flip) for flip in (1, 2)]
-    point = join(point, qkv_low, gate_far, output_one, up_first)
+    up_first = [
+        from_shard(after(point, half), flip) for half in (up_top, up_bottom) for flip in (1, 2)
+    ]
+    point = join(point, qkv_low, gate_far, output_one, output_three, up_first)
 
     head_qkv = lax.all_to_all(
         after(point, qkv_low), "shard", split_axis=0, concat_axis=0, tiled=True
@@ -1248,8 +1269,7 @@
     output_two = from_chip(after(point, output_one), 1)
     own_grad = after(point, output_grad)
     grad_one = from_chip(own_grad, 1)
-    up_first += [from_shard(after(point, up_bottom), flip) for flip in (1, 2)]
-    point = join(point, head_qkv, output_two, grad_one, up_first)
+    point = join(point, head_qkv, output_two, grad_one)
     output_own = jnp.concatenate(after(point, [output_own, output_one, output_two, output_three]))
     output_first = first_hops(output_own)
     output_swapped = [swap_cores(output_own)]
@@ -1277,25 +1297,25 @@
     middle, normed_two, scale_two = project(
         rel_heads, after(point, token_blocks), layer_input, gain_two, output_pieces
     )
-    point = join(point, normed_two, up_far)
+    point = join(point, normed_two)
 
     own_tokens = after(point, normed_two)
     tokens_one, tokens_three = from_chip(own_tokens, 1), from_chip(own_tokens, -1)
     down_first = first_hops(after(point, down_weight))
     grad_slots = both_cores(after(point, [output_grad, grad_one, grad_two, grad_three]))
+    point = join(point, tokens_one, tokens_three, down_first, grad_slots, up_far)
+    tokens_two = from_chip(after(point, tokens_one), 1)
+    down_far = second_hops(after(point, down_first))
+    feed_slots = both_cores([own_tokens, after(point, tokens_one)])
     first_two = load_weights(
         [
             after(point, [gate_weight, *gate_first, *gate_far]),
             [up_weight, up_first[0], up_first[2], up_first[1], up_first[3], *up_far],
         ]
     )
-    point = join(point, tokens_one, tokens_three, down_first, grad_slots, first_two)
-    tokens_two = from_chip(after(point, tokens_one), 1)
-    down_far = second_hops(after(point, down_first))
-    feed_slots = both_cores([own_tokens, after(point, tokens_one)])
     output_here = load_weights([after(point, output_pieces)])
     feed_last = both_cores([after(point, tokens_three)])
-    point = join(point, tokens_two, down_far, feed_slots, feed_last, output_here)
+    point = join(point, tokens_two, down_far, feed_slots, feed_last, first_two, output_here)
     feed_slots += both_cores([after(point, tokens_two)]) + feed_last
     down_here = load_weights([[down_weight, *down_first, *after(point, down_far)]])
     order = (2, 1, 3, 0)
@@ -1313,7 +1333,8 @@
     parts_one, whole = feed(1, after(point, feed_slots[2:4]), whole)
     parts_three, whole = feed(3, feed_slots[6:8], whole)
     parts_own, whole = feed(0, feed_slots[0:2], whole)
-    point = join(point, arrived_two, parts_one, parts_three, parts_own)
+    head_slots = [head_low[0]] + [from_shard(after(point, head_low[k]), k) for k in range(1, 4)]
+    point = join(point, arrived_two, parts_one, parts_three, parts_own, head_slots)
     sum_one = core_sum(*after(point, parts_one)).astype(BF16)
     sum_three = core_sum(*after(point, parts_three)).astype(BF16)
     point = join(point, sum_one, sum_three)
@@ -1344,9 +1365,9 @@
     agrad_one = from_chip(own_agrad, 1)
     down_all = core_sum(after(point, down_near), down_other).astype(BF16)
     down_sums = [down_all[order.index(step)] for step in range(steps)]
-    head_slots = [head_low[0]] + [from_shard(after(point, head_low[k]), k) for k in range(1, 4)]
-    point = join(point, out_grad_blocks, agrad_one, down_sums, head_slots)
-    both = from_chip(jnp.concatenate([own_agrad, after(point, down_sums[2])]), -1)
+    pair = jnp.concatenate([own_agrad, down_sums[2]])
+    point = join(point, out_grad_blocks, agrad_one, pair, down_sums[3])
+    both = from_chip(after(point, pair), -1)
     down_three = from_chip(after(point, down_sums[3]), 1)
     back = attend_back(
         head_qkv, lse, head_out, after(point, out_grad_blocks), cos_all, sin_all, tok, bounds
@@ -1384,15 +1405,20 @@
         + after(point, down_one).astype(F32)
         + down_three.astype(F32)
     ).astype(BF16)
-    point, layer_output = lax.optimization_barrier(
-        (join(point, unit_two, unit_three, cols_first, out_last), layer_output)
+    gain_rows_back = out_grad_blocks[:, HEAD_DIM].astype(F32)
+    gain_two_out = jnp.sum(
+        gain_rows_back[:, :own_rows] + gain_rows_back[:, own_rows : 2 * own_rows], axis=0
+    )
+    point, layer_output, gain_two_out = lax.optimization_barrier(
+        (join(point, unit_two, unit_three, cols_first, out_last), layer_output, gain_two_out)
     )
     unit_one = from_chip((unit_sums[1] + after(point, unit_two).astype(F32)).astype(BF16), -1)
     cols_last = scatter_shard_last(cols_parts, after(point, cols_first))
     point = join(point, unit_one, cols_last)
-    cols_spread = spread_columns(place, cols_parts[0], *after(point, cols_last), steps)
-    cols_other = swap_cores(cols_spread[1])
-    cols_blocks = pair_columns(cols_spread, cols_other)
+    cols_near, cols_other = spread_columns(
+        place, cols_parts[0], *after(point, cols_last), steps
+    )
+    cols_blocks = pair_columns(cols_near, swap_cores(cols_other))
     point = join(point, cols_blocks)
     cols_same = list(after(point, cols_blocks))
     cols_same = cols_same[:1] + [from_chip(cols_same[step], -step) for step in range(1, steps)]
@@ -1409,14 +1435,10 @@
     gate_wgrad, up_wgrad, down_wgrad = [
         after(point, feed_wsum)[m].astype(F32) for m in range(3)
     ]
-    gain_rows_back = out_grad_blocks[:, HEAD_DIM].astype(F32)
-    gain_two_out = jnp.sum(
-        gain_rows_back[:, :own_rows] + gain_rows_back[:, own_rows : 2 * own_rows], axis=0
-    )
-    point, output_wgrad, input_grad, gate_wgrad, up_wgrad, down_wgrad, gain_two_out, cols_same = (
+    point, output_wgrad, input_grad, gate_wgrad, up_wgrad, down_wgrad, cols_same = (
         lax.optimization_barrier(
             (
-                *(point, output_wgrad, input_grad, gate_wgrad, up_wgrad, down_wgrad, gain_two_out),
+                *(point, output_wgrad, input_grad, gate_wgrad, up_wgrad, down_wgrad),
                 cols_same,
             )
         )
@@ -1427,7 +1449,7 @@
     return (
         layer_output,
         input_grad,
-        gain_one_out[0],
+        gain_one_out.reshape(-1),
         query_wgrad,
         key_wgrad,
         value_wgrad,

time: 571 us -> 561 us (0.982)
  waiting for transfers between devices: 230 us -> 212 us
  starting transfers between devices: 93.1 us -> 101 us
    ppermute x33, waiting for transfers between devices: 105 us -> 54.7 us  [from_shard(): return lax.ppermute(values, 'shard', [(i, i ^ flip) for i in range(4)])]
    ppermute x29, waiting for transfers between devices: 116 us -> 147 us  [from_chip(): lax.ppermute(values, 'seq', [((i + 2 * step) % count, i) for i in range(c...]
    ppermute x29, starting transfers between devices: 33.8 us -> 41 us  [from_chip(): lax.ppermute(values, 'seq', [((i + 2 * step) % count, i) for i in range(c...]
    unnamed x154 -> x148, local copies, waits for them, and re-layouts: 17.6 us -> 17.1 us
  transfers between devices with their start and end apart: 96 -> 96, of which waited for: 45 -> 41; matrix products, arithmetic and copies ran while one was open for 10% -> 10% of each run, Pallas kernels for 24% -> 24%
where the time goes in v4:
time: 561 us; the launch traced here: 551 us
  waiting for transfers between devices  212 us (38%)
  Pallas kernels  154 us (27%)
  starting transfers between devices  101 us (18%)
  local copies, waits for them, and re-layouts  35.3 us (6%)
  other arithmetic  30.7 us (5%)
  between operations  15.4 us (3%)
    ppermute x29, waiting for transfers between devices, from_chip(): lax.ppermute(values, 'seq', [((i + 2 * step) % count, i) for i in range(c...  147 us
    ppermute x33, waiting for transfers between devices, from_shard(): return lax.ppermute(values, 'shard', [(i, i ^ flip) for i in range(4)])  54.7 us
    ppermute x29, starting transfers between devices, from_chip(): lax.ppermute(values, 'seq', [((i + 2 * step) % count, i) for i in range(c...  41 us
    ppermute x33, starting transfers between devices, from_shard(): return lax.ppermute(values, 'shard', [(i, i ^ flip) for i in range(4)])  40.5 us
    pallas_call x4, Pallas kernels, feed_blocks(): pl.pallas_call(functools.partial(feed_kernel, call, len(whole)), in_specs...  36 us
    pallas_call x1, Pallas kernels, attend_back(): pl.pallas_call(functools.partial(bwd_kernel, tok), grid=(spans,), in_spec...  30.1 us
    pallas_call x1, Pallas kernels, feed_wgrads(): pl.pallas_call(feed_wgrad_kernel, grid=(cuts, shards), in_specs=[rows] *...  20.7 us
    pallas_call x1, Pallas kernels, attend(): pl.pallas_call(functools.partial(fwd_kernel, tok), grid=(spans,), in_spec...  19.9 us
  transfers between devices with their start and end apart: 96, of which 41 were waited for; matrix products, arithmetic and copies ran while one was open for 10% of the time, Pallas kernels for 24%

profile of v4, /device:TPU:8, one launch (start us, length us, event | category | flops | bytes accessed | tf_op | source)
XLA Modules:
  0.0 551.3 jit_solution(13593517156629285177)
XLA Ops:
  19.9 10.5 %collective-permute-done.1 = bf16[128,768]{1,0:T(8,128)(2,1)S(1)} collective-permute-done((bf16[128,768]{1,0:T(8,128)(2,1)S(1)}, bf16[128,768]{1,0:T(8,128)(2,1)S(1)}, u32[]{:S(2)}, u32[]{:S(2)}) %collective-permute-start.1) | collective-permute-done | bytes 196640 | tf_op jit(solution)/shard_map/ppermute | solution.py:1126
  40.1 12.2 %collective-permute-done.7.refs_6_ = bf16[128,2048]{1,0:T(8,128)(2,1)S(1)} collective-permute-done((bf16[128,2048]{1,0:T(8,128)(2,1)S(1)}, bf16[128,2048]{1,0:T(8,128)(2,1)S(1)}, u32[]{:S(2)}, u32[]{:S(2)}) %collective-permute-start.7) | collective-permute-done | bytes 524320 | tf_op jit(solution)/shard_map/ppermute | solution.py:1126
  52.3 8.5 %collective-permute-done.6.refs_2_ = bf16[128,2048]{1,0:T(8,128)(2,1)S(1)} collective-permute-done((bf16[128,2048]{1,0:T(8,128)(2,1)S(1)}, bf16[128,2048]{1,0:T(8,128)(2,1)S(1)}, u32[]{:S(2)}, u32[]{:S(2)}) %collective-permute-start.6) | collective-permute-done | bytes 524320 | tf_op jit(solution)/shard_map/ppermute | solution.py:1126
  99.5 5.5 collective-permute-done.20
  124.2 23.9 %collective-permute-done.25 = bf16[64,2048]{1,0:T(8,128)(2,1)} collective-permute-done((bf16[64,2048]{1,0:T(8,128)(2,1)}, bf16[64,2048]{1,0:T(8,128)(2,1)}, u32[]{:S(2)}, u32[]{:S(2)}) %collective-permute-start.25) | collective-permute-done | bytes 262176 | tf_op jit(solution)/shard_map/ppermute | solution.py:1126
  157.1 19.9 %attend.1 = (f32[4,64,1024]{2,1,0:T(8,128)}, bf16[4,64,1024]{2,1,0:T(8,128)(2,1)}, bf16[32,80,128]{2,1,0:T(8,128)(2,1)}, f32[4,1,1024]{2,1,0:T(1,128)S(1)}) custom-call(s32[1]{0:T(128)} %bitcast.19.shard_ref.refs_0_, s32[4]{0:T(128)S(1)} %and_select_fusion.7.lo_ref, s32[4]{0:T(128)S(1)} %iota_minimum_fusion.full_ref, ...), custom_call_target="tpu_custom_call" | custom-call | flops 21474836480 | bytes 4194304 | tf_op jit(solution)/shard_map/attend/pallas_call | solution.py:497
  189.1 15.2 %collective-permute-done.33.refs_4_ = bf16[128,2048]{1,0:T(8,128)(2,1)S(1)} collective-permute-done((bf16[128,2048]{1,0:T(8,128)(2,1)S(1)}, bf16[128,2048]{1,0:T(8,128)(2,1)S(1)}, u32[]{:S(2)}, u32[]{:S(2)}) %collective-permute-start.33) | collective-permute-done | bytes 524320 | tf_op jit(solution)/shard_map/ppermute | solution.py:1130
  222.9 5.5 %collective-permute-done.39.refs_1_ = bf16[128,2048]{1,0:T(8,128)(2,1)S(1)} collective-permute-done((bf16[128,2048]{1,0:T(8,128)(2,1)S(1)}, bf16[128,2048]{1,0:T(8,128)(2,1)S(1)}, u32[]{:S(2)}, u32[]{:S(2)}) %collective-permute-start.39) | collective-permute-done | bytes 524320 | tf_op jit(solution)/shard_map/ppermute | solution.py:1126
  228.4 11.4 %collective-permute-done.38.refs_1_ = bf16[128,2048]{1,0:T(8,128)(2,1)S(1)} collective-permute-done((bf16[128,2048]{1,0:T(8,128)(2,1)S(1)}, bf16[128,2048]{1,0:T(8,128)(2,1)S(1)}, u32[]{:S(2)}, u32[]{:S(2)}) %collective-permute-start.38) | collective-permute-done | bytes 524320 | tf_op jit(solution)/shard_map/ppermute | solution.py:1126
  255.7 5.3 collective-permute-done.50.refs_4_
  264.7 8.9 %feed_blocks.4 = (f32[128,2048]{1,0:T(8,128)S(1)}, bf16[128,2048]{1,0:T(8,128)(2,1)S(1)}, bf16[1024,2048]{1,0:T(8,128)(2,1)}, bf16[1024,2048]{1,0:T(8,128)(2,1)}...) custom-call(s32[1]{0:T(128)} %bitcast.19.shard_ref.refs_0_, ...), custom_call_target="tpu_custom_call" | custom-call | tf_op jit(solution)/shard_map/feed_blocks/pallas_call | solution.py:932
  281.9 8.6 %feed_blocks.5 = (f32[128,2048]{1,0:T(8,128)S(1)}, bf16[128,2048]{1,0:T(8,128)(2,1)S(1)}, bf16[1024,2048]{1,0:T(8,128)(2,1)}, bf16[1024,2048]{1,0:T(8,128)(2,1)}...) custom-call(s32[1]{0:T(128)} %bitcast.19.shard_ref.refs_0_, ...), custom_call_target="tpu_custom_call", output_to_operand_aliasing={{2}: (7, {}), {3}: (8, {}), {4}: (9, {}), {5}: (10, {}), {6... | custom-call | tf_op jit(solution)/shard_map/feed_blocks/pallas_call | solution.py:932
  290.6 9.5 %feed_blocks.6 = (f32[128,2048]{1,0:T(8,128)S(1)}, bf16[128,2048]{1,0:T(8,128)(2,1)S(1)}, bf16[1024,2048]{1,0:T(8,128)(2,1)}, bf16[1024,2048]{1,0:T(8,128)(2,1)}...) custom-call(s32[1]{0:T(128)} %bitcast.19.shard_ref.refs_0_, ...), custom_call_target="tpu_custom_call", output_to_operand_aliasing={{2}: (7, {}), {3}: (8, {}), {4}: (9, {}), {5}: (10, {}), {6... | custom-call | tf_op jit(solution)/shard_map/feed_blocks/pallas_call | solution.py:932
  300.1 8.9 %feed_blocks.7 = (f32[128,2048]{1,0:T(8,128)S(1)}, bf16[128,2048]{1,0:T(8,128)(2,1)S(1)}, bf16[1024,2048]{1,0:T(8,128)(2,1)}, bf16[1024,2048]{1,0:T(8,128)(2,1)}...) custom-call(s32[1]{0:T(128)} %bitcast.19.shard_ref.refs_0_, ...), custom_call_target="tpu_custom_call", output_to_operand_aliasing={{2}: (7, {}), {3}: (8, {}), {4}: (9, {}), {5}: (10, {}), {6... | custom-call | tf_op jit(solution)/shard_map/feed_blocks/pallas_call | solution.py:932
  314.8 20.7 %feed_wgrads.1 = bf16[4,3,256,2048]{3,2,1,0:T(8,128)(2,1)} custom-call(bf16[1024,1024]{1,0:T(8,128)(2,1)} %get-tuple-element.355.gate_ref, bf16[1024,1024]{1,0:T(8,128)(2,1)} %get-tuple-element.356.up_ref, bf16[1024,1024]{1,0:T(8,128)(2,1)} %get-tuple-element.357.hidden_ref, bf16[1024,2048]{1,0:T(8,128)(2,1)} %get-tuple-element.358.tokens_ref, ...), custom_call_target="tpu_custom_call" | custom-call | tf_op jit(solution)/shard_map/feed_wgrads/pallas_call | solution.py:1083
  354.8 21.6 %collective-permute-done.65.refs_2_ = bf16[128,2048]{1,0:T(8,128)(2,1)} collective-permute-done((bf16[128,2048]{1,0:T(8,128)(2,1)S(1)}, bf16[128,2048]{1,0:T(8,128)(2,1)}, u32[]{:S(2)}, u32[]{:S(2)}) %collective-permute-start.65) | collective-permute-done | bytes 524320 | tf_op jit(solution)/shard_map/ppermute | solution.py:1126
  378.5 30.1 %attend_back.1 = bf16[4,192,1024]{2,1,0:T(8,128)(2,1)} custom-call(s32[4]{0:T(128)S(1)} %and_select_fusion.hi_ref, s32[4]{0:T(128)S(1)} %iota_minimum_fusion.full_ref, s32[4,1,1024]{2,1,0:T(1,128)S(1)} %broadcast_in_dim.40.start_ref, bf16[4,192,1024]{2,1,0:T(8,128)(2,1)S(1)} %copy-done.16, f32[4,1,1024]{2,1,0:T(1,128)S(1)} %get-tuple-element.377.lse_ref, ...), custom_call_target="tpu_custom_call" | custom-call | flops 30064771072 | bytes 4194304 | tf_op jit(solution)/shard_map/attend_back/pallas_call | solution.py:537
  409.4 4.9 collective-permute-done.67
  420.3 7.9 %collective-permute-done.72.refs_4_ = bf16[128,2048]{1,0:T(8,128)(2,1)S(1)} collective-permute-done((bf16[128,2048]{1,0:T(8,128)(2,1)}, bf16[128,2048]{1,0:T(8,128)(2,1)S(1)}, u32[]{:S(2)}, u32[]{:S(2)}) %collective-permute-start.72) | collective-permute-done | bytes 524320 | tf_op jit(solution)/shard_map/ppermute | solution.py:1126
  440.1 5.0 collective-permute-done.69
  445.3 5.6 %cols_parts.1 = bf16[4,768,512]{2,1,0:T(8,128)(2,1)S(1)} custom-call(s32[1]{0:T(128)} %bitcast.19.shard_ref.refs_0_, bf16[768,1024]{1,0:T(8,128)(2,1)S(1)} %bitcast.136, bf16[1024,2048]{1,0:T(8,128)(2,1)} %copy-done.2), custom_call_target="tpu_custom_call" | custom-call | tf_op jit(solution)/shard_map/cols_parts/pallas_call | solution.py:646
  466.3 10.9 %collective-permute-done.81 = bf16[384,512]{1,0:T(8,128)(2,1)S(1)} collective-permute-done((bf16[384,512]{1,0:T(8,128)(2,1)S(1)}, bf16[384,512]{1,0:T(8,128)(2,1)S(1)}, u32[]{:S(2)}, u32[]{:S(2)}) %collective-permute-start.81) | collective-permute-done | bytes 393248 | tf_op jit(solution)/shard_map/ppermute | solution.py:1130
  481.0 8.5 %collective-permute-done.82 = bf16[64,2048]{1,0:T(8,128)(2,1)S(1)} collective-permute-done((bf16[64,2048]{1,0:T(8,128)(2,1)S(1)}, bf16[64,2048]{1,0:T(8,128)(2,1)S(1)}, u32[]{:S(2)}, u32[]{:S(2)}) %collective-permute-start.82) | collective-permute-done | bytes 262176 | tf_op jit(solution)/shard_map/ppermute | solution.py:1130
  495.5 12.5 %collective-permute-done.84 = bf16[128,2048]{1,0:T(8,128)(2,1)S(1)} collective-permute-done((bf16[128,2048]{1,0:T(8,128)(2,1)S(1)}, bf16[128,2048]{1,0:T(8,128)(2,1)S(1)}, u32[]{:S(2)}, u32[]{:S(2)}) %collective-permute-start.84) | collective-permute-done | bytes 524320 | tf_op jit(solution)/shard_map/ppermute | solution.py:1126
  (415 shorter events, 254.1 us)
Async XLA Ops:
  10.9 26.6 %collective-permute-start.9 = (bf16[256,2048]{1,0:T(8,128)(2,1)}, bf16[256,2048]{1,0:T(8,128)(2,1)S(1)}, u32[]{:S(2)}, u32[]{:S(2)}) collective-permute-start(bf16[256,2048]{1,0:T(8,128)(2,1)} %refs_0_.2), channel_id=1, source_target_pairs={{0,16},{8,24},{16,0},{24,8},{1,17},{9,25},{17,1},{25,9},{2,18},{10... | collective-permute-start | bytes 3145736 | tf_op jit(solution)/shard_map/ppermute | solution.py:1130
  12.4 27.0 %collective-permute-start.8 = (bf16[256,2048]{1,0:T(8,128)(2,1)}, bf16[256,2048]{1,0:T(8,128)(2,1)S(1)}, u32[]{:S(2)}, u32[]{:S(2)}) collective-permute-start(bf16[256,2048]{1,0:T(8,128)(2,1)} %refs_0_.2), channel_id=1, source_target_pairs={{0,8},{8,0},{16,24},{24,16},{1,9},{9,1},{17,25},{25,17},{2,10},{10... | collective-permute-start | bytes 3145736 | tf_op jit(solution)/shard_map/ppermute | solution.py:1130
  79.9 33.6 %collective-permute-start.22 = (bf16[128,2048]{1,0:T(8,128)(2,1)}, bf16[128,2048]{1,0:T(8,128)(2,1)}, u32[]{:S(2)}, u32[]{:S(2)}) collective-permute-start(bf16[128,2048]{1,0:T(8,128)(2,1)} %get-tuple-element.247), channel_id=1, source_target_pairs={{0,16},{8,24},{16,0},{24,8},{1,17},{9,25},{17,1},{25,9},{2,18},{10... | collective-permute-start | bytes 1572872 | tf_op jit(solution)/shard_map/ppermute | solution.py:1130
  80.4 33.1 %collective-permute-start.21 = (bf16[128,2048]{1,0:T(8,128)(2,1)}, bf16[128,2048]{1,0:T(8,128)(2,1)}, u32[]{:S(2)}, u32[]{:S(2)}) collective-permute-start(bf16[128,2048]{1,0:T(8,128)(2,1)} %get-tuple-element.247), channel_id=1, source_target_pairs={{0,8},{8,0},{16,24},{24,16},{1,9},{9,1},{17,25},{25,17},{2,10},{10... | collective-permute-start | bytes 1572872 | tf_op jit(solution)/shard_map/ppermute | solution.py:1130
  86.1 27.5 %collective-permute-start.24 = (bf16[128,2048]{1,0:T(8,128)(2,1)}, bf16[128,2048]{1,0:T(8,128)(2,1)S(1)}, u32[]{:S(2)}, u32[]{:S(2)}) collective-permute-start(bf16[128,2048]{1,0:T(8,128)(2,1)} %get-tuple-element.248), channel_id=1, source_target_pairs={{0,16},{8,24},{16,0},{24,8},{1,17},{9,25},{17,1},{25,9},{2,18},{10... | collective-permute-start | bytes 1572872 | tf_op jit(solution)/shard_map/ppermute | solution.py:1130
  114.5 33.6 %all-to-all-start = ((bf16[4,192,1024]{2,1,0:T(8,128)(2,1)}), bf16[4,192,1024]{2,1,0:T(8,128)(2,1)S(1)}, u32[]{:S(2)}, u32[]{:S(2)}) async-start(bf16[4,192,1024]{2,1,0:T(8,128)(2,1)} %bitcast.139), calls=%async_computation | async-start | bytes 3145728 | tf_op jit(solution)/shard_map/all_to_all | solution.py:1266
  118.4 29.7 %collective-permute-start.26 = (bf16[128,2048]{1,0:T(8,128)(2,1)S(1)}, bf16[128,2048]{1,0:T(8,128)(2,1)S(1)}, u32[]{:S(2)}, u32[]{:S(2)}) collective-permute-start(bf16[128,2048]{1,0:T(8,128)(2,1)S(1)} %copy-done.8), channel_id=1, source_target_pairs={{2,0},{3,1},{4,2},{5,3},{6,4},{7,5},{0,6},{1,7},{10,8},{11,9},{12,... | collective-permute-start | bytes 1572872 | tf_op jit(solution)/shard_map/ppermute | solution.py:1126
  121.6 26.5 %collective-permute-start.25 = (bf16[64,2048]{1,0:T(8,128)(2,1)}, bf16[64,2048]{1,0:T(8,128)(2,1)}, u32[]{:S(2)}, u32[]{:S(2)}) collective-permute-start(bf16[64,2048]{1,0:T(8,128)(2,1)} %collective-permute-done.19), channel_id=1, source_target_pairs={{2,0},{3,1},{4,2},{5,3},{6,4},{7,5},{0,6},{1,7},{10,8},{11,9},{12,... | collective-permute-start | bytes 786440 | tf_op jit(solution)/shard_map/ppermute | solution.py:1126
  123.2 53.8 %collective-permute-start.31 = (bf16[128,2048]{1,0:T(8,128)(2,1)S(1)}, bf16[128,2048]{1,0:T(8,128)(2,1)}, u32[]{:S(2)}, u32[]{:S(2)}) collective-permute-start(bf16[128,2048]{1,0:T(8,128)(2,1)S(1)} %copy-done.8), channel_id=1, source_target_pairs={{6,0},{7,1},{0,2},{1,3},{2,4},{3,5},{4,6},{5,7},{14,8},{15,9},{8,1... | collective-permute-start | bytes 1572872 | tf_op jit(solution)/shard_map/ppermute | solution.py:1126
  151.3 26.5 %collective-permute-start.29 = (bf16[256,2048]{1,0:T(8,128)(2,1)S(1)}, bf16[256,2048]{1,0:T(8,128)(2,1)S(1)}, u32[]{:S(2)}, u32[]{:S(2)}) collective-permute-start(bf16[256,2048]{1,0:T(8,128)(2,1)S(1)} %constant_dynamic-update-slice_fusion.4.refs_0_), channel_id=1, source_target_pairs={{0,1},{1,0},{2,3},{3,2},{4,5},{5,4},{6,7},{7,6},{8,9},{9,8},{10,11... | collective-permute-start | bytes 3145736 | tf_op jit(solution)/shard_map/ppermute | solution.py:1121
  151.3 26.5 %collective-permute-start.28 = (bf16[256,2048]{1,0:T(8,128)(2,1)S(1)}, bf16[256,2048]{1,0:T(8,128)(2,1)}, u32[]{:S(2)}, u32[]{:S(2)}) collective-permute-start(bf16[256,2048]{1,0:T(8,128)(2,1)S(1)} %constant_dynamic-update-slice_fusion.4.refs_0_), channel_id=1, source_target_pairs={{0,16},{8,24},{16,0},{24,8},{1,17},{9,25},{17,1},{25,9},{2,18},{10... | collective-permute-start | bytes 3145736 | tf_op jit(solution)/shard_map/ppermute | solution.py:1130
  178.8 26.8 %all-to-all-start.1 = ((bf16[32,80,128]{2,1,0:T(8,128)(2,1)}), bf16[32,80,128]{2,1,0:T(8,128)(2,1)S(1)}, u32[]{:S(2)}, u32[]{:S(2)}) async-start(bf16[32,80,128]{2,1,0:T(8,128)(2,1)} %get-tuple-element.262), calls=%async_computation.1 | async-start | bytes 1310720 | tf_op jit(solution)/shard_map/all_to_all | solution.py:1282
  183.2 347.1 %reduce-scatter.2.cloned.1.call-start = ((), (), s32[]{:S(2)}) async-start(), calls=%async_computation.5 | async-start | bytes 15728640 | tf_op jit(solution)/shard_map/reduce_scatter | solution.py:1361
  275.7 33.3 %collective-permute-start.56 = (bf16[128,2048]{1,0:T(8,128)(2,1)S(1)}, bf16[128,2048]{1,0:T(8,128)(2,1)S(1)}, u32[]{:S(2)}, u32[]{:S(2)}) collective-permute-start(bf16[128,2048]{1,0:T(8,128)(2,1)S(1)} %add_convert_fusion.3), channel_id=1, source_target_pairs={{4,0},{5,1},{6,2},{7,3},{0,4},{1,5},{2,6},{3,7},{12,8},{13,9},{14,... | collective-permute-start | bytes 1572872 | tf_op jit(solution)/shard_map/ppermute | solution.py:1126
  278.4 30.6 %collective-permute-start.57 = (bf16[64,1024]{1,0:T(8,128)(2,1)S(1)}, bf16[64,1024]{1,0:T(8,128)(2,1)S(1)}, u32[]{:S(2)}, u32[]{:S(2)}) collective-permute-start(bf16[64,1024]{1,0:T(8,128)(2,1)S(1)} %get-tuple-element.337), channel_id=1, source_target_pairs={{0,8},{8,0},{16,24},{24,16},{1,9},{9,1},{17,25},{25,17},{2,10},{10... | collective-permute-start | bytes 393224 | tf_op jit(solution)/shard_map/ppermute | solution.py:1130
  279.4 29.6 %collective-permute-start.58 = (bf16[64,1024]{1,0:T(8,128)(2,1)S(1)}, bf16[64,1024]{1,0:T(8,128)(2,1)S(1)}, u32[]{:S(2)}, u32[]{:S(2)}) collective-permute-start(bf16[64,1024]{1,0:T(8,128)(2,1)S(1)} %get-tuple-element.338), channel_id=1, source_target_pairs={{0,16},{8,24},{16,0},{24,8},{1,17},{9,25},{17,1},{25,9},{2,18},{10... | collective-permute-start | bytes 393224 | tf_op jit(solution)/shard_map/ppermute | solution.py:1130
  280.1 28.9 %collective-permute-start.59 = (bf16[64,1024]{1,0:T(8,128)(2,1)S(1)}, bf16[64,1024]{1,0:T(8,128)(2,1)S(1)}, u32[]{:S(2)}, u32[]{:S(2)}) collective-permute-start(bf16[64,1024]{1,0:T(8,128)(2,1)S(1)} %get-tuple-element.339), channel_id=1, source_target_pairs={{0,24},{8,16},{16,8},{24,0},{1,25},{9,17},{17,9},{25,1},{2,26},{10... | collective-permute-start | bytes 393224 | tf_op jit(solution)/shard_map/ppermute | solution.py:1130
  344.6 31.8 %all-to-all-start.2 = ((bf16[32,80,128]{2,1,0:T(8,128)(2,1)}), bf16[32,80,128]{2,1,0:T(8,128)(2,1)S(1)}, u32[]{:S(2)}, u32[]{:S(2)}) async-start(bf16[32,80,128]{2,1,0:T(8,128)(2,1)} %get-tuple-element.370), calls=%async_computation.2 | async-start | bytes 1310720 | tf_op jit(solution)/shard_map/all_to_all | solution.py:1358
  348.5 27.9 %collective-permute-start.65 = (bf16[128,2048]{1,0:T(8,128)(2,1)S(1)}, bf16[128,2048]{1,0:T(8,128)(2,1)}, u32[]{:S(2)}, u32[]{:S(2)}) collective-permute-start(bf16[128,2048]{1,0:T(8,128)(2,1)S(1)} %get-tuple-element.385.refs_0_), channel_id=1, source_target_pairs={{2,0},{3,1},{4,2},{5,3},{6,4},{7,5},{0,6},{1,7},{10,8},{11,9},{12,... | collective-permute-start | bytes 1572872 | tf_op jit(solution)/shard_map/ppermute | solution.py:1126
  376.5 32.1 %collective-permute-start.68 = (bf16[128,2048]{1,0:T(8,128)(2,1)}, bf16[128,2048]{1,0:T(8,128)(2,1)S(1)}, u32[]{:S(2)}, u32[]{:S(2)}) collective-permute-start(bf16[128,2048]{1,0:T(8,128)(2,1)} %get-tuple-element.381), channel_id=1, source_target_pairs={{2,0},{3,1},{4,2},{5,3},{6,4},{7,5},{0,6},{1,7},{10,8},{11,9},{12,... | collective-permute-start | bytes 1572872 | tf_op jit(solution)/shard_map/ppermute | solution.py:1126
  376.5 37.9 %collective-permute-start.67 = (bf16[256,2048]{1,0:T(8,128)(2,1)}, bf16[256,2048]{1,0:T(8,128)(2,1)}, u32[]{:S(2)}, u32[]{:S(2)}) collective-permute-start(bf16[256,2048]{1,0:T(8,128)(2,1)} %pad_maximum_fusion.1), channel_id=1, source_target_pairs={{6,0},{7,1},{0,2},{1,3},{2,4},{3,5},{4,6},{5,7},{14,8},{15,9},{8,1... | collective-permute-start | bytes 3145736 | tf_op jit(solution)/shard_map/ppermute | solution.py:1126
  414.7 30.4 %all-to-all-start.3 = ((bf16[4,192,1024]{2,1,0:T(8,128)(2,1)}), bf16[4,192,1024]{2,1,0:T(8,128)(2,1)S(1)}, u32[]{:S(2)}, u32[]{:S(2)}) async-start(bf16[4,192,1024]{2,1,0:T(8,128)(2,1)} %attend_back.1), calls=%async_computation.3 | async-start | bytes 3145728 | tf_op jit(solution)/shard_map/all_to_all | solution.py:1377
  460.3 29.3 %collective-permute-start.82 = (bf16[64,2048]{1,0:T(8,128)(2,1)S(1)}, bf16[64,2048]{1,0:T(8,128)(2,1)S(1)}, u32[]{:S(2)}, u32[]{:S(2)}) collective-permute-start(bf16[64,2048]{1,0:T(8,128)(2,1)S(1)} %pad_maximum_fusion.5), channel_id=1, source_target_pairs={{0,8},{8,0},{16,24},{24,16},{1,9},{9,1},{17,25},{25,17},{2,10},{10... | collective-permute-start | bytes 786440 | tf_op jit(solution)/shard_map/ppermute | solution.py:1130
  461.7 27.9 %collective-permute-start.83 = (bf16[64,2048]{1,0:T(8,128)(2,1)S(1)}, bf16[64,2048]{1,0:T(8,128)(2,1)S(1)}, u32[]{:S(2)}, u32[]{:S(2)}) collective-permute-start(bf16[64,2048]{1,0:T(8,128)(2,1)S(1)} %pad_maximum_fusion.6), channel_id=1, source_target_pairs={{0,16},{8,24},{16,0},{24,8},{1,17},{9,25},{17,1},{25,9},{2,18},{10... | collective-permute-start | bytes 786440 | tf_op jit(solution)/shard_map/ppermute | solution.py:1130
  (143 other events, 1883.0 us)
Sparse Core Ops, SparseCore 0:
  344.5 155.2 reduce-scatter.1

commit v5 on v4

--- a/solution.py
+++ b/solution.py
@@ -1267,24 +1267,24 @@
         after(point, qkv_low), "shard", split_axis=0, concat_axis=0, tiled=True
     )
     output_two = from_chip(after(point, output_one), 1)
-    own_grad = after(point, output_grad)
-    grad_one = from_chip(own_grad, 1)
-    point = join(point, head_qkv, output_two, grad_one)
+    point = join(point, head_qkv, output_two)
     output_own = jnp.concatenate(after(point, [output_own, output_one, output_two, output_three]))
     output_first = first_hops(output_own)
     output_swapped = [swap_cores(output_own)]
-    grad_two, grad_three = from_chip(after(point, grad_one), 1), from_chip(own_grad, -1)
+    own_grad = after(point, output_grad)
+    grad_one, grad_three = from_chip(own_grad, 1), from_chip(own_grad, -1)
     gain_rows = jnp.pad(feed_gain[None, :], ((0, EXTRA - 1), (0, tok - own_rows)))
     head_out, head_low, out_blocks, lse = attend(
         after(point, head_qkv), gain_rows, tok, shard_at, bounds
     )
-    point = join(point, out_blocks, output_first, output_swapped, grad_two, grad_three)
+    point = join(point, out_blocks, output_first, output_swapped, grad_one, grad_three)
     token_blocks = lax.all_to_all(
         after(point, out_blocks), ("shard", "seq"), split_axis=0, concat_axis=0, tiled=True
     )
     output_far = second_hops(after(point, output_first))
     output_swapped += [swap_cores(piece) for piece in after(point, output_first)]
-    point = join(point, token_blocks, output_far, output_swapped)
+    grad_two = from_chip(after(point, grad_one), 1)
+    point = join(point, token_blocks, output_far, output_swapped, grad_two)
     gain_two = token_blocks[:, HEAD_DIM, :own_rows].astype(F32).reshape(1, width)
     output_swapped += [swap_cores(piece) for piece in after(point, output_far)]
     up_far = [from_shard(after(point, up_first[0]), 2), from_shard(after(point, up_first[3]), 1)]

time: 561 us -> 556 us (level)
    ppermute x29, waiting for transfers between devices: 147 us -> 131 us  [from_chip(): lax.ppermute(values, 'seq', [((i + 2 * step) % count, i) for i in range(c...]
    all_to_all x1, waiting for transfers between devices: 0.01 us -> 10.1 us  [per_device(): lax.all_to_all(after(point, qkv_low), 'shard', split_axis=0, concat_axis=...]
  transfers between devices with their start and end apart: 96 -> 96, of which waited for: 41 -> 44; matrix products, arithmetic and copies ran while one was open for 10% -> 10% of each run, Pallas kernels for 24% -> 24%
where the time goes in v5:
time: 556 us; the launch traced here: 546 us
  waiting for transfers between devices  210 us (38%)
  Pallas kernels  153 us (28%)
  starting transfers between devices  99.3 us (18%)
  local copies, waits for them, and re-layouts  33.9 us (6%)
  other arithmetic  30.8 us (6%)
  between operations  15.4 us (3%)
    ppermute x29, waiting for transfers between devices, from_chip(): lax.ppermute(values, 'seq', [((i + 2 * step) % count, i) for i in range(c...  131 us
    ppermute x33, waiting for transfers between devices, from_shard(): return lax.ppermute(values, 'shard', [(i, i ^ flip) for i in range(4)])  60.3 us
    ppermute x33, starting transfers between devices, from_shard(): return lax.ppermute(values, 'shard', [(i, i ^ flip) for i in range(4)])  40.7 us
    ppermute x29, starting transfers between devices, from_chip(): lax.ppermute(values, 'seq', [((i + 2 * step) % count, i) for i in range(c...  38.2 us
    pallas_call x4, Pallas kernels, feed_blocks(): pl.pallas_call(functools.partial(feed_kernel, call, len(whole)), in_specs...  34.9 us
    pallas_call x1, Pallas kernels, attend_back(): pl.pallas_call(functools.partial(bwd_kernel, tok), grid=(spans,), in_spec...  30.1 us
    pallas_call x1, Pallas kernels, feed_wgrads(): pl.pallas_call(feed_wgrad_kernel, grid=(cuts, shards), in_specs=[rows] *...  20.7 us
    pallas_call x1, Pallas kernels, attend(): pl.pallas_call(functools.partial(fwd_kernel, tok), grid=(spans,), in_spec...  19.9 us
  transfers between devices with their start and end apart: 96, of which 44 were waited for; matrix products, arithmetic and copies ran while one was open for 10% of the time, Pallas kernels for 24%

profile of v5, /device:TPU:8, one launch (start us, length us, event | category | flops | bytes accessed | tf_op | source)
XLA Modules:
  0.0 545.9 jit_solution(4841508563039335455)
XLA Ops:
  19.9 10.5 %collective-permute-done.1 = bf16[128,768]{1,0:T(8,128)(2,1)S(1)} collective-permute-done((bf16[128,768]{1,0:T(8,128)(2,1)S(1)}, bf16[128,768]{1,0:T(8,128)(2,1)S(1)}, u32[]{:S(2)}, u32[]{:S(2)}) %collective-permute-start.1) | collective-permute-done | bytes 196640 | tf_op jit(solution)/shard_map/ppermute | solution.py:1126
  40.1 12.2 %collective-permute-done.7.refs_6_ = bf16[128,2048]{1,0:T(8,128)(2,1)S(1)} collective-permute-done((bf16[128,2048]{1,0:T(8,128)(2,1)S(1)}, bf16[128,2048]{1,0:T(8,128)(2,1)S(1)}, u32[]{:S(2)}, u32[]{:S(2)}) %collective-permute-start.7) | collective-permute-done | bytes 524320 | tf_op jit(solution)/shard_map/ppermute | solution.py:1126
  52.3 8.5 %collective-permute-done.6.refs_2_ = bf16[128,2048]{1,0:T(8,128)(2,1)S(1)} collective-permute-done((bf16[128,2048]{1,0:T(8,128)(2,1)S(1)}, bf16[128,2048]{1,0:T(8,128)(2,1)S(1)}, u32[]{:S(2)}, u32[]{:S(2)}) %collective-permute-start.6) | collective-permute-done | bytes 524320 | tf_op jit(solution)/shard_map/ppermute | solution.py:1126
  99.5 5.5 %collective-permute-done.20 = bf16[64,2048]{1,0:T(8,128)(2,1)S(1)} collective-permute-done((bf16[64,2048]{1,0:T(8,128)(2,1)}, bf16[64,2048]{1,0:T(8,128)(2,1)S(1)}, u32[]{:S(2)}, u32[]{:S(2)}) %collective-permute-start.20) | collective-permute-done | bytes 262176 | tf_op jit(solution)/shard_map/ppermute | solution.py:1126
  125.7 10.1 %all-to-all-done.qkv_ref = bf16[4,192,1024]{2,1,0:T(8,128)(2,1)S(1)} async-done(((bf16[4,192,1024]{2,1,0:T(8,128)(2,1)}), bf16[4,192,1024]{2,1,0:T(8,128)(2,1)S(1)}, u32[]{:S(2)}, u32[]{:S(2)}) %all-to-all-start) | async-done | bytes 1572896 | tf_op jit(solution)/shard_map/all_to_all | solution.py:1266
  142.5 19.9 %attend.1 = (f32[4,64,1024]{2,1,0:T(8,128)}, bf16[4,64,1024]{2,1,0:T(8,128)(2,1)}, bf16[32,80,128]{2,1,0:T(8,128)(2,1)}, f32[4,1,1024]{2,1,0:T(1,128)S(1)}) custom-call(s32[1]{0:T(128)} %bitcast.19.shard_ref.refs_0_, s32[4]{0:T(128)S(1)} %and_select_fusion.7.lo_ref, s32[4]{0:T(128)S(1)} %iota_minimum_fusion.full_ref, ...), custom_call_target="tpu_custom_call" | custom-call | flops 21474836480 | bytes 4194304 | tf_op jit(solution)/shard_map/attend/pallas_call | solution.py:497
  167.3 6.0 %all-to-all-start.1 = ((bf16[32,80,128]{2,1,0:T(8,128)(2,1)}), bf16[32,80,128]{2,1,0:T(8,128)(2,1)S(1)}, u32[]{:S(2)}, u32[]{:S(2)}) async-start(bf16[32,80,128]{2,1,0:T(8,128)(2,1)} %get-tuple-element.261), calls=%async_computation.1 | async-start | bytes 1310720 | tf_op jit(solution)/shard_map/all_to_all | solution.py:1281
  179.7 14.7 %collective-permute-done.32.refs_4_ = bf16[128,2048]{1,0:T(8,128)(2,1)S(1)} collective-permute-done((bf16[128,2048]{1,0:T(8,128)(2,1)S(1)}, bf16[128,2048]{1,0:T(8,128)(2,1)S(1)}, u32[]{:S(2)}, u32[]{:S(2)}) %collective-permute-start.32) | collective-permute-done | bytes 524320 | tf_op jit(solution)/shard_map/ppermute | solution.py:1130
  194.9 6.4 %collective-permute-done.35.refs_3_ = bf16[128,2048]{1,0:T(8,128)(2,1)S(1)} collective-permute-done((bf16[128,2048]{1,0:T(8,128)(2,1)S(1)}, bf16[128,2048]{1,0:T(8,128)(2,1)S(1)}, u32[]{:S(2)}, u32[]{:S(2)}) %collective-permute-start.35) | collective-permute-done | bytes 524320 | tf_op jit(solution)/shard_map/ppermute | solution.py:1126
  220.0 5.6 %collective-permute-done.39.refs_1_ = bf16[128,2048]{1,0:T(8,128)(2,1)S(1)} collective-permute-done((bf16[128,2048]{1,0:T(8,128)(2,1)S(1)}, bf16[128,2048]{1,0:T(8,128)(2,1)S(1)}, u32[]{:S(2)}, u32[]{:S(2)}) %collective-permute-start.39) | collective-permute-done | bytes 524320 | tf_op jit(solution)/shard_map/ppermute | solution.py:1126
  225.6 8.4 %collective-permute-done.38.refs_1_ = bf16[128,2048]{1,0:T(8,128)(2,1)S(1)} collective-permute-done((bf16[128,2048]{1,0:T(8,128)(2,1)S(1)}, bf16[128,2048]{1,0:T(8,128)(2,1)S(1)}, u32[]{:S(2)}, u32[]{:S(2)}) %collective-permute-start.38) | collective-permute-done | bytes 524320 | tf_op jit(solution)/shard_map/ppermute | solution.py:1126
  252.3 5.2 collective-permute-done.50.refs_4_
  261.7 8.9 %feed_blocks.4 = (f32[128,2048]{1,0:T(8,128)S(1)}, bf16[128,2048]{1,0:T(8,128)(2,1)S(1)}, bf16[1024,2048]{1,0:T(8,128)(2,1)}, bf16[1024,2048]{1,0:T(8,128)(2,1)}...) custom-call(s32[1]{0:T(128)} %bitcast.19.shard_ref.refs_0_, ...), custom_call_target="tpu_custom_call" | custom-call | tf_op jit(solution)/shard_map/feed_blocks/pallas_call | solution.py:932
  277.1 8.6 %feed_blocks.5 = (f32[128,2048]{1,0:T(8,128)S(1)}, bf16[128,2048]{1,0:T(8,128)(2,1)S(1)}, bf16[1024,2048]{1,0:T(8,128)(2,1)}, bf16[1024,2048]{1,0:T(8,128)(2,1)}...) custom-call(s32[1]{0:T(128)} %bitcast.19.shard_ref.refs_0_, ...), custom_call_target="tpu_custom_call", output_to_operand_aliasing={{2}: (7, {}), {3}: (8, {}), {4}: (9, {}), {5}: (10, {}), {6... | custom-call | tf_op jit(solution)/shard_map/feed_blocks/pallas_call | solution.py:932
  285.8 8.5 %feed_blocks.6 = (f32[128,2048]{1,0:T(8,128)S(1)}, bf16[128,2048]{1,0:T(8,128)(2,1)S(1)}, bf16[1024,2048]{1,0:T(8,128)(2,1)}, bf16[1024,2048]{1,0:T(8,128)(2,1)}...) custom-call(s32[1]{0:T(128)} %bitcast.19.shard_ref.refs_0_, ...), custom_call_target="tpu_custom_call", output_to_operand_aliasing={{2}: (7, {}), {3}: (8, {}), {4}: (9, {}), {5}: (10, {}), {6... | custom-call | tf_op jit(solution)/shard_map/feed_blocks/pallas_call | solution.py:932
  294.2 8.9 %feed_blocks.7 = (f32[128,2048]{1,0:T(8,128)S(1)}, bf16[128,2048]{1,0:T(8,128)(2,1)S(1)}, bf16[1024,2048]{1,0:T(8,128)(2,1)}, bf16[1024,2048]{1,0:T(8,128)(2,1)}...) custom-call(s32[1]{0:T(128)} %bitcast.19.shard_ref.refs_0_, ...), custom_call_target="tpu_custom_call", output_to_operand_aliasing={{2}: (7, {}), {3}: (8, {}), {4}: (9, {}), {5}: (10, {}), {6... | custom-call | tf_op jit(solution)/shard_map/feed_blocks/pallas_call | solution.py:932
  309.4 20.7 %feed_wgrads.1 = bf16[4,3,256,2048]{3,2,1,0:T(8,128)(2,1)} custom-call(bf16[1024,1024]{1,0:T(8,128)(2,1)} %get-tuple-element.355.gate_ref, bf16[1024,1024]{1,0:T(8,128)(2,1)} %get-tuple-element.356.up_ref, bf16[1024,1024]{1,0:T(8,128)(2,1)} %get-tuple-element.357.hidden_ref, bf16[1024,2048]{1,0:T(8,128)(2,1)} %get-tuple-element.358.tokens_ref, ...), custom_call_target="tpu_custom_call" | custom-call | tf_op jit(solution)/shard_map/feed_wgrads/pallas_call | solution.py:1083
  350.1 21.0 %collective-permute-done.65.refs_2_ = bf16[128,2048]{1,0:T(8,128)(2,1)} collective-permute-done((bf16[128,2048]{1,0:T(8,128)(2,1)S(1)}, bf16[128,2048]{1,0:T(8,128)(2,1)}, u32[]{:S(2)}, u32[]{:S(2)}) %collective-permute-start.65) | collective-permute-done | bytes 524320 | tf_op jit(solution)/shard_map/ppermute | solution.py:1126
  373.1 30.1 %attend_back.1 = bf16[4,192,1024]{2,1,0:T(8,128)(2,1)} custom-call(s32[4]{0:T(128)S(1)} %and_select_fusion.hi_ref, s32[4]{0:T(128)S(1)} %iota_minimum_fusion.full_ref, s32[4,1,1024]{2,1,0:T(1,128)S(1)} %broadcast_in_dim.40.start_ref, bf16[4,192,1024]{2,1,0:T(8,128)(2,1)S(1)} %copy-done.16, f32[4,1,1024]{2,1,0:T(1,128)S(1)} %get-tuple-element.377.lse_ref, ...), custom_call_target="tpu_custom_call" | custom-call | flops 30064771072 | bytes 4194304 | tf_op jit(solution)/shard_map/attend_back/pallas_call | solution.py:537
  414.9 7.9 %collective-permute-done.72.refs_4_ = bf16[128,2048]{1,0:T(8,128)(2,1)S(1)} collective-permute-done((bf16[128,2048]{1,0:T(8,128)(2,1)}, bf16[128,2048]{1,0:T(8,128)(2,1)S(1)}, u32[]{:S(2)}, u32[]{:S(2)}) %collective-permute-start.72) | collective-permute-done | bytes 524320 | tf_op jit(solution)/shard_map/ppermute | solution.py:1126
  439.9 5.7 %cols_parts.1 = bf16[4,768,512]{2,1,0:T(8,128)(2,1)S(1)} custom-call(s32[1]{0:T(128)} %bitcast.19.shard_ref.refs_0_, bf16[768,1024]{1,0:T(8,128)(2,1)S(1)} %bitcast.136, bf16[1024,2048]{1,0:T(8,128)(2,1)} %copy-done.2), custom_call_target="tpu_custom_call" | custom-call | tf_op jit(solution)/shard_map/cols_parts/pallas_call | solution.py:646
  460.9 10.9 %collective-permute-done.81 = bf16[384,512]{1,0:T(8,128)(2,1)S(1)} collective-permute-done((bf16[384,512]{1,0:T(8,128)(2,1)S(1)}, bf16[384,512]{1,0:T(8,128)(2,1)S(1)}, u32[]{:S(2)}, u32[]{:S(2)}) %collective-permute-start.81) | collective-permute-done | bytes 393248 | tf_op jit(solution)/shard_map/ppermute | solution.py:1130
  475.6 8.5 %collective-permute-done.82 = bf16[64,2048]{1,0:T(8,128)(2,1)S(1)} collective-permute-done((bf16[64,2048]{1,0:T(8,128)(2,1)S(1)}, bf16[64,2048]{1,0:T(8,128)(2,1)S(1)}, u32[]{:S(2)}, u32[]{:S(2)}) %collective-permute-start.82) | collective-permute-done | bytes 262176 | tf_op jit(solution)/shard_map/ppermute | solution.py:1130
  490.1 12.5 %collective-permute-done.84 = bf16[128,2048]{1,0:T(8,128)(2,1)S(1)} collective-permute-done((bf16[128,2048]{1,0:T(8,128)(2,1)S(1)}, bf16[128,2048]{1,0:T(8,128)(2,1)S(1)}, u32[]{:S(2)}, u32[]{:S(2)}) %collective-permute-start.84) | collective-permute-done | bytes 524320 | tf_op jit(solution)/shard_map/ppermute | solution.py:1126
  (415 shorter events, 265.3 us)
Async XLA Ops:
  10.9 26.6 %collective-permute-start.9 = (bf16[256,2048]{1,0:T(8,128)(2,1)}, bf16[256,2048]{1,0:T(8,128)(2,1)S(1)}, u32[]{:S(2)}, u32[]{:S(2)}) collective-permute-start(bf16[256,2048]{1,0:T(8,128)(2,1)} %refs_0_.2), channel_id=1, source_target_pairs={{0,16},{8,24},{16,0},{24,8},{1,17},{9,25},{17,1},{25,9},{2,18},{10... | collective-permute-start | bytes 3145736 | tf_op jit(solution)/shard_map/ppermute | solution.py:1130
  12.4 27.0 %collective-permute-start.8 = (bf16[256,2048]{1,0:T(8,128)(2,1)}, bf16[256,2048]{1,0:T(8,128)(2,1)S(1)}, u32[]{:S(2)}, u32[]{:S(2)}) collective-permute-start(bf16[256,2048]{1,0:T(8,128)(2,1)} %refs_0_.2), channel_id=1, source_target_pairs={{0,8},{8,0},{16,24},{24,16},{1,9},{9,1},{17,25},{25,17},{2,10},{10... | collective-permute-start | bytes 3145736 | tf_op jit(solution)/shard_map/ppermute | solution.py:1130
  39.5 26.2 %collective-permute-start.13 = (bf16[128,2048]{1,0:T(8,128)(2,1)S(1)}, bf16[128,2048]{1,0:T(8,128)(2,1)}, u32[]{:S(2)}, u32[]{:S(2)}) collective-permute-start(bf16[128,2048]{1,0:T(8,128)(2,1)S(1)} %copy-done.3), channel_id=1, source_target_pairs={{0,1},{1,0},{2,3},{3,2},{4,5},{5,4},{6,7},{7,6},{8,9},{9,8},{10,11... | collective-permute-start | bytes 1572872 | tf_op jit(solution)/shard_map/ppermute | solution.py:1121
  79.9 33.6 %collective-permute-start.22 = (bf16[128,2048]{1,0:T(8,128)(2,1)}, bf16[128,2048]{1,0:T(8,128)(2,1)}, u32[]{:S(2)}, u32[]{:S(2)}) collective-permute-start(bf16[128,2048]{1,0:T(8,128)(2,1)} %get-tuple-element.247), channel_id=1, source_target_pairs={{0,16},{8,24},{16,0},{24,8},{1,17},{9,25},{17,1},{25,9},{2,18},{10... | collective-permute-start | bytes 1572872 | tf_op jit(solution)/shard_map/ppermute | solution.py:1130
  80.4 33.1 %collective-permute-start.21 = (bf16[128,2048]{1,0:T(8,128)(2,1)}, bf16[128,2048]{1,0:T(8,128)(2,1)}, u32[]{:S(2)}, u32[]{:S(2)}) collective-permute-start(bf16[128,2048]{1,0:T(8,128)(2,1)} %get-tuple-element.247), channel_id=1, source_target_pairs={{0,8},{8,0},{16,24},{24,16},{1,9},{9,1},{17,25},{25,17},{2,10},{10... | collective-permute-start | bytes 1572872 | tf_op jit(solution)/shard_map/ppermute | solution.py:1130
  86.1 27.5 %collective-permute-start.24 = (bf16[128,2048]{1,0:T(8,128)(2,1)}, bf16[128,2048]{1,0:T(8,128)(2,1)S(1)}, u32[]{:S(2)}, u32[]{:S(2)}) collective-permute-start(bf16[128,2048]{1,0:T(8,128)(2,1)} %get-tuple-element.248), channel_id=1, source_target_pairs={{0,16},{8,24},{16,0},{24,8},{1,17},{9,25},{17,1},{25,9},{2,18},{10... | collective-permute-start | bytes 1572872 | tf_op jit(solution)/shard_map/ppermute | solution.py:1130
  135.8 26.6 %collective-permute-start.30 = (bf16[128,2048]{1,0:T(8,128)(2,1)S(1)}, bf16[128,2048]{1,0:T(8,128)(2,1)S(1)}, u32[]{:S(2)}, u32[]{:S(2)}) collective-permute-start(bf16[128,2048]{1,0:T(8,128)(2,1)S(1)} %copy-done.8), channel_id=1, source_target_pairs={{6,0},{7,1},{0,2},{1,3},{2,4},{3,5},{4,6},{5,7},{14,8},{15,9},{8,1... | collective-permute-start | bytes 1572872 | tf_op jit(solution)/shard_map/ppermute | solution.py:1126
  136.3 26.1 %collective-permute-start.29 = (bf16[128,2048]{1,0:T(8,128)(2,1)S(1)}, bf16[128,2048]{1,0:T(8,128)(2,1)S(1)}, u32[]{:S(2)}, u32[]{:S(2)}) collective-permute-start(bf16[128,2048]{1,0:T(8,128)(2,1)S(1)} %copy-done.8), channel_id=1, source_target_pairs={{2,0},{3,1},{4,2},{5,3},{6,4},{7,5},{0,6},{1,7},{10,8},{11,9},{12,... | collective-permute-start | bytes 1572872 | tf_op jit(solution)/shard_map/ppermute | solution.py:1126
  167.3 34.9 %all-to-all-start.1 = ((bf16[32,80,128]{2,1,0:T(8,128)(2,1)}), bf16[32,80,128]{2,1,0:T(8,128)(2,1)S(1)}, u32[]{:S(2)}, u32[]{:S(2)}) async-start(bf16[32,80,128]{2,1,0:T(8,128)(2,1)} %get-tuple-element.261), calls=%async_computation.1 | async-start | bytes 1310720 | tf_op jit(solution)/shard_map/all_to_all | solution.py:1281
  173.4 351.6 %reduce-scatter.2.cloned.1.call-start = ((), (), s32[]{:S(2)}) async-start(), calls=%async_computation.5 | async-start | bytes 15728640 | tf_op jit(solution)/shard_map/reduce_scatter | solution.py:1361
  173.4 27.9 %collective-permute-start.33 = (bf16[256,2048]{1,0:T(8,128)(2,1)}, bf16[256,2048]{1,0:T(8,128)(2,1)S(1)}, u32[]{:S(2)}, u32[]{:S(2)}) collective-permute-start(bf16[256,2048]{1,0:T(8,128)(2,1)} %collective-permute-done.26.refs_1_), channel_id=1, source_target_pairs={{0,1},{1,0},{2,3},{3,2},{4,5},{5,4},{6,7},{7,6},{8,9},{9,8},{10,11... | collective-permute-start | bytes 3145736 | tf_op jit(solution)/shard_map/ppermute | solution.py:1121
  173.6 28.6 %collective-permute-start.34 = (bf16[256,2048]{1,0:T(8,128)(2,1)}, bf16[256,2048]{1,0:T(8,128)(2,1)}, u32[]{:S(2)}, u32[]{:S(2)}) collective-permute-start(bf16[256,2048]{1,0:T(8,128)(2,1)} %collective-permute-done.27.refs_2_), channel_id=1, source_target_pairs={{0,1},{1,0},{2,3},{3,2},{4,5},{5,4},{6,7},{7,6},{8,9},{9,8},{10,11... | collective-permute-start | bytes 3145736 | tf_op jit(solution)/shard_map/ppermute | solution.py:1121
  272.7 30.5 %collective-permute-start.56 = (bf16[128,2048]{1,0:T(8,128)(2,1)S(1)}, bf16[128,2048]{1,0:T(8,128)(2,1)S(1)}, u32[]{:S(2)}, u32[]{:S(2)}) collective-permute-start(bf16[128,2048]{1,0:T(8,128)(2,1)S(1)} %add_convert_fusion.3), channel_id=1, source_target_pairs={{4,0},{5,1},{6,2},{7,3},{0,4},{1,5},{2,6},{3,7},{12,8},{13,9},{14,... | collective-permute-start | bytes 1572872 | tf_op jit(solution)/shard_map/ppermute | solution.py:1126
  273.6 29.6 %collective-permute-start.57 = (bf16[64,1024]{1,0:T(8,128)(2,1)S(1)}, bf16[64,1024]{1,0:T(8,128)(2,1)S(1)}, u32[]{:S(2)}, u32[]{:S(2)}) collective-permute-start(bf16[64,1024]{1,0:T(8,128)(2,1)S(1)} %get-tuple-element.337), channel_id=1, source_target_pairs={{0,8},{8,0},{16,24},{24,16},{1,9},{9,1},{17,25},{25,17},{2,10},{10... | collective-permute-start | bytes 393224 | tf_op jit(solution)/shard_map/ppermute | solution.py:1130
  274.3 28.8 %collective-permute-start.58 = (bf16[64,1024]{1,0:T(8,128)(2,1)S(1)}, bf16[64,1024]{1,0:T(8,128)(2,1)S(1)}, u32[]{:S(2)}, u32[]{:S(2)}) collective-permute-start(bf16[64,1024]{1,0:T(8,128)(2,1)S(1)} %get-tuple-element.338), channel_id=1, source_target_pairs={{0,16},{8,24},{16,0},{24,8},{1,17},{9,25},{17,1},{25,9},{2,18},{10... | collective-permute-start | bytes 393224 | tf_op jit(solution)/shard_map/ppermute | solution.py:1130
  275.8 27.4 %collective-permute-start.59 = (bf16[64,1024]{1,0:T(8,128)(2,1)S(1)}, bf16[64,1024]{1,0:T(8,128)(2,1)S(1)}, u32[]{:S(2)}, u32[]{:S(2)}) collective-permute-start(bf16[64,1024]{1,0:T(8,128)(2,1)S(1)} %get-tuple-element.339), channel_id=1, source_target_pairs={{0,24},{8,16},{16,8},{24,0},{1,25},{9,17},{17,9},{25,1},{2,26},{10... | collective-permute-start | bytes 393224 | tf_op jit(solution)/shard_map/ppermute | solution.py:1130
  339.8 31.3 %all-to-all-start.2 = ((bf16[32,80,128]{2,1,0:T(8,128)(2,1)}), bf16[32,80,128]{2,1,0:T(8,128)(2,1)S(1)}, u32[]{:S(2)}, u32[]{:S(2)}) async-start(bf16[32,80,128]{2,1,0:T(8,128)(2,1)} %get-tuple-element.370), calls=%async_computation.2 | async-start | bytes 1310720 | tf_op jit(solution)/shard_map/all_to_all | solution.py:1358
  343.1 27.9 %collective-permute-start.65 = (bf16[128,2048]{1,0:T(8,128)(2,1)S(1)}, bf16[128,2048]{1,0:T(8,128)(2,1)}, u32[]{:S(2)}, u32[]{:S(2)}) collective-permute-start(bf16[128,2048]{1,0:T(8,128)(2,1)S(1)} %get-tuple-element.385.refs_0_), channel_id=1, source_target_pairs={{2,0},{3,1},{4,2},{5,3},{6,4},{7,5},{0,6},{1,7},{10,8},{11,9},{12,... | collective-permute-start | bytes 1572872 | tf_op jit(solution)/shard_map/ppermute | solution.py:1126
  371.1 32.1 %collective-permute-start.68 = (bf16[128,2048]{1,0:T(8,128)(2,1)}, bf16[128,2048]{1,0:T(8,128)(2,1)S(1)}, u32[]{:S(2)}, u32[]{:S(2)}) collective-permute-start(bf16[128,2048]{1,0:T(8,128)(2,1)} %get-tuple-element.381), channel_id=1, source_target_pairs={{2,0},{3,1},{4,2},{5,3},{6,4},{7,5},{0,6},{1,7},{10,8},{11,9},{12,... | collective-permute-start | bytes 1572872 | tf_op jit(solution)/shard_map/ppermute | solution.py:1126
  371.1 37.9 %collective-permute-start.67 = (bf16[256,2048]{1,0:T(8,128)(2,1)}, bf16[256,2048]{1,0:T(8,128)(2,1)}, u32[]{:S(2)}, u32[]{:S(2)}) collective-permute-start(bf16[256,2048]{1,0:T(8,128)(2,1)} %pad_maximum_fusion.1), channel_id=1, source_target_pairs={{6,0},{7,1},{0,2},{1,3},{2,4},{3,5},{4,6},{5,7},{14,8},{15,9},{8,1... | collective-permute-start | bytes 3145736 | tf_op jit(solution)/shard_map/ppermute | solution.py:1126
  409.3 30.4 %all-to-all-start.3 = ((bf16[4,192,1024]{2,1,0:T(8,128)(2,1)}), bf16[4,192,1024]{2,1,0:T(8,128)(2,1)S(1)}, u32[]{:S(2)}, u32[]{:S(2)}) async-start(bf16[4,192,1024]{2,1,0:T(8,128)(2,1)} %attend_back.1), calls=%async_computation.3 | async-start | bytes 3145728 | tf_op jit(solution)/shard_map/all_to_all | solution.py:1377
  454.9 29.3 %collective-permute-start.82 = (bf16[64,2048]{1,0:T(8,128)(2,1)S(1)}, bf16[64,2048]{1,0:T(8,128)(2,1)S(1)}, u32[]{:S(2)}, u32[]{:S(2)}) collective-permute-start(bf16[64,2048]{1,0:T(8,128)(2,1)S(1)} %pad_maximum_fusion.5), channel_id=1, source_target_pairs={{0,8},{8,0},{16,24},{24,16},{1,9},{9,1},{17,25},{25,17},{2,10},{10... | collective-permute-start | bytes 786440 | tf_op jit(solution)/shard_map/ppermute | solution.py:1130
  456.3 27.9 %collective-permute-start.83 = (bf16[64,2048]{1,0:T(8,128)(2,1)S(1)}, bf16[64,2048]{1,0:T(8,128)(2,1)S(1)}, u32[]{:S(2)}, u32[]{:S(2)}) collective-permute-start(bf16[64,2048]{1,0:T(8,128)(2,1)S(1)} %pad_maximum_fusion.6), channel_id=1, source_target_pairs={{0,16},{8,24},{16,0},{24,8},{1,17},{9,25},{17,1},{25,9},{2,18},{10... | collective-permute-start | bytes 786440 | tf_op jit(solution)/shard_map/ppermute | solution.py:1130
  457.8 26.4 %collective-permute-start.79 = (bf16[128,2048]{1,0:T(8,128)(2,1)S(1)}, bf16[128,2048]{1,0:T(8,128)(2,1)S(1)}, u32[]{:S(2)}, u32[]{:S(2)}) collective-permute-start(bf16[128,2048]{1,0:T(8,128)(2,1)S(1)} %get-tuple-element.459), channel_id=1, source_target_pairs={{2,0},{3,1},{4,2},{5,3},{6,4},{7,5},{0,6},{1,7},{10,8},{11,9},{12,... | collective-permute-start | bytes 1572872 | tf_op jit(solution)/shard_map/ppermute | solution.py:1126
  (143 other events, 1855.1 us)
Sparse Core Ops, SparseCore 0:
  339.7 154.7 reduce-scatter.1

commit v6 on v5

--- a/solution.py
+++ b/solution.py
@@ -1279,7 +1279,7 @@
     )
     point = join(point, out_blocks, output_first, output_swapped, grad_one, grad_three)
     token_blocks = lax.all_to_all(
-        after(point, out_blocks), ("shard", "seq"), split_axis=0, concat_axis=0, tiled=True
+        out_blocks, ("shard", "seq"), split_axis=0, concat_axis=0, tiled=True
     )
     output_far = second_hops(after(point, output_first))
     output_swapped += [swap_cores(piece) for piece in after(point, output_first)]

time: 556 us -> 556 us (level)
  waiting for transfers between devices: 210 us -> 204 us
    ppermute x33, waiting for transfers between devices: 60.3 us -> 40.2 us  [from_shard(): return lax.ppermute(values, 'shard', [(i, i ^ flip) for i in range(4)])]
    all_to_all x1, waiting for transfers between devices: 0.01 us -> 16.6 us  [per_device(): lax.all_to_all(out_blocks, ('shard', 'seq'), split_axis=0, concat_axis=0,...]
    unnamed x148 -> x132, local copies, waits for them, and re-layouts: 15.7 us -> 15.2 us
  transfers between devices with their start and end apart: 96 -> 96, of which waited for: 44 -> 42; matrix products, arithmetic and copies ran while one was open for 10% -> 10% of each run, Pallas kernels for 24% -> 25%
where the time goes in v6:
time: 556 us; the launch traced here: 546 us
  waiting for transfers between devices  204 us (37%)
  Pallas kernels  155 us (28%)
  starting transfers between devices  101 us (18%)
  local copies, waits for them, and re-layouts  35.7 us (6%)
  other arithmetic  30.9 us (6%)
  between operations  15.4 us (3%)
    ppermute x29, waiting for transfers between devices, from_chip(): lax.ppermute(values, 'seq', [((i + 2 * step) % count, i) for i in range(c...  128 us
    ppermute x33, starting transfers between devices, from_shard(): return lax.ppermute(values, 'shard', [(i, i ^ flip) for i in range(4)])  40.6 us
    ppermute x33, waiting for transfers between devices, from_shard(): return lax.ppermute(values, 'shard', [(i, i ^ flip) for i in range(4)])  40.2 us
    ppermute x29, starting transfers between devices, from_chip(): lax.ppermute(values, 'seq', [((i + 2 * step) % count, i) for i in range(c...  40.1 us
    pallas_call x4, Pallas kernels, feed_blocks(): pl.pallas_call(functools.partial(feed_kernel, call, len(whole)), in_specs...  37 us
    pallas_call x1, Pallas kernels, attend_back(): pl.pallas_call(functools.partial(bwd_kernel, tok), grid=(spans,), in_spec...  30.1 us
    pallas_call x1, Pallas kernels, feed_wgrads(): pl.pallas_call(feed_wgrad_kernel, grid=(cuts, shards), in_specs=[rows] *...  20.7 us
    pallas_call x1, Pallas kernels, attend(): pl.pallas_call(functools.partial(fwd_kernel, tok), grid=(spans,), in_spec...  19.9 us
  transfers between devices with their start and end apart: 96, of which 42 were waited for; matrix products, arithmetic and copies ran while one was open for 10% of the time, Pallas kernels for 25%

profile of v6, /device:TPU:8, one launch (start us, length us, event | category | flops | bytes accessed | tf_op | source)
XLA Modules:
  0.0 545.9 jit_solution(13645505045018947808)
XLA Ops:
  19.9 10.5 %collective-permute-done.1 = bf16[128,768]{1,0:T(8,128)(2,1)S(1)} collective-permute-done((bf16[128,768]{1,0:T(8,128)(2,1)S(1)}, bf16[128,768]{1,0:T(8,128)(2,1)S(1)}, u32[]{:S(2)}, u32[]{:S(2)}) %collective-permute-start.1) | collective-permute-done | bytes 196640 | tf_op jit(solution)/shard_map/ppermute | solution.py:1126
  40.1 12.2 %collective-permute-done.7.refs_6_ = bf16[128,2048]{1,0:T(8,128)(2,1)S(1)} collective-permute-done((bf16[128,2048]{1,0:T(8,128)(2,1)S(1)}, bf16[128,2048]{1,0:T(8,128)(2,1)S(1)}, u32[]{:S(2)}, u32[]{:S(2)}) %collective-permute-start.7) | collective-permute-done | bytes 524320 | tf_op jit(solution)/shard_map/ppermute | solution.py:1126
  52.3 8.5 %collective-permute-done.6.refs_2_ = bf16[128,2048]{1,0:T(8,128)(2,1)S(1)} collective-permute-done((bf16[128,2048]{1,0:T(8,128)(2,1)S(1)}, bf16[128,2048]{1,0:T(8,128)(2,1)S(1)}, u32[]{:S(2)}, u32[]{:S(2)}) %collective-permute-start.6) | collective-permute-done | bytes 524320 | tf_op jit(solution)/shard_map/ppermute | solution.py:1126
  99.5 5.5 %collective-permute-done.20 = bf16[64,2048]{1,0:T(8,128)(2,1)S(1)} collective-permute-done((bf16[64,2048]{1,0:T(8,128)(2,1)}, bf16[64,2048]{1,0:T(8,128)(2,1)S(1)}, u32[]{:S(2)}, u32[]{:S(2)}) %collective-permute-start.20) | collective-permute-done | bytes 262176 | tf_op jit(solution)/shard_map/ppermute | solution.py:1126
  125.7 10.1 %all-to-all-done.qkv_ref = bf16[4,192,1024]{2,1,0:T(8,128)(2,1)S(1)} async-done(((bf16[4,192,1024]{2,1,0:T(8,128)(2,1)}), bf16[4,192,1024]{2,1,0:T(8,128)(2,1)S(1)}, u32[]{:S(2)}, u32[]{:S(2)}) %all-to-all-start) | async-done | bytes 1572896 | tf_op jit(solution)/shard_map/all_to_all | solution.py:1266
  145.1 19.9 %attend.1 = (f32[4,64,1024]{2,1,0:T(8,128)}, bf16[4,64,1024]{2,1,0:T(8,128)(2,1)}, bf16[32,80,128]{2,1,0:T(8,128)(2,1)}, f32[4,1,1024]{2,1,0:T(1,128)S(1)}) custom-call(s32[1]{0:T(128)} %bitcast.19.shard_ref.refs_0_, s32[4]{0:T(128)S(1)} %and_select_fusion.7.lo_ref, s32[4]{0:T(128)S(1)} %iota_minimum_fusion.full_ref, ...), custom_call_target="tpu_custom_call" | custom-call | flops 21474836480 | bytes 4194304 | tf_op jit(solution)/shard_map/attend/pallas_call | solution.py:497
  165.0 6.1 %all-to-all-start.1 = ((bf16[32,80,128]{2,1,0:T(8,128)(2,1)}), bf16[32,80,128]{2,1,0:T(8,128)(2,1)S(1)}, u32[]{:S(2)}, u32[]{:S(2)}) async-start(bf16[32,80,128]{2,1,0:T(8,128)(2,1)} %get-tuple-element.253), calls=%async_computation.1 | async-start | bytes 1310720 | tf_op jit(solution)/shard_map/all_to_all | solution.py:1281
  180.2 16.6 %all-to-all-done.1.blocks_ref = bf16[32,80,128]{2,1,0:T(8,128)(2,1)S(1)} async-done(((bf16[32,80,128]{2,1,0:T(8,128)(2,1)}), bf16[32,80,128]{2,1,0:T(8,128)(2,1)S(1)}, u32[]{:S(2)}, u32[]{:S(2)}) %all-to-all-start.1) | async-done | bytes 655392 | tf_op jit(solution)/shard_map/all_to_all | solution.py:1281
  216.9 5.6 %collective-permute-done.39.refs_1_ = bf16[128,2048]{1,0:T(8,128)(2,1)S(1)} collective-permute-done((bf16[128,2048]{1,0:T(8,128)(2,1)S(1)}, bf16[128,2048]{1,0:T(8,128)(2,1)S(1)}, u32[]{:S(2)}, u32[]{:S(2)}) %collective-permute-start.39) | collective-permute-done | bytes 524320 | tf_op jit(solution)/shard_map/ppermute | solution.py:1126
  222.5 9.4 %collective-permute-done.38.refs_1_ = bf16[128,2048]{1,0:T(8,128)(2,1)S(1)} collective-permute-done((bf16[128,2048]{1,0:T(8,128)(2,1)S(1)}, bf16[128,2048]{1,0:T(8,128)(2,1)S(1)}, u32[]{:S(2)}, u32[]{:S(2)}) %collective-permute-start.38) | collective-permute-done | bytes 524320 | tf_op jit(solution)/shard_map/ppermute | solution.py:1126
  249.1 5.2 collective-permute-done.50.refs_4_
  258.5 9.0 %feed_blocks.4 = (f32[128,2048]{1,0:T(8,128)S(1)}, bf16[128,2048]{1,0:T(8,128)(2,1)S(1)}, bf16[1024,2048]{1,0:T(8,128)(2,1)}, bf16[1024,2048]{1,0:T(8,128)(2,1)}...) custom-call(s32[1]{0:T(128)} %bitcast.19.shard_ref.refs_0_, ...), custom_call_target="tpu_custom_call" | custom-call | tf_op jit(solution)/shard_map/feed_blocks/pallas_call | solution.py:932
  275.1 9.7 %feed_blocks.5 = (f32[128,2048]{1,0:T(8,128)S(1)}, bf16[128,2048]{1,0:T(8,128)(2,1)S(1)}, bf16[1024,2048]{1,0:T(8,128)(2,1)}, bf16[1024,2048]{1,0:T(8,128)(2,1)}...) custom-call(s32[1]{0:T(128)} %bitcast.19.shard_ref.refs_0_, ...), custom_call_target="tpu_custom_call", output_to_operand_aliasing={{2}: (7, {}), {3}: (8, {}), {4}: (9, {}), {5}: (10, {}), {6... | custom-call | tf_op jit(solution)/shard_map/feed_blocks/pallas_call | solution.py:932
  284.8 9.5 %feed_blocks.6 = (f32[128,2048]{1,0:T(8,128)S(1)}, bf16[128,2048]{1,0:T(8,128)(2,1)S(1)}, bf16[1024,2048]{1,0:T(8,128)(2,1)}, bf16[1024,2048]{1,0:T(8,128)(2,1)}...) custom-call(s32[1]{0:T(128)} %bitcast.19.shard_ref.refs_0_, ...), custom_call_target="tpu_custom_call", output_to_operand_aliasing={{2}: (7, {}), {3}: (8, {}), {4}: (9, {}), {5}: (10, {}), {6... | custom-call | tf_op jit(solution)/shard_map/feed_blocks/pallas_call | solution.py:932
  294.3 8.9 %feed_blocks.7 = (f32[128,2048]{1,0:T(8,128)S(1)}, bf16[128,2048]{1,0:T(8,128)(2,1)S(1)}, bf16[1024,2048]{1,0:T(8,128)(2,1)}, bf16[1024,2048]{1,0:T(8,128)(2,1)}...) custom-call(s32[1]{0:T(128)} %bitcast.19.shard_ref.refs_0_, ...), custom_call_target="tpu_custom_call", output_to_operand_aliasing={{2}: (7, {}), {3}: (8, {}), {4}: (9, {}), {5}: (10, {}), {6... | custom-call | tf_op jit(solution)/shard_map/feed_blocks/pallas_call | solution.py:932
  309.1 20.7 %feed_wgrads.1 = bf16[4,3,256,2048]{3,2,1,0:T(8,128)(2,1)} custom-call(bf16[1024,1024]{1,0:T(8,128)(2,1)} %get-tuple-element.353.gate_ref, bf16[1024,1024]{1,0:T(8,128)(2,1)} %get-tuple-element.354.up_ref, bf16[1024,1024]{1,0:T(8,128)(2,1)} %get-tuple-element.355.hidden_ref, bf16[1024,2048]{1,0:T(8,128)(2,1)} %get-tuple-element.356.tokens_ref, ...), custom_call_target="tpu_custom_call" | custom-call | tf_op jit(solution)/shard_map/feed_wgrads/pallas_call | solution.py:1083
  350.0 21.1 %collective-permute-done.65.refs_2_ = bf16[128,2048]{1,0:T(8,128)(2,1)} collective-permute-done((bf16[128,2048]{1,0:T(8,128)(2,1)S(1)}, bf16[128,2048]{1,0:T(8,128)(2,1)}, u32[]{:S(2)}, u32[]{:S(2)}) %collective-permute-start.65) | collective-permute-done | bytes 524320 | tf_op jit(solution)/shard_map/ppermute | solution.py:1126
  373.1 30.1 %attend_back.1 = bf16[4,192,1024]{2,1,0:T(8,128)(2,1)} custom-call(s32[4]{0:T(128)S(1)} %and_select_fusion.hi_ref, s32[4]{0:T(128)S(1)} %iota_minimum_fusion.full_ref, s32[4,1,1024]{2,1,0:T(1,128)S(1)} %broadcast_in_dim.40.start_ref, bf16[4,192,1024]{2,1,0:T(8,128)(2,1)S(1)} %copy-done.16, f32[4,1,1024]{2,1,0:T(1,128)S(1)} %get-tuple-element.375.lse_ref, ...), custom_call_target="tpu_custom_call" | custom-call | flops 30064771072 | bytes 4194304 | tf_op jit(solution)/shard_map/attend_back/pallas_call | solution.py:537
  414.9 7.9 %collective-permute-done.72.refs_4_ = bf16[128,2048]{1,0:T(8,128)(2,1)S(1)} collective-permute-done((bf16[128,2048]{1,0:T(8,128)(2,1)}, bf16[128,2048]{1,0:T(8,128)(2,1)S(1)}, u32[]{:S(2)}, u32[]{:S(2)}) %collective-permute-start.72) | collective-permute-done | bytes 524320 | tf_op jit(solution)/shard_map/ppermute | solution.py:1126
  434.7 5.0 collective-permute-done.69
  439.9 5.6 %cols_parts.1 = bf16[4,768,512]{2,1,0:T(8,128)(2,1)S(1)} custom-call(s32[1]{0:T(128)} %bitcast.19.shard_ref.refs_0_, bf16[768,1024]{1,0:T(8,128)(2,1)S(1)} %bitcast.136, bf16[1024,2048]{1,0:T(8,128)(2,1)} %copy-done.2), custom_call_target="tpu_custom_call" | custom-call | tf_op jit(solution)/shard_map/cols_parts/pallas_call | solution.py:646
  460.9 10.9 %collective-permute-done.81 = bf16[384,512]{1,0:T(8,128)(2,1)S(1)} collective-permute-done((bf16[384,512]{1,0:T(8,128)(2,1)S(1)}, bf16[384,512]{1,0:T(8,128)(2,1)S(1)}, u32[]{:S(2)}, u32[]{:S(2)}) %collective-permute-start.81) | collective-permute-done | bytes 393248 | tf_op jit(solution)/shard_map/ppermute | solution.py:1130
  475.6 8.5 %collective-permute-done.82 = bf16[64,2048]{1,0:T(8,128)(2,1)S(1)} collective-permute-done((bf16[64,2048]{1,0:T(8,128)(2,1)S(1)}, bf16[64,2048]{1,0:T(8,128)(2,1)S(1)}, u32[]{:S(2)}, u32[]{:S(2)}) %collective-permute-start.82) | collective-permute-done | bytes 262176 | tf_op jit(solution)/shard_map/ppermute | solution.py:1130
  490.1 12.5 %collective-permute-done.84 = bf16[128,2048]{1,0:T(8,128)(2,1)S(1)} collective-permute-done((bf16[128,2048]{1,0:T(8,128)(2,1)S(1)}, bf16[128,2048]{1,0:T(8,128)(2,1)S(1)}, u32[]{:S(2)}, u32[]{:S(2)}) %collective-permute-start.84) | collective-permute-done | bytes 524320 | tf_op jit(solution)/shard_map/ppermute | solution.py:1126
  (399 shorter events, 261.5 us)
Async XLA Ops:
  12.4 27.0 %collective-permute-start.8 = (bf16[256,2048]{1,0:T(8,128)(2,1)}, bf16[256,2048]{1,0:T(8,128)(2,1)S(1)}, u32[]{:S(2)}, u32[]{:S(2)}) collective-permute-start(bf16[256,2048]{1,0:T(8,128)(2,1)} %refs_0_.2), channel_id=1, source_target_pairs={{0,8},{8,0},{16,24},{24,16},{1,9},{9,1},{17,25},{25,17},{2,10},{10... | collective-permute-start | bytes 3145736 | tf_op jit(solution)/shard_map/ppermute | solution.py:1130
  79.9 33.6 %collective-permute-start.22 = (bf16[128,2048]{1,0:T(8,128)(2,1)}, bf16[128,2048]{1,0:T(8,128)(2,1)}, u32[]{:S(2)}, u32[]{:S(2)}) collective-permute-start(bf16[128,2048]{1,0:T(8,128)(2,1)} %get-tuple-element.246), channel_id=1, source_target_pairs={{0,16},{8,24},{16,0},{24,8},{1,17},{9,25},{17,1},{25,9},{2,18},{10... | collective-permute-start | bytes 1572872 | tf_op jit(solution)/shard_map/ppermute | solution.py:1130
  80.4 33.1 %collective-permute-start.21 = (bf16[128,2048]{1,0:T(8,128)(2,1)}, bf16[128,2048]{1,0:T(8,128)(2,1)}, u32[]{:S(2)}, u32[]{:S(2)}) collective-permute-start(bf16[128,2048]{1,0:T(8,128)(2,1)} %get-tuple-element.246), channel_id=1, source_target_pairs={{0,8},{8,0},{16,24},{24,16},{1,9},{9,1},{17,25},{25,17},{2,10},{10... | collective-permute-start | bytes 1572872 | tf_op jit(solution)/shard_map/ppermute | solution.py:1130
  86.1 27.4 %collective-permute-start.24 = (bf16[128,2048]{1,0:T(8,128)(2,1)}, bf16[128,2048]{1,0:T(8,128)(2,1)S(1)}, u32[]{:S(2)}, u32[]{:S(2)}) collective-permute-start(bf16[128,2048]{1,0:T(8,128)(2,1)} %get-tuple-element.247), channel_id=1, source_target_pairs={{0,16},{8,24},{16,0},{24,8},{1,17},{9,25},{17,1},{25,9},{2,18},{10... | collective-permute-start | bytes 1572872 | tf_op jit(solution)/shard_map/ppermute | solution.py:1130
  135.8 35.4 %collective-permute-start.30 = (bf16[128,2048]{1,0:T(8,128)(2,1)S(1)}, bf16[128,2048]{1,0:T(8,128)(2,1)}, u32[]{:S(2)}, u32[]{:S(2)}) collective-permute-start(bf16[128,2048]{1,0:T(8,128)(2,1)S(1)} %copy-done.8), channel_id=1, source_target_pairs={{6,0},{7,1},{0,2},{1,3},{2,4},{3,5},{4,6},{5,7},{14,8},{15,9},{8,1... | collective-permute-start | bytes 1572872 | tf_op jit(solution)/shard_map/ppermute | solution.py:1126
  136.3 34.9 %collective-permute-start.29 = (bf16[128,2048]{1,0:T(8,128)(2,1)S(1)}, bf16[128,2048]{1,0:T(8,128)(2,1)}, u32[]{:S(2)}, u32[]{:S(2)}) collective-permute-start(bf16[128,2048]{1,0:T(8,128)(2,1)S(1)} %copy-done.8), channel_id=1, source_target_pairs={{2,0},{3,1},{4,2},{5,3},{6,4},{7,5},{0,6},{1,7},{10,8},{11,9},{12,... | collective-permute-start | bytes 1572872 | tf_op jit(solution)/shard_map/ppermute | solution.py:1126
  143.1 28.1 %collective-permute-start.28 = (bf16[256,2048]{1,0:T(8,128)(2,1)}, bf16[256,2048]{1,0:T(8,128)(2,1)}, u32[]{:S(2)}, u32[]{:S(2)}) collective-permute-start(bf16[256,2048]{1,0:T(8,128)(2,1)} %constant_dynamic-update-slice_fusion.4.refs_0_), channel_id=1, source_target_pairs={{0,1},{1,0},{2,3},{3,2},{4,5},{5,4},{6,7},{7,6},{8,9},{9,8},{10,11... | collective-permute-start | bytes 3145736 | tf_op jit(solution)/shard_map/ppermute | solution.py:1121
  143.1 28.1 %collective-permute-start.27 = (bf16[256,2048]{1,0:T(8,128)(2,1)}, bf16[256,2048]{1,0:T(8,128)(2,1)}, u32[]{:S(2)}, u32[]{:S(2)}) collective-permute-start(bf16[256,2048]{1,0:T(8,128)(2,1)} %constant_dynamic-update-slice_fusion.4.refs_0_), channel_id=1, source_target_pairs={{0,16},{8,24},{16,0},{24,8},{1,17},{9,25},{17,1},{25,9},{2,18},{10... | collective-permute-start | bytes 3145736 | tf_op jit(solution)/shard_map/ppermute | solution.py:1130
  144.6 26.6 %collective-permute-start.26 = (bf16[256,2048]{1,0:T(8,128)(2,1)}, bf16[256,2048]{1,0:T(8,128)(2,1)}, u32[]{:S(2)}, u32[]{:S(2)}) collective-permute-start(bf16[256,2048]{1,0:T(8,128)(2,1)} %constant_dynamic-update-slice_fusion.4.refs_0_), channel_id=1, source_target_pairs={{0,8},{8,0},{16,24},{24,16},{1,9},{9,1},{17,25},{25,17},{2,10},{10... | collective-permute-start | bytes 3145736 | tf_op jit(solution)/shard_map/ppermute | solution.py:1130
  165.0 31.8 %all-to-all-start.1 = ((bf16[32,80,128]{2,1,0:T(8,128)(2,1)}), bf16[32,80,128]{2,1,0:T(8,128)(2,1)S(1)}, u32[]{:S(2)}, u32[]{:S(2)}) async-start(bf16[32,80,128]{2,1,0:T(8,128)(2,1)} %get-tuple-element.253), calls=%async_computation.1 | async-start | bytes 1310720 | tf_op jit(solution)/shard_map/all_to_all | solution.py:1281
  171.2 353.8 %reduce-scatter.2.cloned.1.call-start = ((), (), s32[]{:S(2)}) async-start(), calls=%async_computation.5 | async-start | bytes 15728640 | tf_op jit(solution)/shard_map/reduce_scatter | solution.py:1361
  171.3 27.8 %collective-permute-start.33 = (bf16[256,2048]{1,0:T(8,128)(2,1)}, bf16[256,2048]{1,0:T(8,128)(2,1)}, u32[]{:S(2)}, u32[]{:S(2)}) collective-permute-start(bf16[256,2048]{1,0:T(8,128)(2,1)} %collective-permute-done.26.refs_1_), channel_id=1, source_target_pairs={{0,1},{1,0},{2,3},{3,2},{4,5},{5,4},{6,7},{7,6},{8,9},{9,8},{10,11... | collective-permute-start | bytes 3145736 | tf_op jit(solution)/shard_map/ppermute | solution.py:1121
  171.5 27.6 %collective-permute-start.34 = (bf16[256,2048]{1,0:T(8,128)(2,1)}, bf16[256,2048]{1,0:T(8,128)(2,1)}, u32[]{:S(2)}, u32[]{:S(2)}) collective-permute-start(bf16[256,2048]{1,0:T(8,128)(2,1)} %collective-permute-done.27.refs_2_), channel_id=1, source_target_pairs={{0,1},{1,0},{2,3},{3,2},{4,5},{5,4},{6,7},{7,6},{8,9},{9,8},{10,11... | collective-permute-start | bytes 3145736 | tf_op jit(solution)/shard_map/ppermute | solution.py:1121
  269.6 33.7 %collective-permute-start.56 = (bf16[128,2048]{1,0:T(8,128)(2,1)S(1)}, bf16[128,2048]{1,0:T(8,128)(2,1)S(1)}, u32[]{:S(2)}, u32[]{:S(2)}) collective-permute-start(bf16[128,2048]{1,0:T(8,128)(2,1)S(1)} %add_convert_fusion.3), channel_id=1, source_target_pairs={{4,0},{5,1},{6,2},{7,3},{0,4},{1,5},{2,6},{3,7},{12,8},{13,9},{14,... | collective-permute-start | bytes 1572872 | tf_op jit(solution)/shard_map/ppermute | solution.py:1126
  271.6 31.6 %collective-permute-start.57 = (bf16[64,1024]{1,0:T(8,128)(2,1)S(1)}, bf16[64,1024]{1,0:T(8,128)(2,1)S(1)}, u32[]{:S(2)}, u32[]{:S(2)}) collective-permute-start(bf16[64,1024]{1,0:T(8,128)(2,1)S(1)} %get-tuple-element.335), channel_id=1, source_target_pairs={{0,8},{8,0},{16,24},{24,16},{1,9},{9,1},{17,25},{25,17},{2,10},{10... | collective-permute-start | bytes 393224 | tf_op jit(solution)/shard_map/ppermute | solution.py:1130
  272.4 30.8 %collective-permute-start.58 = (bf16[64,1024]{1,0:T(8,128)(2,1)S(1)}, bf16[64,1024]{1,0:T(8,128)(2,1)S(1)}, u32[]{:S(2)}, u32[]{:S(2)}) collective-permute-start(bf16[64,1024]{1,0:T(8,128)(2,1)S(1)} %get-tuple-element.336), channel_id=1, source_target_pairs={{0,16},{8,24},{16,0},{24,8},{1,17},{9,25},{17,1},{25,9},{2,18},{10... | collective-permute-start | bytes 393224 | tf_op jit(solution)/shard_map/ppermute | solution.py:1130
  273.7 29.5 %collective-permute-start.59 = (bf16[64,1024]{1,0:T(8,128)(2,1)S(1)}, bf16[64,1024]{1,0:T(8,128)(2,1)S(1)}, u32[]{:S(2)}, u32[]{:S(2)}) collective-permute-start(bf16[64,1024]{1,0:T(8,128)(2,1)S(1)} %get-tuple-element.337), channel_id=1, source_target_pairs={{0,24},{8,16},{16,8},{24,0},{1,25},{9,17},{17,9},{25,1},{2,26},{10... | collective-permute-start | bytes 393224 | tf_op jit(solution)/shard_map/ppermute | solution.py:1130
  339.7 31.4 %all-to-all-start.2 = ((bf16[32,80,128]{2,1,0:T(8,128)(2,1)}), bf16[32,80,128]{2,1,0:T(8,128)(2,1)S(1)}, u32[]{:S(2)}, u32[]{:S(2)}) async-start(bf16[32,80,128]{2,1,0:T(8,128)(2,1)} %get-tuple-element.368), calls=%async_computation.2 | async-start | bytes 1310720 | tf_op jit(solution)/shard_map/all_to_all | solution.py:1358
  343.1 27.9 %collective-permute-start.65 = (bf16[128,2048]{1,0:T(8,128)(2,1)S(1)}, bf16[128,2048]{1,0:T(8,128)(2,1)}, u32[]{:S(2)}, u32[]{:S(2)}) collective-permute-start(bf16[128,2048]{1,0:T(8,128)(2,1)S(1)} %get-tuple-element.383.refs_0_), channel_id=1, source_target_pairs={{2,0},{3,1},{4,2},{5,3},{6,4},{7,5},{0,6},{1,7},{10,8},{11,9},{12,... | collective-permute-start | bytes 1572872 | tf_op jit(solution)/shard_map/ppermute | solution.py:1126
  371.1 32.1 %collective-permute-start.68 = (bf16[128,2048]{1,0:T(8,128)(2,1)}, bf16[128,2048]{1,0:T(8,128)(2,1)S(1)}, u32[]{:S(2)}, u32[]{:S(2)}) collective-permute-start(bf16[128,2048]{1,0:T(8,128)(2,1)} %get-tuple-element.379), channel_id=1, source_target_pairs={{2,0},{3,1},{4,2},{5,3},{6,4},{7,5},{0,6},{1,7},{10,8},{11,9},{12,... | collective-permute-start | bytes 1572872 | tf_op jit(solution)/shard_map/ppermute | solution.py:1126
  371.1 37.9 %collective-permute-start.67 = (bf16[256,2048]{1,0:T(8,128)(2,1)}, bf16[256,2048]{1,0:T(8,128)(2,1)}, u32[]{:S(2)}, u32[]{:S(2)}) collective-permute-start(bf16[256,2048]{1,0:T(8,128)(2,1)} %pad_maximum_fusion.1), channel_id=1, source_target_pairs={{6,0},{7,1},{0,2},{1,3},{2,4},{3,5},{4,6},{5,7},{14,8},{15,9},{8,1... | collective-permute-start | bytes 3145736 | tf_op jit(solution)/shard_map/ppermute | solution.py:1126
  409.3 30.4 %all-to-all-start.3 = ((bf16[4,192,1024]{2,1,0:T(8,128)(2,1)}), bf16[4,192,1024]{2,1,0:T(8,128)(2,1)S(1)}, u32[]{:S(2)}, u32[]{:S(2)}) async-start(bf16[4,192,1024]{2,1,0:T(8,128)(2,1)} %attend_back.1), calls=%async_computation.3 | async-start | bytes 3145728 | tf_op jit(solution)/shard_map/all_to_all | solution.py:1377
  454.9 29.3 %collective-permute-start.82 = (bf16[64,2048]{1,0:T(8,128)(2,1)S(1)}, bf16[64,2048]{1,0:T(8,128)(2,1)S(1)}, u32[]{:S(2)}, u32[]{:S(2)}) collective-permute-start(bf16[64,2048]{1,0:T(8,128)(2,1)S(1)} %pad_maximum_fusion.5), channel_id=1, source_target_pairs={{0,8},{8,0},{16,24},{24,16},{1,9},{9,1},{17,25},{25,17},{2,10},{10... | collective-permute-start | bytes 786440 | tf_op jit(solution)/shard_map/ppermute | solution.py:1130
  456.3 27.9 %collective-permute-start.83 = (bf16[64,2048]{1,0:T(8,128)(2,1)S(1)}, bf16[64,2048]{1,0:T(8,128)(2,1)S(1)}, u32[]{:S(2)}, u32[]{:S(2)}) collective-permute-start(bf16[64,2048]{1,0:T(8,128)(2,1)S(1)} %pad_maximum_fusion.6), channel_id=1, source_target_pairs={{0,16},{8,24},{16,0},{24,8},{1,17},{9,25},{17,1},{25,9},{2,18},{10... | collective-permute-start | bytes 786440 | tf_op jit(solution)/shard_map/ppermute | solution.py:1130
  (135 other events, 1790.4 us)
Sparse Core Ops, SparseCore 0:
  339.6 154.8 reduce-scatter.1
